TPU v7x, 32 devices: a whole 2x2x4 slice. The times are simulated.
32 devices in a mesh: fsdp: 16 (over z, x, core), tp: 2 (over y).
Axes of the slice: x: 2, y: 2, z: 4, core: 2. Of those that a mesh axis runs over, the one named last changes fastest.
Arguments:
- latents_in: float32 [1024, 16, 1024], P('tp', 'fsdp'), may hold values from -6 to 6
- condition: float32 [16, 1024], P('fsdp'), may hold values from -6 to 6
- out_grad: float32 [1024, 16, 1024], P('tp', 'fsdp'), may hold values from -6 to 6
- condition_weight: float32 [1024, 6, 1024], P('fsdp', None, 'tp'), may hold values from -0.1875 to 0.1875
- condition_first: float32 [1024, 6, 1024], P('fsdp', None, 'tp'), may hold values from -80 to 80
- condition_second: float32 [1024, 6, 1024], P('fsdp', None, 'tp'), may hold values from 8.192 to 131.072
- heads_weight: float32 [3, 1024, 1024], P(None, 'fsdp', 'tp'), may hold values from -0.1875 to 0.1875
- heads_first: float32 [3, 1024, 1024], P(None, 'fsdp', 'tp'), may hold values from -80 to 80
- heads_second: float32 [3, 1024, 1024], P(None, 'fsdp', 'tp'), may hold values from 8.192 to 131.072
- merge_weight: float32 [1024, 1024], P('tp', 'fsdp'), may hold values from -1.5 to 1.5
- merge_first: float32 [1024, 1024], P('tp', 'fsdp'), may hold values from -8 to 8
- merge_second: float32 [1024, 1024], P('tp', 'fsdp'), may hold values from 0.08192 to 1.31072
- up_weight: float32 [1024, 4096], P('fsdp', 'tp'), may hold values from -0.1875 to 0.1875
- up_first: float32 [1024, 4096], P('fsdp', 'tp'), may hold values from -20 to 20
- up_second: float32 [1024, 4096], P('fsdp', 'tp'), may hold values from 0.49152 to 8.192
- down_weight: float32 [4096, 1024], P('tp', 'fsdp'), may hold values from -0.09375 to 0.09375
- down_first: float32 [4096, 1024], P('tp', 'fsdp'), may hold values from -32 to 32
- down_second: float32 [4096, 1024], P('tp', 'fsdp'), may hold values from 0.98304 to 16.384
Outputs:
- block_out: float32 [1024, 16, 1024], P('tp', 'fsdp')
- latents_grad: float32 [1024, 16, 1024], P('tp', 'fsdp')
- condition_weight_new: float32 [1024, 6, 1024], P('fsdp', None, 'tp')
- condition_first_new: float32 [1024, 6, 1024], P('fsdp', None, 'tp')
- condition_second_new: float32 [1024, 6, 1024], P('fsdp', None, 'tp')
- heads_weight_new: float32 [3, 1024, 1024], P(None, 'fsdp', 'tp')
- heads_first_new: float32 [3, 1024, 1024], P(None, 'fsdp', 'tp')
- heads_second_new: float32 [3, 1024, 1024], P(None, 'fsdp', 'tp')
- merge_weight_new: float32 [1024, 1024], P('tp', 'fsdp')
- merge_first_new: float32 [1024, 1024], P('tp', 'fsdp')
- merge_second_new: float32 [1024, 1024], P('tp', 'fsdp')
- up_weight_new: float32 [1024, 4096], P('fsdp', 'tp')
- up_first_new: float32 [1024, 4096], P('fsdp', 'tp')
- up_second_new: float32 [1024, 4096], P('fsdp', 'tp')
- down_weight_new: float32 [4096, 1024], P('tp', 'fsdp')
- down_first_new: float32 [4096, 1024], P('tp', 'fsdp')
- down_second_new: float32 [4096, 1024], P('tp', 'fsdp')
All inputs are finite; a program needn't handle non-finite values.
Results may differ from a plain program's by a relative error of at most 0.025.
Values may be sent and summed in bfloat16 or wider, within the bound.
No kernel may reach another device: no remote copies, remote signals or barrier semaphores. Data moves between devices by JAX's collectives and lax.ppermute only.
A program may use at most 192 MiB of HBM per device.

v0:
```python
import jax
import jax.numpy as jnp
from jax import lax
from jax.sharding import PartitionSpec as P

HEAD = 64
STEP = 5


def modulate(values, shift_term, scale_term):
    middle = jnp.mean(values, axis=-1, keepdims=True)
    centred = values - middle
    spread = jnp.mean(centred * centred, axis=-1, keepdims=True)
    return centred * lax.rsqrt(spread + 1e-06) * (1.0 + scale_term) + shift_term


def gelu_tanh(values):
    return jax.nn.gelu(values, approximate=True)


def adam_step(weight, first, second, grad_sum, rate):
    first_new = 0.9 * first + 0.1 * grad_sum
    second_new = 0.999 * second + 0.001 * grad_sum * grad_sum
    first_hat = first_new / (1.0 - 0.9**STEP)
    second_hat = second_new / (1.0 - 0.999**STEP)
    weight_new = weight - rate * (first_hat / (jnp.sqrt(second_hat) + 1e-08) + 0.01 * weight)
    return (weight_new, first_new, second_new)


def attend_forward(query, keyset, valueset):
    total = query.shape[0]
    block_rows = min(512, total)
    scaling = HEAD ** (-0.5)
    blocks = query.reshape(total // block_rows, block_rows, query.shape[1], query.shape[2])

    def one_block(query_block):
        scores = (
            jnp.einsum("qhe,khe->hqk", query_block, keyset, preferred_element_type=jnp.float32)
            * scaling
        )
        peak = jnp.max(scores, axis=-1, keepdims=True)
        raised = jnp.exp(scores - peak)
        totals = jnp.sum(raised, axis=-1, keepdims=True)
        probs_low = (raised / totals).astype(jnp.bfloat16)
        output = jnp.einsum(
            "hqk,khe->qhe", probs_low, valueset, preferred_element_type=jnp.float32
        ).astype(jnp.bfloat16)
        return (output, (peak + jnp.log(totals))[..., 0])

    outputs, logsum = lax.map(one_block, blocks)
    return (outputs.reshape(query.shape), logsum)


def attend_backward(query, keyset, valueset, attended_grad, logsum):
    total = query.shape[0]
    block_rows = min(512, total)
    scaling = HEAD ** (-0.5)
    shape_blocks = (total // block_rows, block_rows, query.shape[1], query.shape[2])

    def one_block(carry, parts):
        key_grad, value_grad = carry
        query_block, grad_block, logsum_block = parts
        scores = (
            jnp.einsum("qhe,khe->hqk", query_block, keyset, preferred_element_type=jnp.float32)
            * scaling
        )
        probs = jnp.exp(scores - logsum_block[..., None])
        value_grad = value_grad + jnp.einsum(
            "hqk,qhe->khe",
            probs.astype(jnp.bfloat16),
            grad_block,
            preferred_element_type=jnp.float32,
        )
        prob_grad = jnp.einsum(
            "qhe,khe->hqk", grad_block, valueset, preferred_element_type=jnp.float32
        )
        inner = jnp.sum(probs * prob_grad, axis=-1, keepdims=True)
        score_grad = (probs * (prob_grad - inner)).astype(jnp.bfloat16)
        query_grad = (
            jnp.einsum("hqk,khe->qhe", score_grad, keyset, preferred_element_type=jnp.float32)
            * scaling
        ).astype(jnp.bfloat16)
        key_grad = (
            key_grad
            + jnp.einsum(
                "hqk,qhe->khe", score_grad, query_block, preferred_element_type=jnp.float32
            )
            * scaling
        )
        return ((key_grad, value_grad), query_grad)

    empty = jnp.zeros(keyset.shape, jnp.float32)
    (key_grad, value_grad), query_grad = lax.scan(
        one_block,
        (empty, empty),
        (query.reshape(shape_blocks), attended_grad.reshape(shape_blocks), logsum),
    )
    return (
        query_grad.reshape(query.shape),
        key_grad.astype(jnp.bfloat16),
        value_grad.astype(jnp.bfloat16),
    )


def local(
    latents_in,
    condition,
    out_grad,
    condition_weight,
    condition_first,
    condition_second,
    heads_weight,
    heads_first,
    heads_second,
    merge_weight,
    merge_first,
    merge_second,
    up_weight,
    up_first,
    up_second,
    down_weight,
    down_first,
    down_second,
):
    low_type = jnp.bfloat16
    latent_count = latents_in.shape[1]
    cond_full, heads_full, merge_full, up_full, down_full = (
        lax.all_gather(condition_weight.astype(low_type), "fsdp", axis=0, tiled=True),
        lax.all_gather(heads_weight.astype(low_type), "fsdp", axis=1, tiled=True),
        lax.all_gather(merge_weight.astype(low_type), "fsdp", axis=1, tiled=True),
        lax.all_gather(up_weight.astype(low_type), "fsdp", axis=0, tiled=True),
        lax.all_gather(down_weight.astype(low_type), "fsdp", axis=1, tiled=True),
    )
    activated = jax.nn.silu(condition).astype(low_type)
    part_modulation = jnp.einsum(
        "bd,dkc->bkc", activated, cond_full, preferred_element_type=jnp.float32
    )
    modulation = lax.all_gather(part_modulation, "tp", axis=2, tiled=True)
    shift_one = modulation[:, 0]
    scale_one = modulation[:, 1]
    gate_one = modulation[:, 2]
    shift_two = modulation[:, 3]
    scale_two = modulation[:, 4]
    gate_two = modulation[:, 5]
    normed_one = modulate(latents_in, shift_one, scale_one).astype(low_type)
    normed_full = lax.all_gather(normed_one, "tp", axis=0, tiled=True)
    seq_total = normed_full.shape[0]
    triple = jnp.einsum(
        "sbd,tdc->bstc", normed_full, heads_full, preferred_element_type=jnp.float32
    ).astype(low_type)
    width_local = triple.shape[-1]
    heads_local = width_local // HEAD
    split = triple.reshape(latent_count, seq_total, 3, heads_local, HEAD)

    def forward_latent(parts):
        return attend_forward(parts[0], parts[1], parts[2])

    attended, logsum = lax.map(forward_latent, (split[:, :, 0], split[:, :, 1], split[:, :, 2]))
    mixed_heads = jnp.moveaxis(attended.reshape(latent_count, seq_total, width_local), 0, 1)
    attn_branch = lax.psum_scatter(
        jnp.einsum(
            "sbc,cd->sbd", mixed_heads, merge_full, preferred_element_type=jnp.float32
        ).astype(jnp.bfloat16),
        "tp",
        scatter_dimension=0,
        tiled=True,
    ).astype(jnp.float32)
    after_attn = latents_in + gate_one * attn_branch
    normed_two = modulate(after_attn, shift_two, scale_two).astype(low_type)
    second_full = lax.all_gather(normed_two, "tp", axis=0, tiled=True)
    hidden_pre = jnp.einsum("sbd,df->sbf", second_full, up_full, preferred_element_type=jnp.float32)
    hidden = gelu_tanh(hidden_pre).astype(low_type)
    mlp_branch = lax.psum_scatter(
        jnp.einsum("sbf,fd->sbd", hidden, down_full, preferred_element_type=jnp.float32).astype(
            jnp.bfloat16
        ),
        "tp",
        scatter_dimension=0,
        tiled=True,
    ).astype(jnp.float32)
    block_out = after_attn + gate_two * mlp_branch
    heads_back, merge_back, up_back, down_back = (
        lax.all_gather(heads_weight.astype(low_type), "fsdp", axis=1, tiled=True),
        lax.all_gather(merge_weight.astype(low_type), "fsdp", axis=1, tiled=True),
        lax.all_gather(up_weight.astype(low_type), "fsdp", axis=0, tiled=True),
        lax.all_gather(down_weight.astype(low_type), "fsdp", axis=1, tiled=True),
    )
    mlp_grad = (gate_two * out_grad).astype(low_type)
    gate_two_grad = jnp.sum(out_grad * mlp_branch, axis=0)
    mlp_grad_full = lax.all_gather(mlp_grad, "tp", axis=0, tiled=True)
    hidden_grad = jnp.einsum(
        "sbd,fd->sbf", mlp_grad_full, down_back, preferred_element_type=jnp.float32
    )
    unused_value, gelu_back = jax.vjp(gelu_tanh, hidden_pre)
    pre_grad = gelu_back(hidden_grad)[0].astype(low_type)
    down_grad = jnp.einsum("sbf,sbd->fd", hidden, mlp_grad_full, preferred_element_type=jnp.float32)
    up_grad = jnp.einsum("sbd,sbf->df", second_full, pre_grad, preferred_element_type=jnp.float32)
    normed_two_grad = lax.psum_scatter(
        jnp.einsum("sbf,df->sbd", pre_grad, up_back, preferred_element_type=jnp.float32).astype(
            jnp.bfloat16
        ),
        "tp",
        scatter_dimension=0,
        tiled=True,
    ).astype(jnp.float32)
    unused_second, modulate_second = jax.vjp(modulate, after_attn, shift_two, scale_two)
    resid_second, shift_two_grad, scale_two_grad = modulate_second(normed_two_grad)
    after_grad = out_grad + resid_second
    attn_grad = (gate_one * after_grad).astype(low_type)
    gate_one_grad = jnp.sum(after_grad * attn_branch, axis=0)
    attn_grad_full = lax.all_gather(attn_grad, "tp", axis=0, tiled=True)
    heads_out_grad = jnp.einsum(
        "sbd,cd->bsc", attn_grad_full, merge_back, preferred_element_type=jnp.float32
    ).astype(low_type)
    merge_grad = jnp.einsum(
        "sbc,sbd->cd", mixed_heads, attn_grad_full, preferred_element_type=jnp.float32
    )

    def backward_latent(parts):
        return attend_backward(parts[0], parts[1], parts[2], parts[3], parts[4])

    query_grad, keys_grad, values_grad = lax.map(
        backward_latent,
        (
            split[:, :, 0],
            split[:, :, 1],
            split[:, :, 2],
            heads_out_grad.reshape(latent_count, seq_total, heads_local, HEAD),
            logsum,
        ),
    )
    triple_grad = jnp.stack((query_grad, keys_grad, values_grad), axis=2).reshape(
        latent_count, seq_total, 3, width_local
    )
    heads_grad = jnp.einsum(
        "sbd,bstc->tdc", normed_full, triple_grad, preferred_element_type=jnp.float32
    )
    normed_one_grad = lax.psum_scatter(
        jnp.einsum(
            "bstc,tdc->sbd", triple_grad, heads_back, preferred_element_type=jnp.float32
        ).astype(jnp.bfloat16),
        "tp",
        scatter_dimension=0,
        tiled=True,
    ).astype(jnp.float32)
    unused_first, modulate_first = jax.vjp(modulate, latents_in, shift_one, scale_one)
    resid_first, shift_one_grad, scale_one_grad = modulate_first(normed_one_grad)
    latents_grad = after_grad + resid_first
    modulation_grad = jnp.stack(
        (
            shift_one_grad,
            scale_one_grad,
            gate_one_grad,
            shift_two_grad,
            scale_two_grad,
            gate_two_grad,
        ),
        axis=1,
    )
    modulation_share = lax.psum_scatter(modulation_grad, "tp", scatter_dimension=2, tiled=True)
    cond_grad = jnp.einsum(
        "bd,bkc->dkc",
        activated.astype(jnp.float32),
        modulation_share,
        precision=lax.Precision.HIGHEST,
    )
    sums = (
        lax.psum_scatter(
            cond_grad.astype(jnp.bfloat16), "fsdp", scatter_dimension=0, tiled=True
        ).astype(jnp.float32),
        lax.psum_scatter(
            heads_grad.astype(jnp.bfloat16), "fsdp", scatter_dimension=1, tiled=True
        ).astype(jnp.float32),
        lax.psum_scatter(
            merge_grad.astype(jnp.bfloat16), "fsdp", scatter_dimension=1, tiled=True
        ).astype(jnp.float32),
        lax.psum_scatter(
            up_grad.astype(jnp.bfloat16), "fsdp", scatter_dimension=0, tiled=True
        ).astype(jnp.float32),
        lax.psum_scatter(
            down_grad.astype(jnp.bfloat16), "fsdp", scatter_dimension=1, tiled=True
        ).astype(jnp.float32),
    )
    cond_new = adam_step(condition_weight, condition_first, condition_second, sums[0], 0.02)
    heads_new = adam_step(heads_weight, heads_first, heads_second, sums[1], 0.02)
    merge_new = adam_step(merge_weight, merge_first, merge_second, sums[2], 0.15)
    up_new = adam_step(up_weight, up_first, up_second, sums[3], 0.02)
    down_new = adam_step(down_weight, down_first, down_second, sums[4], 0.01)
    return (
        block_out,
        latents_grad,
        cond_new[0],
        cond_new[1],
        cond_new[2],
        heads_new[0],
        heads_new[1],
        heads_new[2],
        merge_new[0],
        merge_new[1],
        merge_new[2],
        up_new[0],
        up_new[1],
        up_new[2],
        down_new[0],
        down_new[1],
        down_new[2],
    )


def solution(mesh):
    in_specs = (
        P("tp", "fsdp", None),
        P("fsdp", None),
        P("tp", "fsdp", None),
        P("fsdp", None, "tp"),
        P("fsdp", None, "tp"),
        P("fsdp", None, "tp"),
        P(None, "fsdp", "tp"),
        P(None, "fsdp", "tp"),
        P(None, "fsdp", "tp"),
        P("tp", "fsdp"),
        P("tp", "fsdp"),
        P("tp", "fsdp"),
        P("fsdp", "tp"),
        P("fsdp", "tp"),
        P("fsdp", "tp"),
        P("tp", "fsdp"),
        P("tp", "fsdp"),
        P("tp", "fsdp"),
    )
    out_specs = (
        P("tp", "fsdp", None),
        P("tp", "fsdp", None),
        P("fsdp", None, "tp"),
        P("fsdp", None, "tp"),
        P("fsdp", None, "tp"),
        P(None, "fsdp", "tp"),
        P(None, "fsdp", "tp"),
        P(None, "fsdp", "tp"),
        P("tp", "fsdp"),
        P("tp", "fsdp"),
        P("tp", "fsdp"),
        P("fsdp", "tp"),
        P("fsdp", "tp"),
        P("fsdp", "tp"),
        P("tp", "fsdp"),
        P("tp", "fsdp"),
        P("tp", "fsdp"),
    )
    return jax.shard_map(local, mesh=mesh, in_specs=in_specs, out_specs=out_specs, check_vma=False)
```

profile of v0, /device:TPU:0, one launch (start us, length us, event | category | flops | bytes accessed | tf_op | source)
XLA Modules:
  0.0 1125.7 jit_solution(16114503766555872705)
XLA Ops:
  13.4 62.1 %all-gather.11.cloned.1.call-done = bf16[1024,6,512]{2,0,1:T(8,128)(2,1)} async-done(((bf16[64,6,512]{2,0,1:T(8,128)(2,1)}), bf16[1024,6,512]{2,0,1:T(8,128)(2,1)}) %all-gather.11.cloned.1.call-update) | async-done | bytes 6291472 | tf_op jit(solution)/shard_map/all_gather | solution.py:128
  87.7 34.6 %all-gather.15.cloned.1.call-done = bf16[3,1024,512]{2,1,0:T(8,128)(2,1)} async-done(((bf16[3,64,512]{2,1,0:T(8,128)(2,1)}), bf16[3,1024,512]{2,1,0:T(8,128)(2,1)}) %all-gather.15.cloned.1.call-update) | async-done | bytes 3145744 | tf_op jit(solution)/shard_map/all_gather | solution.py:129
  122.3 34.1 %all-gather.13.cloned.1.call-done = bf16[1024,1,1024]{2,0,1:T(8,128)(2,1)} async-done(((bf16[512,1,1024]{2,0,1:T(8,128)(2,1)}), bf16[1024,1,1024]{2,0,1:T(8,128)(2,1)}) %all-gather.13.cloned.1.call-update) | async-done | bytes 2097168 | tf_op jit(solution)/shard_map/all_gather | solution.py:146
  167.8 22.6 %while.47 = (s32[]{:T(128)}, bf16[2,512,8,64]{1,3,2,0:T(8,128)(2,1)}, f32[2,8,512]{2,1,0:T(8,128)S(1)}, bf16[2,512,8,64]{1,3,2,0:T(8,128)(2,1)S(1)}, bf16[1024,8...) while((s32[]{:T(128)}, bf16[2,512,8,64]{1,3,2,0:T(8,128)(2,1)}, ...), condition=%wide.region_5.6_spmd, body=%wide.region_2.5_spmd.sunk | while | flops 1111748608 | bytes 66191540 | solution.py:50
  203.2 28.9 %reduce-scatter.10.cloned.1.call-done = bf16[512,1,1024]{2,0,1:T(8,128)(2,1)} async-done(((bf16[1024,1,1024]{2,0,1:T(8,128)(2,1)}), bf16[512,1,1024]{2,0,1:T(8,128)(2,1)}) %reduce-scatter.10.cloned.1.call-update) | async-done | bytes 1048592 | tf_op jit(solution)/shard_map/reduce_scatter | solution.py:160
  238.1 47.4 %all-gather.21.cloned.1.call-done = bf16[1024,2048]{1,0:T(8,128)(2,1)} async-done(((bf16[64,2048]{1,0:T(8,128)(2,1)}), bf16[1024,2048]{1,0:T(8,128)(2,1)}) %all-gather.21.cloned.1.call-update) | async-done | bytes 4194320 | tf_op jit(solution)/shard_map/all_gather | solution.py:131
  285.5 33.8 %all-gather.19.cloned.1.call-done = bf16[1024,1,1024]{2,0,1:T(8,128)(2,1)} async-done(((bf16[512,1,1024]{2,0,1:T(8,128)(2,1)}), bf16[1024,1,1024]{2,0,1:T(8,128)(2,1)}) %all-gather.19.cloned.1.call-update) | async-done | bytes 2097168 | tf_op jit(solution)/shard_map/all_gather | solution.py:170
  319.3 10.6 fusion.64
  329.9 43.1 %all-gather.23.cloned.1.call-done = bf16[2048,1024]{0,1:T(8,128)(2,1)} async-done(((bf16[2048,64]{0,1:T(8,128)(2,1)}), bf16[2048,1024]{0,1:T(8,128)(2,1)}) %all-gather.23.cloned.1.call-update) | async-done | bytes 4194320 | tf_op jit(solution)/shard_map/all_gather | solution.py:132
  373.1 11.0 convert_bitcast_fusion.2
  384.1 30.4 %reduce-scatter.12.cloned.1.call-done = bf16[512,1,1024]{2,0,1:T(8,128)(2,1)} async-done(((bf16[1024,1,1024]{2,0,1:T(8,128)(2,1)}), bf16[512,1,1024]{2,0,1:T(8,128)(2,1)}) %reduce-scatter.12.cloned.1.call-update) | async-done | bytes 1048592 | tf_op jit(solution)/shard_map/reduce_scatter | solution.py:173
  419.0 33.0 %all-gather.25.cloned.1.call-done = bf16[1024,1,1024]{2,0,1:T(8,128)(2,1)} async-done(((bf16[512,1,1024]{2,0,1:T(8,128)(2,1)}), bf16[1024,1,1024]{2,0,1:T(8,128)(2,1)}) %all-gather.25.cloned.1.call-update) | async-done | bytes 2097168 | tf_op jit(solution)/shard_map/all_gather | solution.py:190
  452.1 12.5 %fusion.41 = bf16[1024,2048]{1,0:T(8,128)(2,1)S(1)} fusion(f32[1024,2048]{1,0:T(8,128)} %fusion.64, bf16[2048,1024]{0,1:T(8,128)(2,1)} %all-gather.23.cloned.1.call-done, bf16[1024,1,1024]{2,0,1:T(8,128)(2,1)} %all-gather.25.cloned.1.call-done), kind=kOutput, calls=%fused_computation.52 | convolution fusion | flops 4336910336 | bytes 18874368 | tf_op jit(solution)/shard_map/sbd,fd->sbf/dot_general | solution.py:191
  472.4 31.9 %reduce-scatter.14.cloned.1.call-done = bf16[512,1,1024]{2,0,1:T(8,128)(2,1)} async-done(((bf16[1024,1,1024]{2,0,1:T(8,128)(2,1)}), bf16[512,1,1024]{2,0,1:T(8,128)(2,1)}) %reduce-scatter.14.cloned.1.call-update) | async-done | bytes 1048592 | tf_op jit(solution)/shard_map/reduce_scatter | solution.py:198
  515.5 33.2 %all-gather.27.cloned.1.call-done = bf16[1024,1,1024]{2,0,1:T(8,128)(2,1)} async-done(((bf16[512,1,1024]{2,0,1:T(8,128)(2,1)}), bf16[1024,1,1024]{2,0,1:T(8,128)(2,1)}) %all-gather.27.cloned.1.call-update) | async-done | bytes 2097168 | tf_op jit(solution)/shard_map/all_gather | solution.py:211
  561.5 76.5 %while.48 = (s32[]{:T(128)}, f32[1024,8,64]{0,2,1:T(8,128)}, f32[1024,8,64]{0,2,1:T(8,128)}, bf16[2,512,8,64]{1,3,2,0:T(8,128)(2,1)}, bf16[2,512,8,64]{1,3,2,0:T...) while((s32[]{:T(128)}, f32[1024,8,64]{0,2,1:T(8,128)}, ...), condition=%wide.region_15.16_spmd.clone, body=%wide.region_13.15_spmd.clone.sunk | while | flops 2737827840 | bytes 177848528 | solution.py:93
  578.0 10.4 multiply_convert_fusion.8
  655.3 31.9 %reduce-scatter.16.cloned.1.call-done = bf16[512,1,1024]{2,0,1:T(8,128)(2,1)} async-done(((bf16[1024,1,1024]{2,0,1:T(8,128)(2,1)}), bf16[512,1,1024]{2,0,1:T(8,128)(2,1)}) %reduce-scatter.16.cloned.1.call-update) | async-done | bytes 1048592 | tf_op jit(solution)/shard_map/reduce_scatter | solution.py:238
  691.8 10.7 convolution_convert_fusion
  745.0 32.8 %reduce-scatter.26.cloned.1.call-done = bf16[2048,64]{0,1:T(8,128)(2,1)} async-done(((bf16[2048,1024]{0,1:T(8,128)(2,1)}), bf16[2048,64]{0,1:T(8,128)(2,1)}) %reduce-scatter.26.cloned.1.call-update) | async-done | bytes 262160 | tf_op jit(solution)/shard_map/reduce_scatter | solution.py:280
  780.7 72.9 %reduce-scatter.24.cloned.1.call-done = bf16[64,2048]{1,0:T(8,128)(2,1)} async-done(((bf16[1024,2048]{1,0:T(8,128)(2,1)}), bf16[64,2048]{1,0:T(8,128)(2,1)}) %reduce-scatter.24.cloned.1.call-update) | async-done | bytes 262160 | tf_op jit(solution)/shard_map/reduce_scatter | solution.py:277
  856.4 111.1 %all-reduce.3.cloned.1.call-done = bf16[3,1024,512]{2,0,1:T(4,128)(2,1)} async-done(((bf16[3,1024,512]{2,0,1:T(4,128)(2,1)}), bf16[3,1024,512]{2,0,1:T(4,128)(2,1)}) %all-reduce.3.cloned.1.call-update) | async-done | bytes 3145744
  969.3 58.5 %reduce-scatter.22.cloned.1.call-done = bf16[512,64]{0,1:T(8,128)(2,1)} async-done(((bf16[512,1024]{0,1:T(8,128)(2,1)}), bf16[512,64]{0,1:T(8,128)(2,1)}) %reduce-scatter.22.cloned.1.call-update) | async-done | bytes 65552 | tf_op jit(solution)/shard_map/reduce_scatter | solution.py:274
  1037.3 78.8 %reduce-scatter.20.cloned.1.call-done = bf16[64,6,512]{2,0,1:T(8,128)(2,1)} async-done(((bf16[1024,6,512]{2,0,1:T(8,128)(2,1)}), bf16[64,6,512]{2,0,1:T(8,128)(2,1)}) %reduce-scatter.20.cloned.1.call-update) | async-done | bytes 393232 | tf_op jit(solution)/shard_map/reduce_scatter | solution.py:268
  (232 shorter events, 256.2 us)
Async XLA Ops:
  7.2 68.3 %all-gather.11.cloned.1.call-start = ((), (), s32[]{:S(2)}) async-start(), calls=%async_computation.9 | async-start | bytes 6684672 | tf_op jit(solution)/shard_map/all_gather | solution.py:128
  9.3 113.0 %all-gather.15.cloned.1.call-start = ((), (), s32[]{:S(2)}) async-start(), calls=%async_computation.11 | async-start | bytes 3342336 | tf_op jit(solution)/shard_map/all_gather | solution.py:129
  11.1 145.3 %all-gather.13.cloned.1.call-start = ((), (), s32[]{:S(2)}) async-start(), calls=%async_computation.10 | async-start | bytes 3145728 | tf_op jit(solution)/shard_map/all_gather | solution.py:146
  12.9 71.3 %copy-start.27 = (f32[512]{0:T(512)}, f32[512]{0:T(512)S(1)}, u32[]{:S(2)}) copy-start(f32[512]{0:T(512)S(1)} %broadcast_multiply_fusion.1) | copy-start | bytes 6148
  86.4 110.6 %all-gather.17.cloned.1.call-start = ((), (), s32[]{:S(2)}) async-start(), calls=%async_computation.12 | async-start | bytes 1114112 | tf_op jit(solution)/shard_map/all_gather | solution.py:130
  87.1 145.0 %reduce-scatter.10.cloned.1.call-start = ((), (), s32[]{:S(2)}) async-start(), calls=%async_computation.13 | async-start | bytes 3145728 | tf_op jit(solution)/shard_map/reduce_scatter | solution.py:160
  201.2 84.3 %all-gather.21.cloned.1.call-start = ((), (), s32[]{:S(2)}) async-start(), calls=%async_computation.15 | async-start | bytes 4456448 | tf_op jit(solution)/shard_map/all_gather | solution.py:131
  202.9 116.4 %all-gather.19.cloned.1.call-start = ((), (), s32[]{:S(2)}) async-start(), calls=%async_computation.14 | async-start | bytes 3145728 | tf_op jit(solution)/shard_map/all_gather | solution.py:170
  237.2 135.8 %all-gather.23.cloned.1.call-start = ((), (), s32[]{:S(2)}) async-start(), calls=%async_computation.16 | async-start | bytes 4456448 | tf_op jit(solution)/shard_map/all_gather | solution.py:132
  238.0 176.5 %reduce-scatter.12.cloned.1.call-start = ((), (), s32[]{:S(2)}) async-start(), calls=%async_computation.17 | async-start | bytes 3145728 | tf_op jit(solution)/shard_map/reduce_scatter | solution.py:173
  384.1 68.0 %all-gather.25.cloned.1.call-start = ((), (), s32[]{:S(2)}) async-start(), calls=%async_computation.18 | async-start | bytes 3145728 | tf_op jit(solution)/shard_map/all_gather | solution.py:190
  418.8 85.6 %reduce-scatter.14.cloned.1.call-start = ((), (), s32[]{:S(2)}) async-start(), calls=%async_computation.19 | async-start | bytes 3145728 | tf_op jit(solution)/shard_map/reduce_scatter | solution.py:198
  472.4 76.3 %all-gather.27.cloned.1.call-start = ((), (), s32[]{:S(2)}) async-start(), calls=%async_computation.20 | async-start | bytes 3145728 | tf_op jit(solution)/shard_map/all_gather | solution.py:211
  515.4 171.8 %reduce-scatter.16.cloned.1.call-start = ((), (), s32[]{:S(2)}) async-start(), calls=%async_computation.21 | async-start | bytes 3145728 | tf_op jit(solution)/shard_map/reduce_scatter | solution.py:238
  655.3 77.4 %reduce-scatter.18.cloned.1.call-start = ((), (), s32[]{:S(2)}) async-start(), calls=%async_computation.22 | async-start | bytes 49152 | tf_op jit(solution)/shard_map/reduce_scatter | solution.py:260
  691.8 86.0 %reduce-scatter.26.cloned.1.call-start = ((), (), s32[]{:S(2)}) async-start(), calls=%async_computation.26 | async-start | bytes 4456448 | tf_op jit(solution)/shard_map/reduce_scatter | solution.py:280
  702.6 151.0 %reduce-scatter.24.cloned.1.call-start = ((), (), s32[]{:S(2)}) async-start(), calls=%async_computation.25 | async-start | bytes 4456448 | tf_op jit(solution)/shard_map/reduce_scatter | solution.py:277
  712.3 255.3 %all-reduce.3.cloned.1.call-start = ((), (), s32[]{:S(2)}) async-start(), calls=%async_computation.27 | async-start | bytes 8388608
  728.1 299.8 %reduce-scatter.22.cloned.1.call-start = ((), (), s32[]{:S(2)}) async-start(), calls=%async_computation.24 | async-start | bytes 1114112 | tf_op jit(solution)/shard_map/reduce_scatter | solution.py:274
  732.4 383.7 %reduce-scatter.20.cloned.1.call-start = ((), (), s32[]{:S(2)}) async-start(), calls=%async_computation.23 | async-start | bytes 6684672 | tf_op jit(solution)/shard_map/reduce_scatter | solution.py:268
  780.7 249.2 %copy-start.18 = (f32[3,64,512]{2,1,0:T(8,128)S(1)}, f32[3,64,512]{2,1,0:T(8,128)}, u32[]{:S(2)}) copy-start(f32[3,64,512]{2,1,0:T(8,128)} %param.28) | copy-start | bytes 1179652
  1033.8 82.3 %copy-start.15 = (f32[64,6,512]{2,0,1:T(8,128)S(1)}, f32[64,6,512]{2,0,1:T(8,128)}, u32[]{:S(2)}) copy-start(f32[64,6,512]{2,0,1:T(8,128)} %param.25) | copy-start | bytes 2359300
  1033.8 82.3 %copy-start.21 = (f32[64,6,512]{2,0,1:T(8,128)S(1)}, f32[64,6,512]{2,0,1:T(8,128)}, u32[]{:S(2)}) copy-start(f32[64,6,512]{2,0,1:T(8,128)} %param.26) | copy-start | bytes 2359300
  1033.8 82.3 %copy-start.22 = (f32[64,6,512]{2,0,1:T(8,128)S(1)}, f32[64,6,512]{2,0,1:T(8,128)}, u32[]{:S(2)}) copy-start(f32[64,6,512]{2,0,1:T(8,128)} %param.27) | copy-start | bytes 2359300
  (45 other events, 533.7 us)
Sparse Core Ops, SparseCore 0:
  10.8 64.6 all-gather.10
  78.2 44.0 all-gather.14
  124.4 31.9 all-gather.12
  159.0 37.9 all-gather.16
  201.3 30.7 reduce-scatter.9
  234.9 50.5 all-gather.20
  287.7 31.6 all-gather.18
  322.3 50.7 all-gather.22
  384.2 30.3 reduce-scatter.11
  418.9 33.1 all-gather.24
  472.5 31.8 reduce-scatter.13
  515.5 33.1 all-gather.26
  655.4 31.8 reduce-scatter.15
  691.9 9.8 reduce-scatter.17
  705.5 72.2 reduce-scatter.25
  782.0 71.5 reduce-scatter.23
  857.1 110.3 all-reduce.2
  971.5 56.3 reduce-scatter.21
  1031.8 84.2 reduce-scatter.19
where the time goes:
time: 1130 us
  waiting for transfers between devices  802 us (71%)
  matrix products  166 us (15%)
  other arithmetic  83.5 us (7%)
  local copies, waits for them, and re-layouts  51.8 us (5%)
  between operations  15.4 us (1%)
    unnamed x20, waiting for transfers between devices  111 us
    reduce_scatter x1, waiting for transfers between devices, local(): lax.psum_scatter(cond_grad.astype(jnp.bfloat16), 'fsdp', scatter_dimensio...  78.8 us
    reduce_scatter x1, waiting for transfers between devices, local(): lax.psum_scatter(up_grad.astype(jnp.bfloat16), 'fsdp', scatter_dimension=...  72.9 us
    all_gather x1, waiting for transfers between devices, local(): lax.all_gather(condition_weight.astype(low_type), 'fsdp', axis=0, tiled=T...  62.1 us
    reduce_scatter x1, waiting for transfers between devices, local(): lax.psum_scatter(merge_grad.astype(jnp.bfloat16), 'fsdp', scatter_dimensi...  58.5 us
    all_gather x1, waiting for transfers between devices, local(): lax.all_gather(up_weight.astype(low_type), 'fsdp', axis=0, tiled=True)  47.4 us
    all_gather x1, waiting for transfers between devices, local(): lax.all_gather(down_weight.astype(low_type), 'fsdp', axis=1, tiled=True)  43.1 us
    all_gather x1, waiting for transfers between devices, local(): lax.all_gather(heads_weight.astype(low_type), 'fsdp', axis=1, tiled=True)  34.6 us
  transfers between devices with their start and end apart: 19, of which 18 were waited for; matrix products, arithmetic and copies ran while one was open for 12% of the time, Pallas kernels for 0%

commit v1 on v0

v1 whole, which is shorter than its diff:
```python
import functools

import jax
import jax.numpy as jnp
from jax import lax
from jax.experimental import pallas as pl
from jax.experimental.pallas import tpu as pltpu
from jax.sharding import PartitionSpec as P

HEAD = 64
PAIR = 2 * HEAD
STEP = 5
LOW = jnp.bfloat16
FULL = jnp.float32
NT = (((1,), (1,)), ((), ()))
TN = (((0,), (0,)), ((), ()))


def params(limit=56):
    return pltpu.CompilerParams(vmem_limit_bytes=limit * 1024 * 1024)


def cost(flops, moved, raised=0):
    return pl.CostEstimate(flops=int(flops), bytes_accessed=int(moved), transcendentals=int(raised))


def resident(shape):
    return pl.BlockSpec(shape, lambda *step: (0,) * len(shape))


def fit(width, most):
    return next(tile for tile in (most, 512, 256, PAIR) if tile <= most and width % tile == 0)


def product(left, right, out_type, start=0, width=None):
    rows, depth = left.shape
    width = width or right.shape[1]
    tile = fit(width, 512)
    first = start // tile

    def body(left_ref, right_ref, out_ref):
        out_ref[...] = jnp.dot(
            left_ref[...], right_ref[...], preferred_element_type=FULL
        ).astype(out_type)

    return pl.pallas_call(
        body,
        grid=(width // tile,),
        in_specs=[
            resident((rows, depth)),
            pl.BlockSpec((depth, tile), lambda j: (0, first + j)),
        ],
        out_specs=pl.BlockSpec((rows, tile), lambda j: (0, j)),
        out_shape=jax.ShapeDtypeStruct((rows, width), out_type),
        compiler_params=params(),
        cost_estimate=cost(2 * rows * depth * width, 2 * (rows * depth + depth * width) + 4 * rows * width),
        name="product",
    )(left, right)


def product_back(lefts, right, out_type):
    rows = lefts[0].shape[0]
    width, depth = right.shape
    tile = min(256, width)

    def body(*refs):
        total = None
        start = 0
        for left_ref in refs[:-2]:
            extent = left_ref.shape[1]
            term = lax.dot_general(
                left_ref[...], refs[-2][:, start : start + extent], NT, preferred_element_type=FULL
            )
            total = term if total is None else total + term
            start += extent
        refs[-1][...] = total.astype(out_type)

    return pl.pallas_call(
        body,
        grid=(width // tile,),
        in_specs=[resident(left.shape) for left in lefts]
        + [pl.BlockSpec((tile, depth), lambda j: (j, 0))],
        out_specs=pl.BlockSpec((rows, tile), lambda j: (0, j)),
        out_shape=jax.ShapeDtypeStruct((rows, width), out_type),
        compiler_params=params(),
        cost_estimate=cost(2 * rows * depth * width, 2 * (rows * depth + width * depth) + 4 * rows * width),
        name="product_back",
    )(*lefts, right)


def token_sum(jobs, count, ordered=True):
    depth = jobs[0][0][0].shape[1]
    widths = [rights[0].shape[1] for _, rights in jobs]
    width = sum(widths)
    tokens = max(sum(left.shape[0] for left in lefts) for lefts, _ in jobs)
    tile = min(fit(extent, 512) for extent in widths)
    deep, across, cores = digits(count)
    group = depth // count
    pieces = len(jobs[0][0])
    starts = [sum(widths[:index]) // tile for index in range(len(jobs) + 1)]

    def flip(left_refs, turned):
        me = lax.axis_index("fsdp")
        my_z, my_x, my_c = me // (across * cores), (me // cores) % across, me % cores
        start = 0
        for left_ref in left_refs:
            flipped = left_ref[...].T
            extent = left_ref.shape[0]
            if not ordered:
                turned[:, start : start + extent] = flipped
            for source in range(count if ordered else 0):
                z, x, c = source // (across * cores), (source // cores) % across, source % cores
                place = (
                    ((c - my_c + cores) % cores) * across + (x - my_x + across) % across
                ) * deep + (z - my_z + deep) % deep
                turned[pl.ds(pl.multiple_of(place * group, group), group), start : start + extent] = (
                    flipped[source * group : (source + 1) * group]
                )
            start += extent

    def body(*refs):
        out_refs, turned = refs[2 * pieces * len(jobs) : -1], refs[-1]
        step = pl.program_id(0)
        for index in range(len(jobs)):
            mine = refs[2 * pieces * index : 2 * pieces * (index + 1)]

            @pl.when(step == starts[index])
            def _():
                flip(mine[:pieces], turned)

            @pl.when((step >= starts[index]) & (step < starts[index + 1]))
            def _():
                total = None
                start = 0
                for right_ref in mine[pieces:]:
                    extent = right_ref.shape[0]
                    term = jnp.dot(
                        turned[:, start : start + extent], right_ref[...], preferred_element_type=FULL
                    )
                    total = term if total is None else total + term
                    start += extent
                total = total.astype(LOW)
                start = 0
                for out_ref in out_refs:
                    out_ref[...] = total[start : start + out_ref.shape[0]]
                    start += out_ref.shape[0]

    def place_of(index):
        last = widths[index] // tile - 1
        return lambda j: (0, jnp.clip(j - starts[index], 0, last))

    half = depth // cores
    heights = (half, depth - half) if ordered else (depth,)
    in_specs = []
    operands = []
    for index, (lefts, rights) in enumerate(jobs):
        in_specs += [resident(left.shape) for left in lefts]
        in_specs += [pl.BlockSpec((right.shape[0], tile), place_of(index)) for right in rights]
        operands += [*lefts, *rights]
    return pl.pallas_call(
        body,
        grid=(width // tile,),
        in_specs=in_specs,
        out_specs=[pl.BlockSpec((height, tile), lambda j: (0, j)) for height in heights],
        out_shape=[jax.ShapeDtypeStruct((height, width), LOW) for height in heights],
        scratch_shapes=[pltpu.VMEM((depth, tokens), LOW)],
        compiler_params=params(),
        cost_estimate=cost(
            2 * depth * tokens * width, 2 * (len(jobs) * depth * tokens + tokens * width + depth * width)
        ),
        name="token_sum",
    )(*operands)


def head_lanes():
    lane = lax.broadcasted_iota(jnp.int32, (1, PAIR), 1)
    first = (lane < HEAD).astype(FULL)
    return lane, ((first, HEAD), (1.0 - first, 0))


def in_lanes(lane, free, column):
    total = 0.0
    for index in range(3):
        piece = column.astype(LOW).astype(FULL)
        total = total + jnp.where(lane == free + index, piece, 0.0)
        column = column - piece
    return total


def ones_in_lanes(lane, free, values):
    return jnp.where((lane >= free) & (lane < free + 3), 1.0, values.astype(FULL)).astype(LOW)


def attend_forward(triple, width):
    tokens = triple.shape[0]
    pairs = width // PAIR
    block = min(512, tokens)
    scaling = HEAD ** (-0.5)

    def body(query_ref, keys_ref, values_ref, out_ref, level_ref):
        lane, heads = head_lanes()
        keys = keys_ref[...]
        values = values_ref[...].astype(FULL)
        query = query_ref[...].astype(FULL)
        total = level = 0.0
        for mask, free in heads:
            scores = lax.dot_general(
                (query * (mask * scaling)).astype(LOW), keys, NT, preferred_element_type=FULL
            )
            peak = jnp.max(scores, axis=-1, keepdims=True)
            raised = jnp.exp(scores - peak).astype(LOW)
            counted = jnp.where(lane == free, 1.0, values * mask).astype(LOW)
            mixed = jnp.dot(raised, counted, preferred_element_type=FULL)
            sums = mixed[:, free : free + 1]
            total = total + mixed * mask / sums
            level = level + mask * (peak + jnp.log(sums))
        out_ref[...] = total.astype(LOW)
        level_ref[...] = level

    return pl.pallas_call(
        body,
        grid=(pairs, tokens // block),
        in_specs=[
            pl.BlockSpec((block, PAIR), lambda h, i: (i, h)),
            pl.BlockSpec((tokens, PAIR), lambda h, i: (0, pairs + h)),
            pl.BlockSpec((tokens, PAIR), lambda h, i: (0, 2 * pairs + h)),
        ],
        out_specs=[pl.BlockSpec((block, PAIR), lambda h, i: (i, h))] * 2,
        out_shape=[
            jax.ShapeDtypeStruct((tokens, width), LOW),
            jax.ShapeDtypeStruct((tokens, width), FULL),
        ],
        compiler_params=params(),
        cost_estimate=cost(16 * tokens * tokens * width, 12 * tokens * width, tokens * tokens * width // HEAD),
        name="attend_forward",
    )(triple, triple, triple)


def attend_backward(triple, attended, level, grads, width):
    tokens = triple.shape[0]
    pairs = width // PAIR
    block = min(512, tokens)
    steps = tokens // block
    scaling = HEAD ** (-0.5)

    def body(query_ref, keys_ref, values_ref, out_low_ref, level_ref, grad_ref, out_ref, key_sum, value_sum):
        pair = pl.program_id(0)
        step = pl.program_id(1)
        lane, heads = head_lanes()
        keys = keys_ref[...]
        values = values_ref[...]
        query = query_ref[...].astype(FULL)
        grad = grad_ref[...].astype(FULL)
        inner = grad * out_low_ref[...].astype(FULL)
        query_grad = key_grad = value_grad = None
        for index, (mask, free) in enumerate(heads):
            own = HEAD * index
            query_part = query * (mask * scaling)
            grad_part = grad * mask
            probs = jnp.exp(
                lax.dot_general(
                    ones_in_lanes(lane, free, keys),
                    (query_part - in_lanes(lane, free, level_ref[:, own : own + 1])).astype(LOW),
                    NT,
                    preferred_element_type=FULL,
                )
            )
            prob_grad = lax.dot_general(
                ones_in_lanes(lane, free, values),
                (
                    grad_part - in_lanes(lane, free, jnp.sum(inner * mask, axis=-1, keepdims=True))
                ).astype(LOW),
                NT,
                preferred_element_type=FULL,
            )
            score_grad = (probs * prob_grad).astype(LOW)
            value_part = jnp.dot(probs.astype(LOW), grad_part.astype(LOW), preferred_element_type=FULL)
            key_part = jnp.dot(score_grad, query_part.astype(LOW), preferred_element_type=FULL)
            asked_part = lax.dot_general(
                score_grad, keys * (mask * scaling).astype(LOW), TN, preferred_element_type=FULL
            )
            if query_grad is None:
                query_grad, key_grad, value_grad = asked_part, key_part, value_part
            else:
                query_grad, key_grad, value_grad = (
                    query_grad + asked_part,
                    key_grad + key_part,
                    value_grad + value_part,
                )

        @pl.when(step == 0)
        def _():
            key_sum[...] = key_grad
            value_sum[...] = value_grad

        @pl.when(step > 0)
        def _():
            key_sum[...] += key_grad
            value_sum[...] += value_grad

        rows = pl.ds(pl.multiple_of(step * block, block), block)
        out_ref[rows, pl.ds(pl.multiple_of(pair * PAIR, PAIR), PAIR)] = query_grad.astype(LOW)

        @pl.when(step == steps - 1)
        def _():
            out_ref[:, pl.ds(pl.multiple_of(width + pair * PAIR, PAIR), PAIR)] = key_sum[...].astype(LOW)
            out_ref[:, pl.ds(pl.multiple_of(2 * width + pair * PAIR, PAIR), PAIR)] = value_sum[
                ...
            ].astype(LOW)

    rows_of_pair = pl.BlockSpec((block, PAIR), lambda h, i: (i, h))
    return pl.pallas_call(
        body,
        grid=(pairs, steps),
        in_specs=[
            rows_of_pair,
            pl.BlockSpec((tokens, PAIR), lambda h, i: (0, pairs + h)),
            pl.BlockSpec((tokens, PAIR), lambda h, i: (0, 2 * pairs + h)),
            rows_of_pair,
            rows_of_pair,
            rows_of_pair,
        ],
        out_specs=resident((tokens, 3 * width)),
        out_shape=jax.ShapeDtypeStruct((tokens, 3 * width), LOW),
        scratch_shapes=[pltpu.VMEM((tokens, PAIR), FULL), pltpu.VMEM((tokens, PAIR), FULL)],
        compiler_params=params(),
        cost_estimate=cost(40 * tokens * tokens * width, 20 * tokens * width, tokens * tokens * width // HEAD),
        name="attend_backward",
    )(triple, triple, triple, attended, level, grads)


def feed_both(normed, branch_grad, weights, out_type):
    tokens, depth = normed.shape
    units = weights.shape[1] // 2
    tile = min(512, units)
    steps = units // tile

    def body(normed_ref, grad_ref, up_ref, down_ref, out_ref, back_ref, hidden_ref, pre_ref, out_sum, back_sum):
        step = pl.program_id(0)
        up = up_ref[...]
        down = down_ref[...]
        pre = jnp.dot(normed_ref[...], up, preferred_element_type=FULL)
        hidden_grad = jnp.dot(grad_ref[...], down, preferred_element_type=FULL)
        square = pre * pre
        bent = jnp.tanh(0.7978845608028654 * (pre + 0.044715 * (square * pre)))
        half = 0.5 * (1.0 + bent)
        hidden = (pre * half).astype(LOW)
        slope = half + 0.5 * pre * (1.0 - bent * bent) * (
            0.7978845608028654 * (1.0 + 0.134145 * square)
        )
        pre_grad = (hidden_grad * slope).astype(LOW)
        hidden_ref[...] = hidden
        pre_ref[...] = pre_grad
        out_part = lax.dot_general(hidden, down, NT, preferred_element_type=FULL)
        back_part = lax.dot_general(pre_grad, up, NT, preferred_element_type=FULL)

        @pl.when(step == 0)
        def _():
            out_sum[...] = out_part
            back_sum[...] = back_part

        @pl.when(step > 0)
        def _():
            out_sum[...] += out_part
            back_sum[...] += back_part

        @pl.when(step == steps - 1)
        def _():
            out_ref[...] = out_sum[...].astype(out_type)
            back_ref[...] = back_sum[...].astype(out_type)

    return pl.pallas_call(
        body,
        grid=(steps,),
        in_specs=[
            resident((tokens, depth)),
            resident((tokens, depth)),
            pl.BlockSpec((depth, tile), lambda j: (0, j)),
            pl.BlockSpec((depth, tile), lambda j: (0, steps + j)),
        ],
        out_specs=[
            resident((tokens, depth)),
            resident((tokens, depth)),
            pl.BlockSpec((tokens, tile), lambda j: (0, j)),
            pl.BlockSpec((tokens, tile), lambda j: (0, j)),
        ],
        out_shape=[
            jax.ShapeDtypeStruct((tokens, depth), out_type),
            jax.ShapeDtypeStruct((tokens, depth), out_type),
            jax.ShapeDtypeStruct((tokens, units), LOW),
            jax.ShapeDtypeStruct((tokens, units), LOW),
        ],
        scratch_shapes=[pltpu.VMEM((tokens, depth), FULL), pltpu.VMEM((tokens, depth), FULL)],
        compiler_params=params(),
        cost_estimate=cost(8 * tokens * depth * units, 4 * depth * units + 12 * tokens * depth + 4 * tokens * units, tokens * units),
        name="feed_both",
    )(normed, branch_grad, weights, weights)


def standardize(values):
    middle = jnp.mean(values, axis=-1, keepdims=True)
    centred = values - middle
    spread = jnp.mean(centred * centred, axis=-1, keepdims=True)
    rate = lax.rsqrt(spread + 1e-06)
    return centred * rate, rate


def standardize_back(grad, unit, rate, scale_term):
    pulled = grad * (1.0 + scale_term)
    resid = rate * (
        pulled
        - jnp.mean(pulled, axis=-1, keepdims=True)
        - unit * jnp.mean(pulled * unit, axis=-1, keepdims=True)
    )
    return resid, jnp.sum(grad, axis=0), jnp.sum(grad * unit, axis=0)


def adam_step(weight, first, second, grad_sum, rate):
    first_new = 0.9 * first + 0.1 * grad_sum
    second_new = 0.999 * second + 0.001 * grad_sum * grad_sum
    first_hat = first_new / (1.0 - 0.9**STEP)
    second_hat = second_new / (1.0 - 0.999**STEP)
    weight_new = weight - rate * (first_hat / (jnp.sqrt(second_hat) + 1e-08) + 0.01 * weight)
    return (weight_new, first_new, second_new)


def shift_tp(values, steps, count):
    steps = steps % count
    if steps == 0:
        return values
    return lax.ppermute(values, "tp", [(i, (i + steps) % count) for i in range(count)])


def digits(count):
    if count % 8 == 0:
        return 4, count // 8, 2
    return count // 2, 1, 2


def shift_fsdp(values, digit, steps, count):
    sizes = digits(count)
    scale = (sizes[1] * sizes[2], sizes[2], 1)[digit]
    size = sizes[digit]
    pairs = []
    for source in range(count):
        own = (source // scale) % size
        pairs.append((source, source + ((own + steps) % size - own) * scale))
    return lax.ppermute(values, "fsdp", pairs)


def arrange(pieces, count, group):
    deep, across, cores = digits(count)
    width = pieces[0].shape[1]
    tile = fit(width, 512)

    def body(*refs):
        out_ref = refs[-1]
        me = lax.axis_index("fsdp")
        my_z, my_x, my_c = me // (across * cores), (me // cores) % across, me % cores
        for core in range(cores):
            for x in range(across):
                source = refs[core * across + x]
                for z in range(deep):
                    place = (
                        ((my_z - z + deep) % deep) * across + (my_x - x + across) % across
                    ) * cores + (my_c - core + cores) % cores
                    out_ref[pl.ds(pl.multiple_of(place * group, group), group), :] = source[
                        z * group : (z + 1) * group, :
                    ]

    return pl.pallas_call(
        body,
        grid=(width // tile,),
        in_specs=[pl.BlockSpec((piece.shape[0], tile), lambda j: (0, j)) for piece in pieces],
        out_specs=pl.BlockSpec((count * group, tile), lambda j: (0, j)),
        out_shape=jax.ShapeDtypeStruct((count * group, width), LOW),
        compiler_params=params(),
        cost_estimate=cost(0, 4 * count * group * width),
        name="arrange",
    )(*pieces)


def gather_z(shard, count):
    deep = digits(count)[0]
    return [shard] + [shift_fsdp(shard, 0, k, count) for k in range(1, deep)]


def gather_x(line, count):
    across = digits(count)[1]
    line = jnp.concatenate(line, axis=0)
    return [line] + [shift_fsdp(line, 1, k, count) for k in range(1, across)]


def gather_core(plane, count):
    cores = digits(count)[2]
    return plane + [shift_fsdp(piece, 2, k, count) for k in range(1, cores) for piece in plane]


def scatter_core(pair, count):
    kept, sent = pair
    return kept, shift_fsdp(sent, 2, 1, count)


def scatter_x(pair, count):
    kept, came = pair
    across = digits(count)[1]
    rows = kept.shape[0] // across

    def both(x):
        part = slice(x * rows, (x + 1) * rows)
        return kept[part].astype(FULL) + came[part].astype(FULL)

    return kept[:rows], came[:rows], [
        shift_fsdp(both(k).astype(LOW), 1, k, count) for k in range(1, across)
    ]


def scatter_z(state, count):
    kept, came, parts = state
    deep = digits(count)[0]
    group = kept.shape[0] // deep

    def both(z):
        rows = slice(z * group, (z + 1) * group)
        return sum(
            (part[rows].astype(FULL) for part in [came] + parts), start=kept[rows].astype(FULL)
        )

    return both(0), [shift_fsdp(both(k).astype(LOW), 0, k, count) for k in range(1, deep)]


def scatter_end(state):
    own, parts = state
    return sum((part.astype(FULL) for part in parts), start=own)


def gather_rows(shard):
    return lax.all_gather(shard, "fsdp", axis=0, tiled=True)


def scatter_rows(whole):
    return lax.psum_scatter(whole, "fsdp", scatter_dimension=0, tiled=True).astype(FULL)


def together(*values):
    return lax.optimization_barrier(values)


def modulation_shares(grads, tp_count, fsdp_count, part):
    count = grads.shape[0]
    by_owner = grads.reshape(count, tp_count, part)
    place = lax.axis_index("tp")
    total = sum(
        shift_tp(
            lax.dynamic_index_in_dim(by_owner, (place + k) % tp_count, axis=1, keepdims=False),
            k,
            tp_count,
        )
        for k in range(tp_count)
    )
    every = lax.all_to_all(
        jnp.broadcast_to(total.reshape(1, count * part), (fsdp_count, count * part)),
        "fsdp",
        split_axis=0,
        concat_axis=0,
        tiled=True,
    )
    return every


def local(
    fsdp_count,
    tp_count,
    latents_in,
    condition,
    out_grad,
    condition_weight,
    condition_first,
    condition_second,
    heads_weight,
    heads_first,
    heads_second,
    merge_weight,
    merge_first,
    merge_second,
    up_weight,
    up_first,
    up_second,
    down_weight,
    down_first,
    down_second,
):
    own, _, depth = latents_in.shape
    latents = latents_in.reshape(own, depth)
    cotangent = out_grad.reshape(own, depth)
    shard_rows = condition_weight.shape[0]
    part = condition_weight.shape[2]
    width = heads_weight.shape[2]
    units = up_weight.shape[1]
    ring = range(tp_count)
    others = range(1, tp_count)

    def blocks_of_tokens(values):
        return [shift_tp(values, -k, tp_count) for k in ring]

    pairs = width // PAIR
    spans = [(0, pairs // 2), (pairs // 2, pairs)] if pairs > 1 else [(0, pairs)]
    spans = [(start * PAIR, end * PAIR) for start, end in spans]

    activated = jax.nn.silu(condition).astype(LOW)
    activated_rows = lax.all_to_all(
        activated.reshape(fsdp_count, shard_rows), "fsdp", split_axis=0, concat_axis=0, tiled=True
    )

    heads_low = jnp.moveaxis(heads_weight.astype(LOW), 0, 1)
    heads_whole = gather_rows(
        jnp.concatenate(
            [heads_low[:, :, start:end].reshape(shard_rows, -1) for start, end in spans], axis=1
        )
    )
    unit_one, rate_one = standardize(latents)
    unit_blocks = blocks_of_tokens(unit_one.astype(LOW))
    shares = jnp.dot(
        activated_rows,
        condition_weight.astype(LOW).reshape(shard_rows, 6 * part),
        preferred_element_type=FULL,
    )
    shares = lax.all_to_all(shares, "fsdp", split_axis=0, concat_axis=0, tiled=True)
    merge_shard = merge_weight.astype(LOW).T
    merge_shard = jnp.concatenate([shift_tp(merge_shard, k, tp_count) for k in ring], axis=1)
    merge_line = gather_z(merge_shard, fsdp_count)
    feed_shard = jnp.concatenate([up_weight.astype(LOW), down_weight.astype(LOW).T], axis=1)
    shares, unit_blocks = together(shares, unit_blocks)
    modulation_part = jnp.sum(shares, axis=0).reshape(6, part)
    modulation = lax.all_gather(modulation_part, "tp", axis=1, tiled=True)
    shift_one, scale_one, gate_one, shift_two, scale_two, gate_two = (
        modulation[k : k + 1] for k in range(6)
    )

    branch_grad = (gate_two * cotangent).astype(LOW)
    branch_grad_blocks = blocks_of_tokens(branch_grad)

    normed_one = jnp.concatenate(
        [
            ((unit_one if k == 0 else unit_blocks[k].astype(FULL)) * (1.0 + scale_one) + shift_one).astype(LOW)
            for k in ring
        ],
        axis=0,
    )
    heads_whole, feed_shard, normed_one, merge_line = together(
        heads_whole, feed_shard, normed_one, merge_line
    )
    feed_whole = gather_rows(feed_shard)
    triples = [
        product(normed_one, heads_whole, LOW, 3 * start, 3 * (end - start)) for start, end in spans
    ]
    triples[0], merge_line = together(triples[0], merge_line)
    merge_plane = gather_x(merge_line, fsdp_count)
    attended = []
    mixes = []
    for index, (start, end) in enumerate(spans):
        mixed, level = attend_forward(triples[index], end - start)
        if index == 0:
            mixed, merge_plane, branch_grad_blocks = together(mixed, merge_plane, branch_grad_blocks)
            merge_whole = arrange(gather_core(merge_plane, fsdp_count), fsdp_count, shard_rows)
        mixes.append((mixed, level))
        attended.append([shift_tp(mixed[k * own : (k + 1) * own], k, tp_count) for k in ring])
    attended_own = jnp.concatenate([part[k] for k in ring for part in attended], axis=1)
    attn_branch = product_back([attended_own], merge_whole, FULL)
    after_attn = latents + gate_one * attn_branch
    unit_two, rate_two = standardize(after_attn)
    normed_two = (unit_two * (1.0 + scale_two) + shift_two).astype(LOW)
    normed_two_blocks = blocks_of_tokens(normed_two)

    fed = [feed_both(normed_two_blocks[0], branch_grad_blocks[0], feed_whole, FULL)]
    if tp_count > 1:
        fed, normed_two_blocks = together(fed, normed_two_blocks)
    fed += [feed_both(normed_two_blocks[k], branch_grad_blocks[k], feed_whole, LOW) for k in others]
    back_parts = [shift_tp(fed[k][1], k, tp_count) for k in others]
    (feed_grad,) = token_sum(
        [
            (normed_two_blocks, [fed[k][3] for k in ring]),
            (branch_grad_blocks, [fed[k][2] for k in ring]),
        ],
        fsdp_count,
        ordered=False,
    )
    branch_parts = [fed[k][0] for k in others]
    back_parts, branch_parts, feed_grad = together(back_parts, branch_parts, feed_grad)
    feed_sum = scatter_rows(feed_grad)
    branch_parts = [shift_tp(values, k, tp_count) for k, values in zip(others, branch_parts)]
    normed_two_grad = fed[0][1]
    for part_grad in back_parts:
        normed_two_grad = normed_two_grad + part_grad.astype(FULL)
    resid_two, shift_two_grad, scale_two_grad = standardize_back(
        normed_two_grad, unit_two, rate_two, scale_two
    )
    after_grad = cotangent + resid_two
    attn_grad = (gate_one * after_grad).astype(LOW)
    gate_one_grad = jnp.sum(after_grad * attn_branch, axis=0)
    attended_grad_own = product(attn_grad, merge_whole, LOW)
    attended_grads = [
        jnp.concatenate(
            [
                shift_tp(attended_grad_own[:, k * width + start : k * width + end], -k, tp_count)
                for k in ring
            ],
            axis=0,
        )
        for start, end in spans
    ]

    triple_grads = [
        attend_backward(triples[0], *mixes[0], attended_grads[0], spans[0][1] - spans[0][0])
    ]
    triple_grads, branch_parts = together(triple_grads, branch_parts)
    mlp_branch = fed[0][0]
    for part_branch in branch_parts:
        mlp_branch = mlp_branch + part_branch.astype(FULL)
    block_out = after_attn + gate_two * mlp_branch
    gate_two_grad = jnp.sum(cotangent * mlp_branch, axis=0)
    early_grads = jnp.stack([gate_one_grad, shift_two_grad, scale_two_grad, gate_two_grad], axis=0)

    pair = token_sum([([attn_grad], [attended_own]), ([normed_one], triple_grads)], fsdp_count)
    state = scatter_core(pair, fsdp_count)
    if len(spans) > 1:
        attended_grads, state, early_grads, block_out = together(
            attended_grads, state, early_grads, block_out
        )
    state = scatter_x(state, fsdp_count)
    for index in range(1, len(spans)):
        start, end = spans[index]
        triple_grads.append(
            attend_backward(triples[index], *mixes[index], attended_grads[index], end - start)
        )
    triple_grads, state = together(triple_grads, state)
    parts = [
        product_back([grad[k * own : (k + 1) * own] for grad in triple_grads], heads_whole, LOW)
        for k in others
    ]
    one_parts = [shift_tp(values, k, tp_count) for k, values in zip(others, parts)]
    triple_grads, parts = together(triple_grads, parts)
    last = None
    if len(spans) > 1:
        pair = token_sum([([normed_one], triple_grads[1:])], fsdp_count)
        triple_grads, pair = together(triple_grads, pair)
        last = scatter_core(pair, fsdp_count)
    normed_one_grad = product_back([grad[:own] for grad in triple_grads], heads_whole, FULL)
    up_new = adam_step(up_weight, up_first, up_second, feed_sum[:, :units], 0.02)
    down_new = adam_step(down_weight, down_first, down_second, feed_sum[:, units:].T, 0.01)
    one_parts, normed_one_grad, state, last, up_new, down_new = together(
        one_parts, normed_one_grad, state, last, up_new, down_new
    )
    if last:
        last = scatter_x(last, fsdp_count)
    for part_grad in one_parts:
        normed_one_grad = normed_one_grad + part_grad.astype(FULL)
    resid_one, shift_one_grad, scale_one_grad = standardize_back(
        normed_one_grad, unit_one, rate_one, scale_one
    )
    shift_one_grad, scale_one_grad, last = together(shift_one_grad, scale_one_grad, last)
    first_sum = scatter_end(scatter_z(state, fsdp_count))
    merge_sum_all, heads_sums = first_sum[:, : tp_count * width], [first_sum[:, tp_count * width :]]
    if last:
        heads_sums.append(scatter_end(scatter_z(last, fsdp_count)))
    heads_sums = [total.reshape(shard_rows, 3, -1) for total in heads_sums]
    latents_grad = after_grad + resid_one
    modulation_all = modulation_shares(
        jnp.concatenate([jnp.stack([shift_one_grad, scale_one_grad], axis=0), early_grads], axis=0),
        tp_count,
        fsdp_count,
        part,
    )
    condition_sum = lax.dot_general(
        activated_rows.astype(FULL),
        modulation_all,
        TN,
        precision=lax.Precision.HIGHEST,
        preferred_element_type=FULL,
    ).reshape(shard_rows, 6, part)
    merge_sum = merge_sum_all[:, :width]
    for k in others:
        merge_sum = merge_sum + shift_tp(
            merge_sum_all[:, k * width : (k + 1) * width], -k, tp_count
        )
    heads_sum = jnp.moveaxis(jnp.concatenate(heads_sums, axis=2), 1, 0)
    cond_new = adam_step(condition_weight, condition_first, condition_second, condition_sum, 0.02)
    heads_new = adam_step(heads_weight, heads_first, heads_second, heads_sum, 0.02)
    merge_new = adam_step(merge_weight, merge_first, merge_second, merge_sum.T, 0.15)
    return (
        block_out.reshape(own, 1, depth),
        latents_grad.reshape(own, 1, depth),
        *cond_new,
        *heads_new,
        *merge_new,
        *up_new,
        *down_new,
    )


def solution(mesh):
    stream = P("tp", "fsdp", None)
    cond = P("fsdp", None, "tp")
    heads = P(None, "fsdp", "tp")
    wide = P("tp", "fsdp")
    tall = P("fsdp", "tp")
    in_specs = (stream, P("fsdp", None), stream) + (cond,) * 3 + (heads,) * 3 + (wide,) * 3 + (tall,) * 3 + (wide,) * 3
    out_specs = (stream, stream) + (cond,) * 3 + (heads,) * 3 + (wide,) * 3 + (tall,) * 3 + (wide,) * 3
    return jax.shard_map(
        functools.partial(local, mesh.shape["fsdp"], mesh.shape["tp"]),
        mesh=mesh,
        in_specs=in_specs,
        out_specs=out_specs,
        check_vma=False,
    )
```

time: 1130 us -> 409 us (0.36)
  waiting for transfers between devices: 802 us -> 88.7 us
  matrix products: 166 us -> 4 us
  Pallas kernels: 0 us -> 153 us
  starting transfers between devices: 2.16 us -> 51.4 us
  other arithmetic: 83.5 us -> 56.4 us
  local copies, waits for them, and re-layouts: 51.8 us -> 29.6 us
    reduce_scatter x9 -> x1, waiting for transfers between devices: 366 us -> 0.01 us  [scatter_rows(): lax.psum_scatter(whole, 'fsdp', scatter_dimension=0, tiled=True)]
    all_gather x9 -> x2, waiting for transfers between devices: 324 us -> 19.8 us  [gather_rows(): return lax.all_gather(shard, 'fsdp', axis=0, tiled=True)]
    dot_general x27 -> x2, matrix products: 166 us -> 4 us  [the longest x1 3.83 us: local(): lax.dot_general(activated_rows.astype(FULL), modulation_all, TN, precisio...]
    pallas_call x0 -> x16, Pallas kernels: none -> 153 us  [the longest x2 35.2 us: attend_backward(): pl.pallas_call(body, grid=(pairs, steps), in_specs=[rows_of_pair, pl.Bloc...]
    unnamed x20 -> x3, waiting for transfers between devices: 111 us -> 0.05 us
    ppermute x0 -> x29, waiting for transfers between devices: none -> 59.9 us  [the longest x13 39.7 us: shift_tp(): lax.ppermute(values, 'tp', [(i, (i + steps) % count) for i in range(count)])]
    ppermute x0 -> x29, starting transfers between devices: none -> 37.8 us  [the longest x16 20.8 us: shift_fsdp(): return lax.ppermute(values, 'fsdp', pairs)]
    convert_element_type x14 -> x12, other arithmetic: 40.5 us -> 14.4 us  [the longest x2 3.42 us: scatter_x(): both(k).astype(LOW)]
  transfers between devices with their start and end apart: 19 -> 35, of which waited for: 18 -> 16; matrix products, arithmetic and copies ran while one was open for 12% -> 19% of each run, Pallas kernels for 0% -> 34%
where the time goes in v1:
time: 409 us; the launch traced here: 403 us
  Pallas kernels  153 us (37%)
  waiting for transfers between devices  88.7 us (22%)
  other arithmetic  56.4 us (14%)
  starting transfers between devices  51.4 us (13%)
  local copies, waits for them, and re-layouts  29.6 us (7%)
  between operations  15 us (4%)
  blocking collectives  4.42 us (1%)
    ppermute x13, waiting for transfers between devices, shift_tp(): lax.ppermute(values, 'tp', [(i, (i + steps) % count) for i in range(count)])  39.7 us
    pallas_call x2, Pallas kernels, attend_backward(): pl.pallas_call(body, grid=(pairs, steps), in_specs=[rows_of_pair, pl.Bloc...  35.2 us
    pallas_call x3, Pallas kernels, token_sum(): pl.pallas_call(body, grid=(width // tile,), in_specs=in_specs, out_specs=...  32.2 us
    pallas_call x2, Pallas kernels, feed_both(): pl.pallas_call(body, grid=(steps,), in_specs=[resident((tokens, depth)),...  31.9 us
    ppermute x16, starting transfers between devices, shift_fsdp(): return lax.ppermute(values, 'fsdp', pairs)  20.8 us
    ppermute x16, waiting for transfers between devices, shift_fsdp(): return lax.ppermute(values, 'fsdp', pairs)  20.2 us
    pallas_call x2, Pallas kernels, attend_forward(): pl.pallas_call(body, grid=(pairs, tokens // block), in_specs=[pl.BlockSpe...  20 us
    all_gather x2, waiting for transfers between devices, gather_rows(): return lax.all_gather(shard, 'fsdp', axis=0, tiled=True)  19.8 us
  transfers between devices with their start and end apart: 35, of which 16 were waited for; matrix products, arithmetic and copies ran while one was open for 19% of the time, Pallas kernels for 34%

profile of v1, /device:TPU:0, one launch (start us, length us, event | category | flops | bytes accessed | tf_op | source)
XLA Modules:
  0.0 402.6 jit_solution(6513146357978899793)
XLA Ops:
  18.1 5.9 %all-to-all-start = ((bf16[16,1,64]{2,1,0:T(2,128)(2,1)}), bf16[16,1,64]{2,1,0:T(2,128)(2,1)S(1)}, u32[]{:S(2)}, u32[]{:S(2)}) async-start(bf16[16,1,64]{2,1,0:T(2,128)(2,1)} %all_to_all.30), calls=%async_computation | async-start | bytes 16384 | tf_op jit(solution)/shard_map/all_to_all | solution.py:611
  36.8 5.4 %collective-permute-done.1 = bf16[64,512]{1,0:T(8,128)(2,1)} collective-permute-done((bf16[64,512]{1,0:T(8,128)(2,1)}, bf16[64,512]{1,0:T(8,128)(2,1)}, u32[]{:S(2)}, u32[]{:S(2)}) %collective-permute-start.1) | collective-permute-done | bytes 65568 | tf_op jit(solution)/shard_map/ppermute | solution.py:431
  57.6 5.3 %collective-permute-done.3 = bf16[64,1024]{1,0:T(8,128)(2,1)S(1)} collective-permute-done((bf16[64,1024]{1,0:T(8,128)(2,1)S(1)}, bf16[64,1024]{1,0:T(8,128)(2,1)S(1)}, u32[]{:S(2)}, u32[]{:S(2)}) %collective-permute-start.3) | collective-permute-done | bytes 131104 | tf_op jit(solution)/shard_map/ppermute | solution.py:448
  70.9 5.3 %product.3.query_ref.keys_ref.values_ref = bf16[1024,768]{1,0:T(8,128)(2,1)} custom-call(bf16[1024,1024]{1,0:T(8,128)(2,1)} %pad_maximum_fusion.left_ref.refs_2_.refs_0_, bf16[1024,1536]{1,0:T(8,128)(2,1)} %all-gather.3.cloned.1.call-done.right_ref.refs_2_), custom_call_target="tpu_custom_call" | custom-call | flops 1610612736 | bytes 6815744 | tf_op jit(solution)/shard_map/product/pallas_call | solution.py:46
  77.9 5.3 %product.4.query_ref.keys_ref.values_ref = bf16[1024,768]{1,0:T(8,128)(2,1)} custom-call(bf16[1024,1024]{1,0:T(8,128)(2,1)} %pad_maximum_fusion.left_ref.refs_2_.refs_0_, bf16[1024,1536]{1,0:T(8,128)(2,1)} %all-gather.3.cloned.1.call-done.right_ref.refs_2_), custom_call_target="tpu_custom_call" | custom-call | flops 1610612736 | bytes 6815744 | tf_op jit(solution)/shard_map/product/pallas_call | solution.py:46
  83.2 10.0 %attend_forward.3 = (bf16[1024,256]{1,0:T(8,128)(2,1)}, f32[1024,256]{1,0:T(8,128)}) custom-call(bf16[1024,768]{1,0:T(8,128)(2,1)} %product.4.query_ref.keys_ref.values_ref, bf16[1024,768]{1,0:T(8,128)(2,1)} %product.4.query_ref.keys_ref.values_ref, bf16[1024,768]{1,0:T(8,128)(2,1)} %product.4.query_ref.keys_ref.values_ref), custom_call_target="tpu_custom_call" | custom-call | flops 4294967296 | bytes 3145728 | tf_op jit(solution)/shard_map/attend_forward/pallas_call | solution.py:220
  95.4 10.0 %attend_forward.2 = (bf16[1024,256]{1,0:T(8,128)(2,1)}, f32[1024,256]{1,0:T(8,128)}) custom-call(bf16[1024,768]{1,0:T(8,128)(2,1)} %product.3.query_ref.keys_ref.values_ref, bf16[1024,768]{1,0:T(8,128)(2,1)} %product.3.query_ref.keys_ref.values_ref, bf16[1024,768]{1,0:T(8,128)(2,1)} %product.3.query_ref.keys_ref.values_ref), custom_call_target="tpu_custom_call" | custom-call | flops 4294967296 | bytes 3145728 | tf_op jit(solution)/shard_map/attend_forward/pallas_call | solution.py:220
  109.1 7.2 %collective-permute-done.7 = bf16[512,256]{1,0:T(8,128)(2,1)S(1)} collective-permute-done((bf16[512,256]{1,0:T(8,128)(2,1)S(1)}, bf16[512,256]{1,0:T(8,128)(2,1)S(1)}, u32[]{:S(2)}, u32[]{:S(2)}) %collective-permute-start.7) | collective-permute-done | bytes 262176 | tf_op jit(solution)/shard_map/ppermute | solution.py:431
  131.2 15.5 %all-gather.5.cloned.1.call-done.up_ref.down_ref = bf16[1024,4096]{1,0:T(8,128)(2,1)} async-done(((bf16[64,4096]{1,0:T(8,128)(2,1)}), bf16[1024,4096]{1,0:T(8,128)(2,1)}) %all-gather.5.cloned.1.call-update) | async-done | bytes 8388624 | tf_op jit(solution)/shard_map/all_gather | solution.py:538
  146.7 16.2 %feed_both.2 = (f32[512,1024]{1,0:T(8,128)}, f32[512,1024]{1,0:T(8,128)}, bf16[512,2048]{1,0:T(8,128)(2,1)}, bf16[512,2048]{1,0:T(8,128)(2,1)}) custom-call(bf16[512,1024]{1,0:T(8,128)(2,1)} %copy-done.18, bf16[512,1024]{1,0:T(8,128)(2,1)} %copy-done.17, bf16[1024,4096]{1,0:T(8,128)(2,1)} %all-gather.5.cloned.1.call-done.up_ref.down_ref, ...), custom_call_target="tpu_custom_call" | custom-call | flops 8589934592 | bytes 18874368 | tf_op jit(solution)/shard_map/feed_both/pallas_call | solution.py:372
  162.9 15.7 %feed_both.3 = (bf16[512,1024]{1,0:T(8,128)(2,1)}, bf16[512,1024]{1,0:T(8,128)(2,1)}, bf16[512,2048]{1,0:T(8,128)(2,1)}, bf16[512,2048]{1,0:T(8,128)(2,1)}) custom-call(bf16[512,1024]{1,0:T(8,128)(2,1)} %collective-permute-done.11.normed_ref.refs_1_, bf16[512,1024]{1,0:T(8,128)(2,1)} %copy-done.49, ...), custom_call_target="tpu_custom_call" | custom-call | flops 8589934592 | bytes 18874368 | tf_op jit(solution)/shard_map/feed_both/pallas_call | solution.py:372
  180.1 16.4 %token_sum.3 = bf16[1024,4096]{1,0:T(8,128)(2,1)} custom-call(bf16[512,1024]{1,0:T(8,128)(2,1)} %copy-done.18, bf16[512,1024]{1,0:T(8,128)(2,1)} %collective-permute-done.11.normed_ref.refs_1_, bf16[512,2048]{1,0:T(8,128)(2,1)} %get-tuple-element.127.refs_2_, bf16[512,2048]{1,0:T(8,128)(2,1)} %get-tuple-element.128.refs_3_, bf16[512,1024]{1,0:T(8,128)(2,1)} %copy-done.17, ...), custom_call_target="tpu_custom_call" | custom-call | flops 8589934592 | bytes 20971520 | tf_op jit(solution)/shard_map/token_sum/pallas_call | solution.py:160
  196.5 7.7 %collective-permute-done.12 = bf16[512,1024]{1,0:T(8,128)(2,1)S(1)} collective-permute-done((bf16[512,1024]{1,0:T(8,128)(2,1)}, bf16[512,1024]{1,0:T(8,128)(2,1)S(1)}, u32[]{:S(2)}, u32[]{:S(2)}) %collective-permute-start.12) | collective-permute-done | bytes 1048608 | tf_op jit(solution)/shard_map/ppermute | solution.py:431
  222.7 7.2 %collective-permute-done.13 = bf16[512,256]{1,0:T(8,128)(2,1)S(1)} collective-permute-done((bf16[512,256]{1,0:T(8,128)(2,1)S(1)}, bf16[512,256]{1,0:T(8,128)(2,1)S(1)}, u32[]{:S(2)}, u32[]{:S(2)}) %collective-permute-start.13) | collective-permute-done | bytes 262176 | tf_op jit(solution)/shard_map/ppermute | solution.py:431
  230.7 17.6 %attend_backward.2.refs_3_ = bf16[1024,768]{1,0:T(8,128)(2,1)} custom-call(bf16[1024,768]{1,0:T(8,128)(2,1)} %product.3.query_ref.keys_ref.values_ref, bf16[1024,768]{1,0:T(8,128)(2,1)} %product.3.query_ref.keys_ref.values_ref, bf16[1024,768]{1,0:T(8,128)(2,1)} %product.3.query_ref.keys_ref.values_ref, bf16[1024,256]{1,0:T(8,128)(2,1)} %get-tuple-element.111.out_low_ref, ...), custom_call_target="tpu_custom_call" | custom-call | flops 10737418240 | bytes 5242880 | tf_op jit(solution)/shard_map/attend_backward/pallas_call | solution.py:312
  250.7 9.9 %token_sum.4 = (bf16[512,1792]{1,0:T(8,128)(2,1)}, bf16[512,1792]{1,0:T(8,128)(2,1)}) custom-call(bf16[512,1024]{1,0:T(8,128)(2,1)} %multiply_convert_fusion.left_ref.refs_0_, bf16[512,1024]{1,0:T(8,128)(2,1)} %pad_maximum_fusion.1.refs_0_.refs_1_, bf16[1024,1024]{1,0:T(8,128)(2,1)} %pad_maximum_fusion.left_ref.refs_2_.refs_0_, ...), custom_call_target="tpu_custom_call" | custom-call | flops 3758096384 | bytes 11534336 | tf_op jit(solution)/shard_map/token_sum/pallas_call | solution.py:160
  262.3 7.3 %collective-permute-done.14 = bf16[512,256]{1,0:T(8,128)(2,1)} collective-permute-done((bf16[512,256]{1,0:T(8,128)(2,1)}, bf16[512,256]{1,0:T(8,128)(2,1)}, u32[]{:S(2)}, u32[]{:S(2)}) %collective-permute-start.14) | collective-permute-done | bytes 262176 | tf_op jit(solution)/shard_map/ppermute | solution.py:431
  271.4 5.5 %multiply_add_fusion = (f32[512,1024]{1,0:T(8,128)}, f32[1024]{0:T(1024)S(1)}) fusion(f32[512,1024]{1,0:T(8,128)} %copy-done.1, f32[512,1024]{1,0:T(8,128)} %get-tuple-element.137, bf16[512,1024]{1,0:T(8,128)(2,1)S(1)} %collective-permute-done.15, f32[1024]{0:T(1024)S(1)} %bitcast.132, f32[512,1,1024]{2,1,0:T(1,128)} %param.20), kind=kLoop, calls=%fused_computation.13 | loop fusion | flops 3144704 | bytes 9445376 | tf_op jit(solution)/shard_map/add | solution.py:720
  288.9 17.6 %attend_backward.3.refs_1_ = bf16[1024,768]{1,0:T(8,128)(2,1)} custom-call(bf16[1024,768]{1,0:T(8,128)(2,1)} %product.4.query_ref.keys_ref.values_ref, bf16[1024,768]{1,0:T(8,128)(2,1)} %product.4.query_ref.keys_ref.values_ref, bf16[1024,768]{1,0:T(8,128)(2,1)} %product.4.query_ref.keys_ref.values_ref, bf16[1024,256]{1,0:T(8,128)(2,1)} %get-tuple-element.112.out_low_ref, ...), custom_call_target="tpu_custom_call" | custom-call | flops 10737418240 | bytes 5242880 | tf_op jit(solution)/shard_map/attend_backward/pallas_call | solution.py:312
  312.2 5.5 %product_back.4 = bf16[512,1024]{1,0:T(8,128)(2,1)} custom-call(bf16[512,768]{1,0:T(8,128)(2,1)} %slice.194.refs_0_, bf16[512,768]{1,0:T(8,128)(2,1)} %slice.195.refs_1_, bf16[1024,1536]{1,0:T(8,128)(2,1)} %all-gather.3.cloned.1.call-done.right_ref.refs_2_), custom_call_target="tpu_custom_call" | custom-call | flops 1610612736 | bytes 6815744 | tf_op jit(solution)/shard_map/product_back/pallas_call | solution.py:78
  319.4 6.0 %token_sum.5 = (bf16[512,768]{1,0:T(8,128)(2,1)}, bf16[512,768]{1,0:T(8,128)(2,1)}) custom-call(bf16[1024,1024]{1,0:T(8,128)(2,1)} %pad_maximum_fusion.left_ref.refs_2_.refs_0_, bf16[1024,768]{1,0:T(8,128)(2,1)} %attend_backward.3.refs_1_), custom_call_target="tpu_custom_call" | custom-call | flops 1610612736 | bytes 5242880 | tf_op jit(solution)/shard_map/token_sum/pallas_call | solution.py:160
  328.0 5.9 %product_back.5 = f32[512,1024]{1,0:T(8,128)} custom-call(bf16[512,768]{1,0:T(8,128)(2,1)} %slice.196.refs_0_, bf16[512,768]{1,0:T(8,128)(2,1)} %slice.197.refs_1_, bf16[1024,1536]{1,0:T(8,128)(2,1)} %all-gather.3.cloned.1.call-done.right_ref.refs_2_), custom_call_target="tpu_custom_call" | custom-call | flops 1610612736 | bytes 6815744 | tf_op jit(solution)/shard_map/product_back/pallas_call | solution.py:78
  352.7 7.7 %collective-permute-done.23 = bf16[64,1792]{1,0:T(8,128)(2,1)S(1)} collective-permute-done((bf16[64,1792]{1,0:T(8,128)(2,1)S(1)}, bf16[64,1792]{1,0:T(8,128)(2,1)S(1)}, u32[]{:S(2)}, u32[]{:S(2)}) %collective-permute-start.23) | collective-permute-done | bytes 229408 | tf_op jit(solution)/shard_map/ppermute | solution.py:448
  386.1 5.7 %all-to-all-done.2 = f32[16,1,3072]{2,1,0:T(1,128)S(1)} async-done(((f32[16,1,3072]{2,1,0:T(1,128)}), f32[16,1,3072]{2,1,0:T(1,128)S(1)}, u32[]{:S(2)}, u32[]{:S(2)}) %all-to-all-start.2) | async-done | bytes 196640 | tf_op jit(solution)/shard_map/all_to_all | solution.py:561
  (259 shorter events, 165.8 us)
Async XLA Ops:
  7.2 60.0 %all-gather.3.cloned.1.call-start = ((), (), s32[]{:S(2)}) async-start(), calls=%async_computation.4 | async-start | bytes 3342336 | tf_op jit(solution)/shard_map/all_gather | solution.py:538
  14.4 34.6 %collective-permute-start = (bf16[512,1024]{1,0:T(8,128)(2,1)}, bf16[512,1024]{1,0:T(8,128)(2,1)}, u32[]{:S(2)}, u32[]{:S(2)}) collective-permute-start(bf16[512,1024]{1,0:T(8,128)(2,1)} %fusion.18), channel_id=1, source_target_pairs={{0,1},{1,0},{2,3},{3,2},{4,5},{5,4},{6,7},{7,6},{8,9},{9,8},{10,11... | collective-permute-start | bytes 3145736 | tf_op jit(solution)/shard_map/ppermute | solution.py:431
  18.1 12.3 %all-to-all-start = ((bf16[16,1,64]{2,1,0:T(2,128)(2,1)}), bf16[16,1,64]{2,1,0:T(2,128)(2,1)S(1)}, u32[]{:S(2)}, u32[]{:S(2)}) async-start(bf16[16,1,64]{2,1,0:T(2,128)(2,1)} %all_to_all.30), calls=%async_computation | async-start | bytes 16384 | tf_op jit(solution)/shard_map/all_to_all | solution.py:611
  24.6 17.6 %collective-permute-start.1 = (bf16[64,512]{1,0:T(8,128)(2,1)}, bf16[64,512]{1,0:T(8,128)(2,1)}, u32[]{:S(2)}, u32[]{:S(2)}) collective-permute-start(bf16[64,512]{1,0:T(8,128)(2,1)} %convert_bitcast_fusion.3), channel_id=1, source_target_pairs={{0,1},{1,0},{2,3},{3,2},{4,5},{5,4},{6,7},{7,6},{8,9},{9,8},{10,11... | collective-permute-start | bytes 196616 | tf_op jit(solution)/shard_map/ppermute | solution.py:431
  31.5 17.4 %all-to-all-start.1 = ((f32[16,1,3072]{2,1,0:T(1,128)}), f32[16,1,3072]{2,1,0:T(1,128)S(1)}, u32[]{:S(2)}, u32[]{:S(2)}) async-start(f32[16,1,3072]{2,1,0:T(1,128)} %copy.85), calls=%async_computation.1 | async-start | bytes 393216 | tf_op jit(solution)/shard_map/all_to_all | solution.py:628
  35.0 111.7 %all-gather.5.cloned.1.call-start = ((), (), s32[]{:S(2)}) async-start(), calls=%async_computation.5 | async-start | bytes 8912896 | tf_op jit(solution)/shard_map/all_gather | solution.py:538
  43.1 14.5 %collective-permute-start.2 = (bf16[64,1024]{1,0:T(8,128)(2,1)S(1)}, bf16[64,1024]{1,0:T(8,128)(2,1)S(1)}, u32[]{:S(2)}, u32[]{:S(2)}) collective-permute-start(bf16[64,1024]{1,0:T(8,128)(2,1)S(1)} %pad_maximum_fusion.6), channel_id=1, source_target_pairs={{0,8},{2,10},{4,12},{6,14},{8,16},{10,18},{12,20},{14,22},{16,24},... | collective-permute-start | bytes 393224 | tf_op jit(solution)/shard_map/ppermute | solution.py:448
  45.0 17.9 %collective-permute-start.3 = (bf16[64,1024]{1,0:T(8,128)(2,1)S(1)}, bf16[64,1024]{1,0:T(8,128)(2,1)S(1)}, u32[]{:S(2)}, u32[]{:S(2)}) collective-permute-start(bf16[64,1024]{1,0:T(8,128)(2,1)S(1)} %pad_maximum_fusion.6), channel_id=1, source_target_pairs={{0,16},{2,18},{4,20},{6,22},{8,24},{10,26},{12,28},{14,30},{16,0},... | collective-permute-start | bytes 393224 | tf_op jit(solution)/shard_map/ppermute | solution.py:448
  47.5 15.4 %collective-permute-start.4 = (bf16[64,1024]{1,0:T(8,128)(2,1)S(1)}, bf16[64,1024]{1,0:T(8,128)(2,1)S(1)}, u32[]{:S(2)}, u32[]{:S(2)}) collective-permute-start(bf16[64,1024]{1,0:T(8,128)(2,1)S(1)} %pad_maximum_fusion.6), channel_id=1, source_target_pairs={{0,24},{2,26},{4,28},{6,30},{8,0},{10,2},{12,4},{14,6},{16,8},{18,... | collective-permute-start | bytes 393224 | tf_op jit(solution)/shard_map/ppermute | solution.py:448
  67.2 266.7 %reduce-scatter.2.cloned.1.call-start = ((), (), s32[]{:S(2)}) async-start(), calls=%async_computation.6 | async-start | bytes 8912896 | tf_op jit(solution)/shard_map/reduce_scatter | solution.py:542
  69.7 35.6 %collective-permute-start.6 = (bf16[512,1024]{1,0:T(8,128)(2,1)S(1)}, bf16[512,1024]{1,0:T(8,128)(2,1)S(1)}, u32[]{:S(2)}, u32[]{:S(2)}) collective-permute-start(bf16[512,1024]{1,0:T(8,128)(2,1)S(1)} %fusion.grad_ref.refs_4_), channel_id=1, source_target_pairs={{0,1},{1,0},{2,3},{3,2},{4,5},{5,4},{6,7},{7,6},{8,9},{9,8},{10,11... | collective-permute-start | bytes 3145736 | tf_op jit(solution)/shard_map/ppermute | solution.py:431
  76.4 29.0 %collective-permute-start.5 = (bf16[256,1024]{1,0:T(8,128)(2,1)S(1)}, bf16[256,1024]{1,0:T(8,128)(2,1)S(1)}, u32[]{:S(2)}, u32[]{:S(2)}) collective-permute-start(bf16[256,1024]{1,0:T(8,128)(2,1)S(1)} %constant_dynamic-update-slice_fusion.refs_0_), channel_id=1, source_target_pairs={{0,4},{2,6},{4,0},{6,2},{8,12},{10,14},{12,8},{14,10},{16,20},{18,... | collective-permute-start | bytes 1572872 | tf_op jit(solution)/shard_map/ppermute | solution.py:448
  94.3 14.8 %collective-permute-start.8 = (bf16[512,256]{1,0:T(8,128)(2,1)S(1)}, bf16[512,256]{1,0:T(8,128)(2,1)S(1)}, u32[]{:S(2)}, u32[]{:S(2)}) collective-permute-start(bf16[512,256]{1,0:T(8,128)(2,1)S(1)} %get-tuple-element.304), channel_id=1, source_target_pairs={{0,1},{1,0},{2,3},{3,2},{4,5},{5,4},{6,7},{7,6},{8,9},{9,8},{10,11... | collective-permute-start | bytes 786440 | tf_op jit(solution)/shard_map/ppermute | solution.py:431
  130.2 32.7 %collective-permute-start.11 = (bf16[512,1024]{1,0:T(8,128)(2,1)S(1)}, bf16[512,1024]{1,0:T(8,128)(2,1)}, u32[]{:S(2)}, u32[]{:S(2)}) collective-permute-start(bf16[512,1024]{1,0:T(8,128)(2,1)S(1)} %add_convert_fusion.normed_ref.refs_0_), channel_id=1, source_target_pairs={{0,1},{1,0},{2,3},{3,2},{4,5},{5,4},{6,7},{7,6},{8,9},{9,8},{10,11... | collective-permute-start | bytes 3145736 | tf_op jit(solution)/shard_map/ppermute | solution.py:431
  178.6 25.6 %collective-permute-start.12 = (bf16[512,1024]{1,0:T(8,128)(2,1)}, bf16[512,1024]{1,0:T(8,128)(2,1)S(1)}, u32[]{:S(2)}, u32[]{:S(2)}) collective-permute-start(bf16[512,1024]{1,0:T(8,128)(2,1)} %get-tuple-element.124), channel_id=1, source_target_pairs={{0,1},{1,0},{2,3},{3,2},{4,5},{5,4},{6,7},{7,6},{8,9},{9,8},{10,11... | collective-permute-start | bytes 3145736 | tf_op jit(solution)/shard_map/ppermute | solution.py:431
  222.0 28.6 %collective-permute-start.15 = (bf16[512,1024]{1,0:T(8,128)(2,1)S(1)}, bf16[512,1024]{1,0:T(8,128)(2,1)S(1)}, u32[]{:S(2)}, u32[]{:S(2)}) collective-permute-start(bf16[512,1024]{1,0:T(8,128)(2,1)S(1)} %copy-done.50), channel_id=1, source_target_pairs={{0,1},{1,0},{2,3},{3,2},{4,5},{5,4},{6,7},{7,6},{8,9},{9,8},{10,11... | collective-permute-start | bytes 3145736 | tf_op jit(solution)/shard_map/ppermute | solution.py:431
  260.6 16.4 %collective-permute-start.16 = (bf16[512,1792]{1,0:T(8,128)(2,1)}, bf16[512,1792]{1,0:T(8,128)(2,1)}, u32[]{:S(2)}, u32[]{:S(2)}) collective-permute-start(bf16[512,1792]{1,0:T(8,128)(2,1)} %get-tuple-element.136), channel_id=1, source_target_pairs={{0,2},{2,0},{4,6},{6,4},{8,10},{10,8},{12,14},{14,12},{16,18},{18,... | collective-permute-start | bytes 5505032 | tf_op jit(solution)/shard_map/ppermute | solution.py:448
  282.5 27.7 %collective-permute-start.17 = (bf16[256,1792]{1,0:T(8,128)(2,1)}, bf16[256,1792]{1,0:T(8,128)(2,1)S(1)}, u32[]{:S(2)}, u32[]{:S(2)}) collective-permute-start(bf16[256,1792]{1,0:T(8,128)(2,1)} %add_convert_fusion.3), channel_id=1, source_target_pairs={{0,4},{2,6},{4,0},{6,2},{8,12},{10,14},{12,8},{14,10},{16,20},{18,... | collective-permute-start | bytes 2752520 | tf_op jit(solution)/shard_map/ppermute | solution.py:448
  317.8 24.2 %collective-permute-start.18 = (bf16[512,1024]{1,0:T(8,128)(2,1)}, bf16[512,1024]{1,0:T(8,128)(2,1)S(1)}, u32[]{:S(2)}, u32[]{:S(2)}) collective-permute-start(bf16[512,1024]{1,0:T(8,128)(2,1)} %product_back.4), channel_id=1, source_target_pairs={{0,1},{1,0},{2,3},{3,2},{4,5},{5,4},{6,7},{7,6},{8,9},{9,8},{10,11... | collective-permute-start | bytes 3145736 | tf_op jit(solution)/shard_map/ppermute | solution.py:431
  343.2 17.2 %collective-permute-start.23 = (bf16[64,1792]{1,0:T(8,128)(2,1)S(1)}, bf16[64,1792]{1,0:T(8,128)(2,1)S(1)}, u32[]{:S(2)}, u32[]{:S(2)}) collective-permute-start(bf16[64,1792]{1,0:T(8,128)(2,1)S(1)} %get-tuple-element.293), channel_id=1, source_target_pairs={{0,16},{2,18},{4,20},{6,22},{8,24},{10,26},{12,28},{14,30},{16,0},... | collective-permute-start | bytes 688136 | tf_op jit(solution)/shard_map/ppermute | solution.py:448
  344.3 16.2 %collective-permute-start.24 = (bf16[64,1792]{1,0:T(8,128)(2,1)S(1)}, bf16[64,1792]{1,0:T(8,128)(2,1)S(1)}, u32[]{:S(2)}, u32[]{:S(2)}) collective-permute-start(bf16[64,1792]{1,0:T(8,128)(2,1)S(1)} %get-tuple-element.292), channel_id=1, source_target_pairs={{0,24},{2,26},{4,28},{6,30},{8,0},{10,2},{12,4},{14,6},{16,8},{18,... | collective-permute-start | bytes 688136 | tf_op jit(solution)/shard_map/ppermute | solution.py:448
  348.0 20.1 %collective-permute-start.20 = (bf16[256,768]{1,0:T(8,128)(2,1)S(1)}, bf16[256,768]{1,0:T(8,128)(2,1)}, u32[]{:S(2)}, u32[]{:S(2)}) collective-permute-start(bf16[256,768]{1,0:T(8,128)(2,1)S(1)} %add_convert_fusion.4), channel_id=1, source_target_pairs={{0,4},{2,6},{4,0},{6,2},{8,12},{10,14},{12,8},{14,10},{16,20},{18,... | collective-permute-start | bytes 1179656 | tf_op jit(solution)/shard_map/ppermute | solution.py:448
  371.2 11.6 %collective-permute-start.25 = (bf16[64,768]{1,0:T(8,128)(2,1)}, bf16[64,768]{1,0:T(8,128)(2,1)S(1)}, u32[]{:S(2)}, u32[]{:S(2)}) collective-permute-start(bf16[64,768]{1,0:T(8,128)(2,1)} %get-tuple-element.294), channel_id=1, source_target_pairs={{0,8},{2,10},{4,12},{6,14},{8,16},{10,18},{12,20},{14,22},{16,24},... | collective-permute-start | bytes 294920 | tf_op jit(solution)/shard_map/ppermute | solution.py:448
  379.3 12.5 %all-to-all-start.2 = ((f32[16,1,3072]{2,1,0:T(1,128)}), f32[16,1,3072]{2,1,0:T(1,128)S(1)}, u32[]{:S(2)}, u32[]{:S(2)}) async-start(f32[16,1,3072]{2,1,0:T(1,128)} %broadcast_in_dim.5), calls=%async_computation.3 | async-start | bytes 393216 | tf_op jit(solution)/shard_map/all_to_all | solution.py:561
  (62 other events, 486.9 us)
Sparse Core Ops, SparseCore 0:
  10.9 56.2 all-gather.2
  69.9 76.7 all-gather.4
  204.3 107.6 reduce-scatter.1

commit v2 on v1

--- a/solution.py
+++ b/solution.py
@@ -58,8 +58,7 @@
     )(left, right)
 
 
-def product_back(lefts, right, out_type):
-    rows = lefts[0].shape[0]
+def product_back(lefts, right, out_type, rows, part):
     width, depth = right.shape
     tile = min(256, width)
 
@@ -78,7 +77,7 @@
     return pl.pallas_call(
         body,
         grid=(width // tile,),
-        in_specs=[resident(left.shape) for left in lefts]
+        in_specs=[pl.BlockSpec((rows, left.shape[1]), lambda j: (part, 0)) for left in lefts]
         + [pl.BlockSpec((tile, depth), lambda j: (j, 0))],
         out_specs=pl.BlockSpec((rows, tile), lambda j: (0, j)),
         out_shape=jax.ShapeDtypeStruct((rows, width), out_type),
@@ -405,14 +404,163 @@
     return centred * rate, rate
 
 
-def standardize_back(grad, unit, rate, scale_term):
+def standardize_back(grad, values, scale_term):
+    unit, rate = standardize(values)
     pulled = grad * (1.0 + scale_term)
     resid = rate * (
         pulled
         - jnp.mean(pulled, axis=-1, keepdims=True)
         - unit * jnp.mean(pulled * unit, axis=-1, keepdims=True)
     )
-    return resid, jnp.sum(grad, axis=0), jnp.sum(grad * unit, axis=0)
+    return resid, jnp.sum(grad, axis=0, keepdims=True), jnp.sum(grad * unit, axis=0, keepdims=True)
+
+
+def store_sums(sums_ref, rows):
+    @pl.when(pl.program_id(0) == 0)
+    def _():
+        sums_ref[...] = jnp.zeros_like(sums_ref)
+
+    for index, row in enumerate(rows):
+        sums_ref[index : index + 1, :] += row
+
+
+def store_lines(out_ref, values):
+    for index in range(out_ref.shape[1]):
+        out_ref[:, index, :] = values[:, index * PAIR : (index + 1) * PAIR]
+
+
+def by_tokens(body, arrays, wholes, outs, sums, flops, name):
+    tokens = arrays[0].shape[0]
+    block = min(256, tokens)
+
+    def cut(shape):
+        return pl.BlockSpec((block,) + shape[1:], lambda j: (j,) + (0,) * (len(shape) - 1))
+
+    out_specs = [cut(shape) for shape, _ in outs]
+    out_shape = [jax.ShapeDtypeStruct(shape, kind) for shape, kind in outs]
+    if sums:
+        out_specs.append(resident((8, sums)))
+        out_shape.append(jax.ShapeDtypeStruct((8, sums), FULL))
+    moved = sum(value.size * value.dtype.itemsize for value in list(arrays) + list(wholes) + out_shape)
+    return pl.pallas_call(
+        body,
+        grid=(tokens // block,),
+        in_specs=[cut(value.shape) for value in arrays] + [resident(value.shape) for value in wholes],
+        out_specs=out_specs,
+        out_shape=out_shape,
+        compiler_params=params(),
+        cost_estimate=cost(flops, moved),
+        name=name,
+    )(*arrays, *wholes)
+
+
+def merge_and_normalize(attended, latents, merge, gate, shift, scale):
+    tokens, depth = latents.shape
+
+    def body(attended_ref, latents_ref, merge_ref, gate_ref, shift_ref, scale_ref, branch_ref, after_ref, normed_ref):
+        branch = lax.dot_general(attended_ref[...], merge_ref[...], NT, preferred_element_type=FULL)
+        after = latents_ref[...] + gate_ref[...] * branch
+        branch_ref[...] = branch
+        after_ref[...] = after
+        normed_ref[...] = (
+            standardize(after)[0] * (1.0 + scale_ref[...]) + shift_ref[...]
+        ).astype(LOW)
+
+    shape = (tokens, depth)
+    return by_tokens(
+        body,
+        [attended, latents],
+        [merge, gate, shift, scale],
+        [(shape, FULL), (shape, FULL), (shape, LOW)],
+        0,
+        2 * tokens * depth * merge.shape[1],
+        "merge_and_normalize",
+    )
+
+
+def second_back(grad, parts, after, branch, cotangent, merge, gate, scale, spans):
+    tokens, depth = after.shape
+    count = len(parts)
+
+    def body(*refs):
+        total = refs[0][...]
+        for part_ref in refs[1 : 1 + count]:
+            total = total + part_ref[...].astype(FULL)
+        after_ref, branch_ref, cotangent_ref, merge_ref, gate_ref, scale_ref = refs[1 + count : 7 + count]
+        grad_ref, low_ref = refs[7 + count : 9 + count]
+        piece_refs, sums_ref = refs[9 + count : -1], refs[-1]
+        resid, shift_grad, scale_grad = standardize_back(total, after_ref[...], scale_ref[...])
+        after_grad = cotangent_ref[...] + resid
+        low = (gate_ref[...] * after_grad).astype(LOW)
+        grad_ref[...] = after_grad
+        low_ref[...] = low
+        back = jnp.dot(low, merge_ref[...], preferred_element_type=FULL).astype(LOW)
+        for piece_ref, (start, end) in zip(piece_refs, spans):
+            piece_ref[...] = back[:, start:end]
+        store_sums(
+            sums_ref,
+            [jnp.sum(after_grad * branch_ref[...], axis=0, keepdims=True), shift_grad, scale_grad],
+        )
+
+    outs = [((tokens, depth), FULL), ((tokens, depth), LOW)]
+    outs += [((tokens, end - start), LOW) for start, end in spans]
+    results = by_tokens(
+        body,
+        [grad, *parts, after, branch, cotangent],
+        [merge, gate, scale],
+        outs,
+        depth,
+        2 * tokens * depth * merge.shape[1],
+        "second_back",
+    )
+    return results[0], results[1], results[2:-1], results[-1]
+
+
+def first_back(grad, parts, latents, after_grad, scale):
+    tokens, depth = latents.shape
+    count = len(parts)
+
+    def body(*refs):
+        total = refs[0][...]
+        for part_ref in refs[1 : 1 + count]:
+            total = total + part_ref[...].astype(FULL)
+        latents_ref, after_ref, scale_ref, out_ref, sums_ref = refs[1 + count :]
+        resid, shift_grad, scale_grad = standardize_back(total, latents_ref[...], scale_ref[...])
+        store_lines(out_ref, after_ref[...] + resid)
+        store_sums(sums_ref, [shift_grad, scale_grad])
+
+    return by_tokens(
+        body,
+        [grad, *parts, latents, after_grad],
+        [scale],
+        [((tokens, depth // PAIR, PAIR), FULL)],
+        depth,
+        20 * tokens * depth,
+        "first_back",
+    )
+
+
+def last_forward(branch, parts, after, cotangent, gate):
+    tokens, depth = after.shape
+    count = len(parts)
+
+    def body(*refs):
+        total = refs[0][...]
+        for part_ref in refs[1 : 1 + count]:
+            total = total + part_ref[...].astype(FULL)
+        after_ref, cotangent_ref, gate_ref, out_ref, sums_ref = refs[1 + count :]
+        store_lines(out_ref, after_ref[...] + gate_ref[...] * total)
+        store_sums(sums_ref, [jnp.sum(cotangent_ref[...] * total, axis=0, keepdims=True)])
+
+    return by_tokens(
+        body,
+        [branch, *parts, after, cotangent],
+        [gate],
+        [((tokens, depth // PAIR, PAIR), FULL)],
+        depth,
+        6 * tokens * depth,
+        "last_forward",
+    )
 
 
 def adam_step(weight, first, second, grad_sum, rate):
@@ -539,7 +687,7 @@
 
 
 def scatter_rows(whole):
-    return lax.psum_scatter(whole, "fsdp", scatter_dimension=0, tiled=True).astype(FULL)
+    return lax.psum_scatter(whole, "fsdp", scatter_dimension=0, tiled=True)
 
 
 def together(*values):
@@ -548,13 +696,10 @@
 
 def modulation_shares(grads, tp_count, fsdp_count, part):
     count = grads.shape[0]
-    by_owner = grads.reshape(count, tp_count, part)
     place = lax.axis_index("tp")
     total = sum(
         shift_tp(
-            lax.dynamic_index_in_dim(by_owner, (place + k) % tp_count, axis=1, keepdims=False),
-            k,
-            tp_count,
+            lax.dynamic_slice_in_dim(grads, (place + k) % tp_count * part, part, axis=1), k, tp_count
         )
         for k in range(tp_count)
     )
@@ -591,8 +736,6 @@
     down_second,
 ):
     own, _, depth = latents_in.shape
-    latents = latents_in.reshape(own, depth)
-    cotangent = out_grad.reshape(own, depth)
     shard_rows = condition_weight.shape[0]
     part = condition_weight.shape[2]
     width = heads_weight.shape[2]
@@ -607,18 +750,20 @@
     spans = [(0, pairs // 2), (pairs // 2, pairs)] if pairs > 1 else [(0, pairs)]
     spans = [(start * PAIR, end * PAIR) for start, end in spans]
 
+    heads_low = jnp.moveaxis(heads_weight.astype(LOW), 0, 1)
+    heads_shard = jnp.concatenate(
+        [heads_low[:, :, start:end].reshape(shard_rows, -1) for start, end in spans], axis=1
+    )
     activated = jax.nn.silu(condition).astype(LOW)
+    activated, heads_shard = together(activated, heads_shard)
+    heads_whole = gather_rows(heads_shard)
     activated_rows = lax.all_to_all(
         activated.reshape(fsdp_count, shard_rows), "fsdp", split_axis=0, concat_axis=0, tiled=True
     )
-
-    heads_low = jnp.moveaxis(heads_weight.astype(LOW), 0, 1)
-    heads_whole = gather_rows(
-        jnp.concatenate(
-            [heads_low[:, :, start:end].reshape(shard_rows, -1) for start, end in spans], axis=1
-        )
-    )
-    unit_one, rate_one = standardize(latents)
+    latents, _ = together(latents_in.reshape(own, depth), heads_shard)
+    (cotangent,) = together(out_grad.reshape(own, depth))
+
+    unit_one, _ = standardize(latents)
     unit_blocks = blocks_of_tokens(unit_one.astype(LOW))
     shares = jnp.dot(
         activated_rows,
@@ -630,7 +775,7 @@
     merge_shard = jnp.concatenate([shift_tp(merge_shard, k, tp_count) for k in ring], axis=1)
     merge_line = gather_z(merge_shard, fsdp_count)
     feed_shard = jnp.concatenate([up_weight.astype(LOW), down_weight.astype(LOW).T], axis=1)
-    shares, unit_blocks = together(shares, unit_blocks)
+    shares, unit_blocks, cotangent = together(shares, unit_blocks, cotangent)
     modulation_part = jnp.sum(shares, axis=0).reshape(6, part)
     modulation = lax.all_gather(modulation_part, "tp", axis=1, tiled=True)
     shift_one, scale_one, gate_one, shift_two, scale_two, gate_two = (
@@ -666,10 +811,9 @@
         mixes.append((mixed, level))
         attended.append([shift_tp(mixed[k * own : (k + 1) * own], k, tp_count) for k in ring])
     attended_own = jnp.concatenate([part[k] for k in ring for part in attended], axis=1)
-    attn_branch = product_back([attended_own], merge_whole, FULL)
-    after_attn = latents + gate_one * attn_branch
-    unit_two, rate_two = standardize(after_attn)
-    normed_two = (unit_two * (1.0 + scale_two) + shift_two).astype(LOW)
+    attn_branch, after_attn, normed_two = merge_and_normalize(
+        attended_own, latents, merge_whole, gate_one, shift_two, scale_two
+    )
     normed_two_blocks = blocks_of_tokens(normed_two)
 
     fed = [feed_both(normed_two_blocks[0], branch_grad_blocks[0], feed_whole, FULL)]
@@ -689,88 +833,65 @@
     back_parts, branch_parts, feed_grad = together(back_parts, branch_parts, feed_grad)
     feed_sum = scatter_rows(feed_grad)
     branch_parts = [shift_tp(values, k, tp_count) for k, values in zip(others, branch_parts)]
-    normed_two_grad = fed[0][1]
-    for part_grad in back_parts:
-        normed_two_grad = normed_two_grad + part_grad.astype(FULL)
-    resid_two, shift_two_grad, scale_two_grad = standardize_back(
-        normed_two_grad, unit_two, rate_two, scale_two
-    )
-    after_grad = cotangent + resid_two
-    attn_grad = (gate_one * after_grad).astype(LOW)
-    gate_one_grad = jnp.sum(after_grad * attn_branch, axis=0)
-    attended_grad_own = product(attn_grad, merge_whole, LOW)
+    cuts = [(k * width + start, k * width + end) for k in ring for start, end in spans]
+    after_grad, attn_grad, pieces, second_sums = second_back(
+        fed[0][1], back_parts, after_attn, attn_branch, cotangent, merge_whole, gate_one, scale_two, cuts
+    )
     attended_grads = [
         jnp.concatenate(
-            [
-                shift_tp(attended_grad_own[:, k * width + start : k * width + end], -k, tp_count)
-                for k in ring
-            ],
-            axis=0,
+            [shift_tp(pieces[k * len(spans) + index], -k, tp_count) for k in ring], axis=0
         )
-        for start, end in spans
+        for index in range(len(spans))
     ]
-
     triple_grads = [
         attend_backward(triples[0], *mixes[0], attended_grads[0], spans[0][1] - spans[0][0])
     ]
     triple_grads, branch_parts = together(triple_grads, branch_parts)
-    mlp_branch = fed[0][0]
-    for part_branch in branch_parts:
-        mlp_branch = mlp_branch + part_branch.astype(FULL)
-    block_out = after_attn + gate_two * mlp_branch
-    gate_two_grad = jnp.sum(cotangent * mlp_branch, axis=0)
-    early_grads = jnp.stack([gate_one_grad, shift_two_grad, scale_two_grad, gate_two_grad], axis=0)
-
     pair = token_sum([([attn_grad], [attended_own]), ([normed_one], triple_grads)], fsdp_count)
+    if len(spans) > 1:
+        attended_grads, pair = together(attended_grads, pair)
     state = scatter_core(pair, fsdp_count)
-    if len(spans) > 1:
-        attended_grads, state, early_grads, block_out = together(
-            attended_grads, state, early_grads, block_out
-        )
-    state = scatter_x(state, fsdp_count)
     for index in range(1, len(spans)):
         start, end = spans[index]
         triple_grads.append(
             attend_backward(triples[index], *mixes[index], attended_grads[index], end - start)
         )
     triple_grads, state = together(triple_grads, state)
-    parts = [
-        product_back([grad[k * own : (k + 1) * own] for grad in triple_grads], heads_whole, LOW)
-        for k in others
-    ]
+    parts = [product_back(triple_grads, heads_whole, LOW, own, k) for k in others]
     one_parts = [shift_tp(values, k, tp_count) for k, values in zip(others, parts)]
+    state = scatter_x(state, fsdp_count)
     triple_grads, parts = together(triple_grads, parts)
     last = None
     if len(spans) > 1:
         pair = token_sum([([normed_one], triple_grads[1:])], fsdp_count)
         triple_grads, pair = together(triple_grads, pair)
         last = scatter_core(pair, fsdp_count)
-    normed_one_grad = product_back([grad[:own] for grad in triple_grads], heads_whole, FULL)
-    up_new = adam_step(up_weight, up_first, up_second, feed_sum[:, :units], 0.02)
-    down_new = adam_step(down_weight, down_first, down_second, feed_sum[:, units:].T, 0.01)
-    one_parts, normed_one_grad, state, last, up_new, down_new = together(
-        one_parts, normed_one_grad, state, last, up_new, down_new
+    normed_one_grad = product_back(triple_grads, heads_whole, FULL, own, 0)
+    block_out, last_sums = last_forward(fed[0][0], branch_parts, after_attn, cotangent, gate_two)
+    up_new = adam_step(up_weight, up_first, up_second, feed_sum[:, :units].astype(FULL), 0.02)
+    down_new = adam_step(down_weight, down_first, down_second, feed_sum[:, units:].T.astype(FULL), 0.01)
+    one_parts, normed_one_grad, block_out, state, last, up_new, down_new = together(
+        one_parts, normed_one_grad, block_out, state, last, up_new, down_new
     )
     if last:
         last = scatter_x(last, fsdp_count)
-    for part_grad in one_parts:
-        normed_one_grad = normed_one_grad + part_grad.astype(FULL)
-    resid_one, shift_one_grad, scale_one_grad = standardize_back(
-        normed_one_grad, unit_one, rate_one, scale_one
-    )
-    shift_one_grad, scale_one_grad, last = together(shift_one_grad, scale_one_grad, last)
-    first_sum = scatter_end(scatter_z(state, fsdp_count))
-    merge_sum_all, heads_sums = first_sum[:, : tp_count * width], [first_sum[:, tp_count * width :]]
+    latents_grad, first_sums = first_back(normed_one_grad, one_parts, latents, after_grad, scale_one)
+    first_sums, last = together(first_sums, last)
+    state = scatter_z(state, fsdp_count)
     if last:
-        heads_sums.append(scatter_end(scatter_z(last, fsdp_count)))
-    heads_sums = [total.reshape(shard_rows, 3, -1) for total in heads_sums]
-    latents_grad = after_grad + resid_one
+        last = scatter_z(last, fsdp_count)
     modulation_all = modulation_shares(
-        jnp.concatenate([jnp.stack([shift_one_grad, scale_one_grad], axis=0), early_grads], axis=0),
+        jnp.concatenate([first_sums[:2], second_sums[:3], last_sums[:1]], axis=0),
         tp_count,
         fsdp_count,
         part,
     )
+    modulation_all, state, last = together(modulation_all, state, last)
+    first_sum = scatter_end(state)
+    merge_sum_all, heads_sums = first_sum[:, : tp_count * width], [first_sum[:, tp_count * width :]]
+    if last:
+        heads_sums.append(scatter_end(last))
+    heads_sums = [total.reshape(shard_rows, 3, -1) for total in heads_sums]
     condition_sum = lax.dot_general(
         activated_rows.astype(FULL),
         modulation_all,

time: 409 us -> 393 us (0.961)
  other arithmetic: 56.4 us -> 26.2 us
  Pallas kernels: 153 us -> 170 us
  waiting for transfers between devices: 88.7 us -> 102 us
  local copies, waits for them, and re-layouts: 29.6 us -> 17.2 us
    pallas_call x3 -> x6, Pallas kernels: 16.5 us -> 37.3 us  [the longest x4 25.4 us: by_tokens(): pl.pallas_call(body, grid=(tokens // block,), in_specs=[cut(value.shape)...]
    ppermute x16, waiting for transfers between devices: 20.2 us -> 35.4 us  [shift_fsdp(): return lax.ppermute(values, 'fsdp', pairs)]
    reduce_sum x3 -> x0, other arithmetic: 9.42 us -> none  [the longest x2 5.81 us: standardize_back(): return (resid, jnp.sum(grad, axis=0), jnp.sum(grad * unit, axis=0))]
    add x3 -> x1, other arithmetic: 6.16 us -> 0.01 us  [modulation_shares(): sum((shift_tp(lax.dynamic_slice_in_dim(grads, (place + k) % tp_count * pa...]
    all_to_all x1, waiting for transfers between devices: 5.7 us -> 0.01 us  [modulation_shares(): lax.all_to_all(jnp.broadcast_to(total.reshape(1, count * part), (fsdp_cou...]
    reduce_sum x2 -> x1, other arithmetic: 5.38 us -> 0.18 us  [standardize(): middle = jnp.mean(values, axis=-1, keepdims=True)]
    ppermute x16, starting transfers between devices: 20.8 us -> 15.6 us  [shift_fsdp(): return lax.ppermute(values, 'fsdp', pairs)]
    slice x5 -> x3, local copies, waits for them, and re-layouts: 5.99 us -> 1.52 us  [the longest x1 0.76 us: local(): last_sums[:1]]
  transfers between devices with their start and end apart: 35 -> 35, of which waited for: 16 -> 16; matrix products, arithmetic and copies ran while one was open for 19% -> 9% of each run, Pallas kernels for 34% -> 40%
where the time goes in v2:
time: 393 us; the launch traced here: 387 us
  Pallas kernels  170 us (43%)
  waiting for transfers between devices  102 us (26%)
  starting transfers between devices  48.3 us (12%)
  other arithmetic  26.2 us (7%)
  local copies, waits for them, and re-layouts  17.2 us (4%)
  between operations  14.5 us (4%)
  blocking collectives  4.42 us (1%)
  matrix products  4.11 us (1%)
    ppermute x13, waiting for transfers between devices, shift_tp(): lax.ppermute(values, 'tp', [(i, (i + steps) % count) for i in range(count)])  40.8 us
    ppermute x16, waiting for transfers between devices, shift_fsdp(): return lax.ppermute(values, 'fsdp', pairs)  35.4 us
    pallas_call x2, Pallas kernels, attend_backward(): pl.pallas_call(body, grid=(pairs, steps), in_specs=[rows_of_pair, pl.Bloc...  35.1 us
    pallas_call x3, Pallas kernels, token_sum(): pl.pallas_call(body, grid=(width // tile,), in_specs=in_specs, out_specs=...  32.5 us
    pallas_call x2, Pallas kernels, feed_both(): pl.pallas_call(body, grid=(steps,), in_specs=[resident((tokens, depth)),...  32 us
    pallas_call x4, Pallas kernels, by_tokens(): pl.pallas_call(body, grid=(tokens // block,), in_specs=[cut(value.shape)...  25.4 us
    all_gather x2, waiting for transfers between devices, gather_rows(): return lax.all_gather(shard, 'fsdp', axis=0, tiled=True)  21.6 us
    pallas_call x2, Pallas kernels, attend_forward(): pl.pallas_call(body, grid=(pairs, tokens // block), in_specs=[pl.BlockSpe...  19.9 us
  transfers between devices with their start and end apart: 35, of which 16 were waited for; matrix products, arithmetic and copies ran while one was open for 9% of the time, Pallas kernels for 40%

profile of v2, /device:TPU:0, one launch (start us, length us, event | category | flops | bytes accessed | tf_op | source)
XLA Modules:
  0.0 387.2 jit_solution(7524285048153218869)
XLA Ops:
  10.4 7.4 %all-to-all-start = ((bf16[16,1,64]{2,1,0:T(2,128)(2,1)}), bf16[16,1,64]{2,1,0:T(2,128)(2,1)}, u32[]{:S(2)}, u32[]{:S(2)}) async-start(bf16[16,1,64]{2,1,0:T(2,128)(2,1)} %all_to_all.30), calls=%async_computation | async-start | bytes 16384 | tf_op jit(solution)/shard_map/all_to_all | solution.py:760
  26.4 6.0 %all-to-all-start.1 = ((f32[16,1,3072]{2,1,0:T(1,128)}), f32[16,1,3072]{2,1,0:T(1,128)S(1)}, u32[]{:S(2)}, u32[]{:S(2)}) async-start(f32[16,1,3072]{2,1,0:T(1,128)} %copy.88), calls=%async_computation.1 | async-start | bytes 393216 | tf_op jit(solution)/shard_map/all_to_all | solution.py:773
  36.6 12.3 %collective-permute-done.1 = bf16[64,512]{1,0:T(8,128)(2,1)} collective-permute-done((bf16[64,512]{1,0:T(8,128)(2,1)}, bf16[64,512]{1,0:T(8,128)(2,1)}, u32[]{:S(2)}, u32[]{:S(2)}) %collective-permute-start.1) | collective-permute-done | bytes 65568 | tf_op jit(solution)/shard_map/ppermute | solution.py:579
  74.9 5.4 %product.3.query_ref.keys_ref.values_ref = bf16[1024,768]{1,0:T(8,128)(2,1)} custom-call(bf16[1024,1024]{1,0:T(8,128)(2,1)} %pad_maximum_fusion.left_ref.refs_2_.refs_0_, bf16[1024,1536]{1,0:T(8,128)(2,1)} %all-gather.3.cloned.1.call-done.right_ref.refs_2_), custom_call_target="tpu_custom_call" | custom-call | flops 1610612736 | bytes 6815744 | tf_op jit(solution)/shard_map/product/pallas_call | solution.py:46
  80.4 10.0 %attend_forward.3 = (bf16[1024,256]{1,0:T(8,128)(2,1)}, f32[1024,256]{1,0:T(8,128)}) custom-call(bf16[1024,768]{1,0:T(8,128)(2,1)} %product.3.query_ref.keys_ref.values_ref, bf16[1024,768]{1,0:T(8,128)(2,1)} %product.3.query_ref.keys_ref.values_ref, bf16[1024,768]{1,0:T(8,128)(2,1)} %product.3.query_ref.keys_ref.values_ref), custom_call_target="tpu_custom_call" | custom-call | flops 4294967296 | bytes 3145728 | tf_op jit(solution)/shard_map/attend_forward/pallas_call | solution.py:219
  92.1 9.9 %attend_forward.2 = (bf16[1024,256]{1,0:T(8,128)(2,1)}, f32[1024,256]{1,0:T(8,128)}) custom-call(bf16[1024,768]{1,0:T(8,128)(2,1)} %product.2.query_ref.keys_ref.values_ref, bf16[1024,768]{1,0:T(8,128)(2,1)} %product.2.query_ref.keys_ref.values_ref, bf16[1024,768]{1,0:T(8,128)(2,1)} %product.2.query_ref.keys_ref.values_ref), custom_call_target="tpu_custom_call" | custom-call | flops 4294967296 | bytes 3145728 | tf_op jit(solution)/shard_map/attend_forward/pallas_call | solution.py:219
  105.2 6.9 %collective-permute-done.7 = bf16[512,256]{1,0:T(8,128)(2,1)S(1)} collective-permute-done((bf16[512,256]{1,0:T(8,128)(2,1)S(1)}, bf16[512,256]{1,0:T(8,128)(2,1)S(1)}, u32[]{:S(2)}, u32[]{:S(2)}) %collective-permute-start.7) | collective-permute-done | bytes 262176 | tf_op jit(solution)/shard_map/ppermute | solution.py:579
  117.4 5.6 %merge_and_normalize.1 = (f32[512,1024]{1,0:T(8,128)}, f32[512,1024]{1,0:T(8,128)}, bf16[512,1024]{1,0:T(8,128)(2,1)}) custom-call(bf16[512,1024]{1,0:T(8,128)(2,1)} %pad_maximum_fusion.1.attended_ref.refs_1_, f32[512,1024]{1,0:T(8,128)} %bitcast.83, bf16[1024,1024]{1,0:T(8,128)(2,1)} %arrange.1.merge_ref.refs_5_, ...), custom_call_target="tpu_custom_call" | custom-call | flops 1073741824 | bytes 10498048 | tf_op jit(solution)/shard_map/merge_and_normalize/pallas_call | solution.py:445
  124.4 20.9 %all-gather.5.cloned.1.call-done.up_ref.down_ref = bf16[1024,4096]{1,0:T(8,128)(2,1)} async-done(((bf16[64,4096]{1,0:T(8,128)(2,1)}), bf16[1024,4096]{1,0:T(8,128)(2,1)}) %all-gather.5.cloned.1.call-update) | async-done | bytes 8388624 | tf_op jit(solution)/shard_map/all_gather | solution.py:686
  145.3 16.2 %feed_both.2 = (f32[512,1024]{1,0:T(8,128)}, f32[512,1024]{1,0:T(8,128)}, bf16[512,2048]{1,0:T(8,128)(2,1)}, bf16[512,2048]{1,0:T(8,128)(2,1)}) custom-call(bf16[512,1024]{1,0:T(8,128)(2,1)} %get-tuple-element.156.normed_ref.refs_0_, bf16[512,1024]{1,0:T(8,128)(2,1)} %copy-done.11, bf16[1024,4096]{1,0:T(8,128)(2,1)} %all-gather.5.cloned.1.call-done.up_ref.down_ref, ...), custom_call_target="tpu_custom_call" | custom-call | flops 8589934592 | bytes 18874368 | tf_op jit(solution)/shard_map/feed_both/pallas_call | solution.py:371
  162.5 15.7 %feed_both.3 = (bf16[512,1024]{1,0:T(8,128)(2,1)}, bf16[512,1024]{1,0:T(8,128)(2,1)}, bf16[512,2048]{1,0:T(8,128)(2,1)}, bf16[512,2048]{1,0:T(8,128)(2,1)}) custom-call(bf16[512,1024]{1,0:T(8,128)(2,1)} %copy-done.34, bf16[512,1024]{1,0:T(8,128)(2,1)} %copy-done.32, bf16[1024,4096]{1,0:T(8,128)(2,1)} %all-gather.5.cloned.1.call-done.up_ref.down_ref, ...), custom_call_target="tpu_custom_call" | custom-call | flops 8589934592 | bytes 18874368 | tf_op jit(solution)/shard_map/feed_both/pallas_call | solution.py:371
  179.7 16.4 %token_sum.3 = bf16[1024,4096]{1,0:T(8,128)(2,1)} custom-call(bf16[512,1024]{1,0:T(8,128)(2,1)} %get-tuple-element.156.normed_ref.refs_0_, bf16[512,1024]{1,0:T(8,128)(2,1)} %copy-done.34, bf16[512,2048]{1,0:T(8,128)(2,1)} %get-tuple-element.157.refs_2_, bf16[512,2048]{1,0:T(8,128)(2,1)} %get-tuple-element.158.refs_3_, bf16[512,1024]{1,0:T(8,128)(2,1)} %copy-done.11, ...), custom_call_target="tpu_custom_call" | custom-call | flops 8589934592 | bytes 20971520 | tf_op jit(solution)/shard_map/token_sum/pallas_call | solution.py:159
  196.2 7.6 %collective-permute-done.12.refs_1_ = bf16[512,1024]{1,0:T(8,128)(2,1)S(1)} collective-permute-done((bf16[512,1024]{1,0:T(8,128)(2,1)}, bf16[512,1024]{1,0:T(8,128)(2,1)S(1)}, u32[]{:S(2)}, u32[]{:S(2)}) %collective-permute-start.12) | collective-permute-done | bytes 1048608 | tf_op jit(solution)/shard_map/ppermute | solution.py:579
  204.8 8.3 %second_back.1 = (f32[512,1024]{1,0:T(8,128)}, bf16[512,1024]{1,0:T(8,128)(2,1)}, bf16[512,256]{1,0:T(8,128)(2,1)}, bf16[512,256]{1,0:T(8,128)(2,1)}, bf16[512,2...) custom-call(f32[512,1024]{1,0:T(8,128)} %get-tuple-element.151.refs_0_, bf16[512,1024]{1,0:T(8,128)(2,1)} %copy-done.10, ...), custom_call_target="tpu_custom_call" | custom-call | flops 1073741824 | bytes 15769600 | tf_op jit(solution)/shard_map/second_back/pallas_call | solution.py:445
  229.0 17.5 %attend_backward.2.refs_3_.refs_0_ = bf16[1024,768]{1,0:T(8,128)(2,1)} custom-call(bf16[1024,768]{1,0:T(8,128)(2,1)} %product.2.query_ref.keys_ref.values_ref, bf16[1024,768]{1,0:T(8,128)(2,1)} %product.2.query_ref.keys_ref.values_ref, bf16[1024,768]{1,0:T(8,128)(2,1)} %product.2.query_ref.keys_ref.values_ref, ...), custom_call_target="tpu_custom_call" | custom-call | flops 10737418240 | bytes 5242880 | tf_op jit(solution)/shard_map/attend_backward/pallas_call | solution.py:311
  248.8 10.1 %token_sum.4 = (bf16[512,1792]{1,0:T(8,128)(2,1)}, bf16[512,1792]{1,0:T(8,128)(2,1)}) custom-call(bf16[512,1024]{1,0:T(8,128)(2,1)} %get-tuple-element.171.refs_0_, bf16[512,1024]{1,0:T(8,128)(2,1)} %pad_maximum_fusion.1.attended_ref.refs_1_, bf16[1024,1024]{1,0:T(8,128)(2,1)} %pad_maximum_fusion.left_ref.refs_2_.refs_0_, ...), custom_call_target="tpu_custom_call" | custom-call | flops 3758096384 | bytes 11534336 | tf_op jit(solution)/shard_map/token_sum/pallas_call | solution.py:159
  263.8 17.6 %attend_backward.3.refs_1_ = bf16[1024,768]{1,0:T(8,128)(2,1)} custom-call(bf16[1024,768]{1,0:T(8,128)(2,1)} %product.3.query_ref.keys_ref.values_ref, bf16[1024,768]{1,0:T(8,128)(2,1)} %product.3.query_ref.keys_ref.values_ref, bf16[1024,768]{1,0:T(8,128)(2,1)} %product.3.query_ref.keys_ref.values_ref, bf16[1024,256]{1,0:T(8,128)(2,1)} %get-tuple-element.141.out_low_ref, ...), custom_call_target="tpu_custom_call" | custom-call | flops 10737418240 | bytes 5242880 | tf_op jit(solution)/shard_map/attend_backward/pallas_call | solution.py:311
  281.4 6.2 %product_back.2 = bf16[512,1024]{1,0:T(8,128)(2,1)} custom-call(bf16[1024,768]{1,0:T(8,128)(2,1)} %attend_backward.2.refs_3_.refs_0_, bf16[1024,768]{1,0:T(8,128)(2,1)} %attend_backward.3.refs_1_, bf16[1024,1536]{1,0:T(8,128)(2,1)} %all-gather.3.cloned.1.call-done.right_ref.refs_2_), custom_call_target="tpu_custom_call" | custom-call | flops 1610612736 | bytes 6815744 | tf_op jit(solution)/shard_map/product_back/pallas_call | solution.py:77
  289.0 5.9 %token_sum.5 = (bf16[512,768]{1,0:T(8,128)(2,1)}, bf16[512,768]{1,0:T(8,128)(2,1)}) custom-call(bf16[1024,1024]{1,0:T(8,128)(2,1)} %pad_maximum_fusion.left_ref.refs_2_.refs_0_, bf16[1024,768]{1,0:T(8,128)(2,1)} %attend_backward.3.refs_1_), custom_call_target="tpu_custom_call" | custom-call | flops 1610612736 | bytes 5242880 | tf_op jit(solution)/shard_map/token_sum/pallas_call | solution.py:159
  296.7 5.8 %product_back.3.refs_0_ = f32[512,1024]{1,0:T(8,128)} custom-call(bf16[1024,768]{1,0:T(8,128)(2,1)} %attend_backward.2.refs_3_.refs_0_, bf16[1024,768]{1,0:T(8,128)(2,1)} %attend_backward.3.refs_1_, bf16[1024,1536]{1,0:T(8,128)(2,1)} %all-gather.3.cloned.1.call-done.right_ref.refs_2_), custom_call_target="tpu_custom_call" | custom-call | flops 1610612736 | bytes 6815744 | tf_op jit(solution)/shard_map/product_back/pallas_call | solution.py:77
  311.0 7.9 %collective-permute-done.18 = bf16[256,1792]{1,0:T(8,128)(2,1)} collective-permute-done((bf16[256,1792]{1,0:T(8,128)(2,1)}, bf16[256,1792]{1,0:T(8,128)(2,1)}, u32[]{:S(2)}, u32[]{:S(2)}) %collective-permute-start.18) | collective-permute-done | bytes 917536 | tf_op jit(solution)/shard_map/ppermute | solution.py:596
  321.2 6.6 %first_back.1 = (f32[512,8,128]{2,1,0:T(8,128)}, f32[8,1024]{1,0:T(8,128)}) custom-call(f32[512,1024]{1,0:T(8,128)} %product_back.3.refs_0_, bf16[512,1024]{1,0:T(8,128)(2,1)} %collective-permute-done.17.refs_1_, f32[512,1024]{1,0:T(8,128)} %bitcast.84, f32[512,1024]{1,0:T(8,128)} %get-tuple-element.196.refs_3_, f32[1,1024]{1,0:T(1,128)} %get-tuple-element.339.refs_4_), custom_call_target="tpu_custom_call" | custom-call | flops 10485760 | bytes 9474048 | tf_op jit(solution)/shard_map/first_back/pallas_call | solution.py:445
  354.2 12.7 %collective-permute-done.23 = bf16[64,1792]{1,0:T(8,128)(2,1)S(1)} collective-permute-done((bf16[64,1792]{1,0:T(8,128)(2,1)}, bf16[64,1792]{1,0:T(8,128)(2,1)S(1)}, u32[]{:S(2)}, u32[]{:S(2)}) %collective-permute-start.23) | collective-permute-done | bytes 229408 | tf_op jit(solution)/shard_map/ppermute | solution.py:596
  366.9 7.1 %collective-permute-done.26 = bf16[64,768]{1,0:T(8,128)(2,1)S(1)} collective-permute-done((bf16[64,768]{1,0:T(8,128)(2,1)}, bf16[64,768]{1,0:T(8,128)(2,1)S(1)}, u32[]{:S(2)}, u32[]{:S(2)}) %collective-permute-start.26) | collective-permute-done | bytes 98336 | tf_op jit(solution)/shard_map/ppermute | solution.py:596
  (212 shorter events, 126.6 us)
Async XLA Ops:
  7.2 59.9 %all-gather.3.cloned.1.call-start = ((), (), s32[]{:S(2)}) async-start(), calls=%async_computation.4 | async-start | bytes 3342336 | tf_op jit(solution)/shard_map/all_gather | solution.py:686
  10.4 14.2 %all-to-all-start = ((bf16[16,1,64]{2,1,0:T(2,128)(2,1)}), bf16[16,1,64]{2,1,0:T(2,128)(2,1)}, u32[]{:S(2)}, u32[]{:S(2)}) async-start(bf16[16,1,64]{2,1,0:T(2,128)(2,1)} %all_to_all.30), calls=%async_computation | async-start | bytes 16384 | tf_op jit(solution)/shard_map/all_to_all | solution.py:760
  21.8 33.6 %collective-permute-start = (bf16[512,1024]{1,0:T(8,128)(2,1)}, bf16[512,1024]{1,0:T(8,128)(2,1)}, u32[]{:S(2)}, u32[]{:S(2)}) collective-permute-start(bf16[512,1024]{1,0:T(8,128)(2,1)} %multiply_convert_fusion.1), channel_id=1, source_target_pairs={{0,1},{1,0},{2,3},{3,2},{4,5},{5,4},{6,7},{7,6},{8,9},{9,8},{10,11... | collective-permute-start | bytes 3145736 | tf_op jit(solution)/shard_map/ppermute | solution.py:579
  23.9 25.0 %collective-permute-start.1 = (bf16[64,512]{1,0:T(8,128)(2,1)}, bf16[64,512]{1,0:T(8,128)(2,1)}, u32[]{:S(2)}, u32[]{:S(2)}) collective-permute-start(bf16[64,512]{1,0:T(8,128)(2,1)} %convert_bitcast_fusion.3), channel_id=1, source_target_pairs={{0,1},{1,0},{2,3},{3,2},{4,5},{5,4},{6,7},{7,6},{8,9},{9,8},{10,11... | collective-permute-start | bytes 196616 | tf_op jit(solution)/shard_map/ppermute | solution.py:579
  26.4 29.0 %all-to-all-start.1 = ((f32[16,1,3072]{2,1,0:T(1,128)}), f32[16,1,3072]{2,1,0:T(1,128)S(1)}, u32[]{:S(2)}, u32[]{:S(2)}) async-start(f32[16,1,3072]{2,1,0:T(1,128)} %copy.88), calls=%async_computation.1 | async-start | bytes 393216 | tf_op jit(solution)/shard_map/all_to_all | solution.py:773
  32.3 113.0 %all-gather.5.cloned.1.call-start = ((), (), s32[]{:S(2)}) async-start(), calls=%async_computation.5 | async-start | bytes 8912896 | tf_op jit(solution)/shard_map/all_gather | solution.py:686
  49.8 14.1 %collective-permute-start.2 = (bf16[64,1024]{1,0:T(8,128)(2,1)S(1)}, bf16[64,1024]{1,0:T(8,128)(2,1)S(1)}, u32[]{:S(2)}, u32[]{:S(2)}) collective-permute-start(bf16[64,1024]{1,0:T(8,128)(2,1)S(1)} %pad_maximum_fusion.5), channel_id=1, source_target_pairs={{0,8},{2,10},{4,12},{6,14},{8,16},{10,18},{12,20},{14,22},{16,24},... | collective-permute-start | bytes 393224 | tf_op jit(solution)/shard_map/ppermute | solution.py:596
  51.5 14.9 %collective-permute-start.3 = (bf16[64,1024]{1,0:T(8,128)(2,1)S(1)}, bf16[64,1024]{1,0:T(8,128)(2,1)S(1)}, u32[]{:S(2)}, u32[]{:S(2)}) collective-permute-start(bf16[64,1024]{1,0:T(8,128)(2,1)S(1)} %pad_maximum_fusion.5), channel_id=1, source_target_pairs={{0,16},{2,18},{4,20},{6,22},{8,24},{10,26},{12,28},{14,30},{16,0},... | collective-permute-start | bytes 393224 | tf_op jit(solution)/shard_map/ppermute | solution.py:596
  67.2 239.8 %reduce-scatter.2.cloned.1.call-start = ((), (), s32[]{:S(2)}) async-start(), calls=%async_computation.6 | async-start | bytes 8912896 | tf_op jit(solution)/shard_map/reduce_scatter | solution.py:690
  67.7 34.4 %collective-permute-start.6 = (bf16[512,1024]{1,0:T(8,128)(2,1)S(1)}, bf16[512,1024]{1,0:T(8,128)(2,1)S(1)}, u32[]{:S(2)}, u32[]{:S(2)}) collective-permute-start(bf16[512,1024]{1,0:T(8,128)(2,1)S(1)} %multiply_convert_fusion.grad_ref.refs_4_), channel_id=1, source_target_pairs={{0,1},{1,0},{2,3},{3,2},{4,5},{5,4},{6,7},{7,6},{8,9},{9,8},{10,11... | collective-permute-start | bytes 3145736 | tf_op jit(solution)/shard_map/ppermute | solution.py:579
  74.5 27.5 %collective-permute-start.5 = (bf16[256,1024]{1,0:T(8,128)(2,1)S(1)}, bf16[256,1024]{1,0:T(8,128)(2,1)S(1)}, u32[]{:S(2)}, u32[]{:S(2)}) collective-permute-start(bf16[256,1024]{1,0:T(8,128)(2,1)S(1)} %constant_dynamic-update-slice_fusion.refs_0_), channel_id=1, source_target_pairs={{0,4},{2,6},{4,0},{6,2},{8,12},{10,14},{12,8},{14,10},{16,20},{18,... | collective-permute-start | bytes 1572872 | tf_op jit(solution)/shard_map/ppermute | solution.py:596
  123.0 38.6 %collective-permute-start.11 = (bf16[512,1024]{1,0:T(8,128)(2,1)}, bf16[512,1024]{1,0:T(8,128)(2,1)S(1)}, u32[]{:S(2)}, u32[]{:S(2)}) collective-permute-start(bf16[512,1024]{1,0:T(8,128)(2,1)} %get-tuple-element.156.normed_ref.refs_0_), channel_id=1, source_target_pairs={{0,1},{1,0},{2,3},{3,2},{4,5},{5,4},{6,7},{7,6},{8,9},{9,8},{10,11... | collective-permute-start | bytes 3145736 | tf_op jit(solution)/shard_map/ppermute | solution.py:579
  178.3 25.6 %collective-permute-start.12 = (bf16[512,1024]{1,0:T(8,128)(2,1)}, bf16[512,1024]{1,0:T(8,128)(2,1)S(1)}, u32[]{:S(2)}, u32[]{:S(2)}) collective-permute-start(bf16[512,1024]{1,0:T(8,128)(2,1)} %get-tuple-element.154), channel_id=1, source_target_pairs={{0,1},{1,0},{2,3},{3,2},{4,5},{5,4},{6,7},{7,6},{8,9},{9,8},{10,11... | collective-permute-start | bytes 3145736 | tf_op jit(solution)/shard_map/ppermute | solution.py:579
  215.2 33.6 %collective-permute-start.14 = (bf16[512,1024]{1,0:T(8,128)(2,1)S(1)}, bf16[512,1024]{1,0:T(8,128)(2,1)S(1)}, u32[]{:S(2)}, u32[]{:S(2)}) collective-permute-start(bf16[512,1024]{1,0:T(8,128)(2,1)S(1)} %copy-done.33), channel_id=1, source_target_pairs={{0,1},{1,0},{2,3},{3,2},{4,5},{5,4},{6,7},{7,6},{8,9},{9,8},{10,11... | collective-permute-start | bytes 3145736 | tf_op jit(solution)/shard_map/ppermute | solution.py:579
  258.9 22.5 %collective-permute-start.16 = (bf16[512,1792]{1,0:T(8,128)(2,1)}, bf16[512,1792]{1,0:T(8,128)(2,1)S(1)}, u32[]{:S(2)}, u32[]{:S(2)}) collective-permute-start(bf16[512,1792]{1,0:T(8,128)(2,1)} %get-tuple-element.176), channel_id=1, source_target_pairs={{0,2},{2,0},{4,6},{6,4},{8,10},{10,8},{12,14},{14,12},{16,18},{18,... | collective-permute-start | bytes 5505032 | tf_op jit(solution)/shard_map/ppermute | solution.py:596
  287.6 31.4 %collective-permute-start.17 = (bf16[512,1024]{1,0:T(8,128)(2,1)}, bf16[512,1024]{1,0:T(8,128)(2,1)}, u32[]{:S(2)}, u32[]{:S(2)}) collective-permute-start(bf16[512,1024]{1,0:T(8,128)(2,1)} %product_back.2), channel_id=1, source_target_pairs={{0,1},{1,0},{2,3},{3,2},{4,5},{5,4},{6,7},{7,6},{8,9},{9,8},{10,11... | collective-permute-start | bytes 3145736 | tf_op jit(solution)/shard_map/ppermute | solution.py:579
  296.2 22.7 %collective-permute-start.18 = (bf16[256,1792]{1,0:T(8,128)(2,1)}, bf16[256,1792]{1,0:T(8,128)(2,1)}, u32[]{:S(2)}, u32[]{:S(2)}) collective-permute-start(bf16[256,1792]{1,0:T(8,128)(2,1)} %add_convert_fusion.2), channel_id=1, source_target_pairs={{0,4},{2,6},{4,0},{6,2},{8,12},{10,14},{12,8},{14,10},{16,20},{18,... | collective-permute-start | bytes 2752520 | tf_op jit(solution)/shard_map/ppermute | solution.py:596
  296.7 14.3 %collective-permute-start.19 = (bf16[512,768]{1,0:T(8,128)(2,1)}, bf16[512,768]{1,0:T(8,128)(2,1)S(1)}, u32[]{:S(2)}, u32[]{:S(2)}) collective-permute-start(bf16[512,768]{1,0:T(8,128)(2,1)} %get-tuple-element.191), channel_id=1, source_target_pairs={{0,2},{2,0},{4,6},{6,4},{8,10},{10,8},{12,14},{14,12},{16,18},{18,... | collective-permute-start | bytes 2359304 | tf_op jit(solution)/shard_map/ppermute | solution.py:596
  335.9 18.3 %all-to-all-start.2 = ((f32[16,1,3072]{2,1,0:T(1,128)}), f32[16,1,3072]{2,1,0:T(1,128)S(1)}, u32[]{:S(2)}, u32[]{:S(2)}) async-start(f32[16,1,3072]{2,1,0:T(1,128)} %broadcast_in_dim.10), calls=%async_computation.3 | async-start | bytes 393216 | tf_op jit(solution)/shard_map/all_to_all | solution.py:706
  343.6 23.3 %collective-permute-start.23 = (bf16[64,1792]{1,0:T(8,128)(2,1)}, bf16[64,1792]{1,0:T(8,128)(2,1)S(1)}, u32[]{:S(2)}, u32[]{:S(2)}) collective-permute-start(bf16[64,1792]{1,0:T(8,128)(2,1)} %get-tuple-element.326), channel_id=1, source_target_pairs={{0,16},{2,18},{4,20},{6,22},{8,24},{10,26},{12,28},{14,30},{16,0},... | collective-permute-start | bytes 688136 | tf_op jit(solution)/shard_map/ppermute | solution.py:596
  346.1 20.8 %collective-permute-start.24 = (bf16[64,1792]{1,0:T(8,128)(2,1)S(1)}, bf16[64,1792]{1,0:T(8,128)(2,1)S(1)}, u32[]{:S(2)}, u32[]{:S(2)}) collective-permute-start(bf16[64,1792]{1,0:T(8,128)(2,1)S(1)} %get-tuple-element.325), channel_id=1, source_target_pairs={{0,24},{2,26},{4,28},{6,30},{8,0},{10,2},{12,4},{14,6},{16,8},{18,... | collective-permute-start | bytes 688136 | tf_op jit(solution)/shard_map/ppermute | solution.py:596
  349.4 17.6 %collective-permute-start.25 = (bf16[64,768]{1,0:T(8,128)(2,1)}, bf16[64,768]{1,0:T(8,128)(2,1)S(1)}, u32[]{:S(2)}, u32[]{:S(2)}) collective-permute-start(bf16[64,768]{1,0:T(8,128)(2,1)} %get-tuple-element.331), channel_id=1, source_target_pairs={{0,8},{2,10},{4,12},{6,14},{8,16},{10,18},{12,20},{14,22},{16,24},... | collective-permute-start | bytes 294920 | tf_op jit(solution)/shard_map/ppermute | solution.py:596
  349.9 24.1 %collective-permute-start.26 = (bf16[64,768]{1,0:T(8,128)(2,1)}, bf16[64,768]{1,0:T(8,128)(2,1)S(1)}, u32[]{:S(2)}, u32[]{:S(2)}) collective-permute-start(bf16[64,768]{1,0:T(8,128)(2,1)} %get-tuple-element.330), channel_id=1, source_target_pairs={{0,16},{2,18},{4,20},{6,22},{8,24},{10,26},{12,28},{14,30},{16,0},... | collective-permute-start | bytes 294920 | tf_op jit(solution)/shard_map/ppermute | solution.py:596
  353.0 21.0 %collective-permute-start.27 = (bf16[64,768]{1,0:T(8,128)(2,1)S(1)}, bf16[64,768]{1,0:T(8,128)(2,1)S(1)}, u32[]{:S(2)}, u32[]{:S(2)}) collective-permute-start(bf16[64,768]{1,0:T(8,128)(2,1)S(1)} %get-tuple-element.329), channel_id=1, source_target_pairs={{0,24},{2,26},{4,28},{6,30},{8,0},{10,2},{12,4},{14,6},{16,8},{18,... | collective-permute-start | bytes 294920 | tf_op jit(solution)/shard_map/ppermute | solution.py:596
  (50 other events, 452.5 us)
Sparse Core Ops, SparseCore 0:
  10.9 56.2 all-gather.2
  69.9 75.4 all-gather.4
  204.0 102.9 reduce-scatter.1

commit v3 on v2

--- a/solution.py
+++ b/solution.py
@@ -32,11 +32,10 @@
     return next(tile for tile in (most, 512, 256, PAIR) if tile <= most and width % tile == 0)
 
 
-def product(left, right, out_type, start=0, width=None):
+def product(left, right, out_type):
     rows, depth = left.shape
-    width = width or right.shape[1]
+    width = right.shape[1]
     tile = fit(width, 512)
-    first = start // tile
 
     def body(left_ref, right_ref, out_ref):
         out_ref[...] = jnp.dot(
@@ -48,7 +47,7 @@
         grid=(width // tile,),
         in_specs=[
             resident((rows, depth)),
-            pl.BlockSpec((depth, tile), lambda j: (0, first + j)),
+            pl.BlockSpec((depth, tile), lambda j: (0, j)),
         ],
         out_specs=pl.BlockSpec((rows, tile), lambda j: (0, j)),
         out_shape=jax.ShapeDtypeStruct((rows, width), out_type),
@@ -190,9 +189,10 @@
     return jnp.where((lane >= free) & (lane < free + 3), 1.0, values.astype(FULL)).astype(LOW)
 
 
-def attend_forward(triple, width):
+def attend_forward(triple, start, width):
     tokens = triple.shape[0]
     pairs = width // PAIR
+    first = start // PAIR
     block = min(512, tokens)
     scaling = HEAD ** (-0.5)
 
@@ -220,9 +220,9 @@
         body,
         grid=(pairs, tokens // block),
         in_specs=[
-            pl.BlockSpec((block, PAIR), lambda h, i: (i, h)),
-            pl.BlockSpec((tokens, PAIR), lambda h, i: (0, pairs + h)),
-            pl.BlockSpec((tokens, PAIR), lambda h, i: (0, 2 * pairs + h)),
+            pl.BlockSpec((block, PAIR), lambda h, i: (i, first + h)),
+            pl.BlockSpec((tokens, PAIR), lambda h, i: (0, first + pairs + h)),
+            pl.BlockSpec((tokens, PAIR), lambda h, i: (0, first + 2 * pairs + h)),
         ],
         out_specs=[pl.BlockSpec((block, PAIR), lambda h, i: (i, h))] * 2,
         out_shape=[
@@ -235,9 +235,10 @@
     )(triple, triple, triple)
 
 
-def attend_backward(triple, attended, level, grads, width):
+def attend_backward(triple, start, attended, level, grads, width):
     tokens = triple.shape[0]
     pairs = width // PAIR
+    first = start // PAIR
     block = min(512, tokens)
     steps = tokens // block
     scaling = HEAD ** (-0.5)
@@ -312,9 +313,9 @@
         body,
         grid=(pairs, steps),
         in_specs=[
-            rows_of_pair,
-            pl.BlockSpec((tokens, PAIR), lambda h, i: (0, pairs + h)),
-            pl.BlockSpec((tokens, PAIR), lambda h, i: (0, 2 * pairs + h)),
+            pl.BlockSpec((block, PAIR), lambda h, i: (i, first + h)),
+            pl.BlockSpec((tokens, PAIR), lambda h, i: (0, first + pairs + h)),
+            pl.BlockSpec((tokens, PAIR), lambda h, i: (0, first + 2 * pairs + h)),
             rows_of_pair,
             rows_of_pair,
             rows_of_pair,
@@ -596,24 +597,26 @@
     return lax.ppermute(values, "fsdp", pairs)
 
 
-def arrange(pieces, count, group):
+def arrange(pieces, count, group, by_z):
     deep, across, cores = digits(count)
     width = pieces[0].shape[1]
     tile = fit(width, 512)
+    outer, inner = (deep, across) if by_z else (across, deep)
 
     def body(*refs):
         out_ref = refs[-1]
         me = lax.axis_index("fsdp")
         my_z, my_x, my_c = me // (across * cores), (me // cores) % across, me % cores
         for core in range(cores):
-            for x in range(across):
-                source = refs[core * across + x]
-                for z in range(deep):
+            for first in range(outer):
+                source = refs[core * outer + first]
+                for second in range(inner):
+                    z, x = (first, second) if by_z else (second, first)
                     place = (
                         ((my_z - z + deep) % deep) * across + (my_x - x + across) % across
                     ) * cores + (my_c - core + cores) % cores
                     out_ref[pl.ds(pl.multiple_of(place * group, group), group), :] = source[
-                        z * group : (z + 1) * group, :
+                        second * group : (second + 1) * group, :
                     ]
 
     return pl.pallas_call(
@@ -771,13 +774,13 @@
         preferred_element_type=FULL,
     )
     shares = lax.all_to_all(shares, "fsdp", split_axis=0, concat_axis=0, tiled=True)
-    merge_shard = merge_weight.astype(LOW).T
-    merge_shard = jnp.concatenate([shift_tp(merge_shard, k, tp_count) for k in ring], axis=1)
-    merge_line = gather_z(merge_shard, fsdp_count)
     feed_shard = jnp.concatenate([up_weight.astype(LOW), down_weight.astype(LOW).T], axis=1)
     shares, unit_blocks, cotangent = together(shares, unit_blocks, cotangent)
     modulation_part = jnp.sum(shares, axis=0).reshape(6, part)
     modulation = lax.all_gather(modulation_part, "tp", axis=1, tiled=True)
+    modulation, merge_shard = together(modulation, merge_weight.astype(LOW).T)
+    merge_shard = jnp.concatenate([shift_tp(merge_shard, k, tp_count) for k in ring], axis=1)
+    merge_line = gather_z(merge_shard, fsdp_count)
     shift_one, scale_one, gate_one, shift_two, scale_two, gate_two = (
         modulation[k : k + 1] for k in range(6)
     )
@@ -796,18 +799,16 @@
         heads_whole, feed_shard, normed_one, merge_line
     )
     feed_whole = gather_rows(feed_shard)
-    triples = [
-        product(normed_one, heads_whole, LOW, 3 * start, 3 * (end - start)) for start, end in spans
-    ]
-    triples[0], merge_line = together(triples[0], merge_line)
+    triple = product(normed_one, heads_whole, LOW)
+    triple, merge_line = together(triple, merge_line)
     merge_plane = gather_x(merge_line, fsdp_count)
     attended = []
     mixes = []
     for index, (start, end) in enumerate(spans):
-        mixed, level = attend_forward(triples[index], end - start)
+        mixed, level = attend_forward(triple, 3 * start, end - start)
         if index == 0:
             mixed, merge_plane, branch_grad_blocks = together(mixed, merge_plane, branch_grad_blocks)
-            merge_whole = arrange(gather_core(merge_plane, fsdp_count), fsdp_count, shard_rows)
+            merge_whole = arrange(gather_core(merge_plane, fsdp_count), fsdp_count, shard_rows, False)
         mixes.append((mixed, level))
         attended.append([shift_tp(mixed[k * own : (k + 1) * own], k, tp_count) for k in ring])
     attended_own = jnp.concatenate([part[k] for k in ring for part in attended], axis=1)
@@ -816,11 +817,12 @@
     )
     normed_two_blocks = blocks_of_tokens(normed_two)
 
-    fed = [feed_both(normed_two_blocks[0], branch_grad_blocks[0], feed_whole, FULL)]
-    if tp_count > 1:
-        fed, normed_two_blocks = together(fed, normed_two_blocks)
-    fed += [feed_both(normed_two_blocks[k], branch_grad_blocks[k], feed_whole, LOW) for k in others]
+    fed = [None] + [feed_both(normed_two_blocks[k], branch_grad_blocks[k], feed_whole, LOW) for k in others]
     back_parts = [shift_tp(fed[k][1], k, tp_count) for k in others]
+    normed_two, fed = together(normed_two, fed)
+    fed[0] = feed_both(normed_two, branch_grad, feed_whole, FULL)
+    fed, branch_parts = together(fed, [fed[k][0] for k in others])
+    branch_parts = [shift_tp(values, k, tp_count) for k, values in zip(others, branch_parts)]
     (feed_grad,) = token_sum(
         [
             (normed_two_blocks, [fed[k][3] for k in ring]),
@@ -829,57 +831,54 @@
         fsdp_count,
         ordered=False,
     )
-    branch_parts = [fed[k][0] for k in others]
-    back_parts, branch_parts, feed_grad = together(back_parts, branch_parts, feed_grad)
+    back_parts, feed_grad = together(back_parts, feed_grad)
     feed_sum = scatter_rows(feed_grad)
-    branch_parts = [shift_tp(values, k, tp_count) for k, values in zip(others, branch_parts)]
     cuts = [(k * width + start, k * width + end) for k in ring for start, end in spans]
     after_grad, attn_grad, pieces, second_sums = second_back(
         fed[0][1], back_parts, after_attn, attn_branch, cotangent, merge_whole, gate_one, scale_two, cuts
     )
-    attended_grads = [
-        jnp.concatenate(
-            [shift_tp(pieces[k * len(spans) + index], -k, tp_count) for k in ring], axis=0
+    attended_grads = []
+    for index in range(len(spans)):
+        mine = pieces[index :: len(spans)]
+        if index:
+            attended_grads, mine = together(attended_grads, mine)
+        attended_grads.append(
+            jnp.concatenate([shift_tp(mine[k], -k, tp_count) for k in ring], axis=0)
         )
-        for index in range(len(spans))
+    triple_grads = [
+        attend_backward(triple, 0, *mixes[0], attended_grads[0], spans[0][1])
     ]
-    triple_grads = [
-        attend_backward(triples[0], *mixes[0], attended_grads[0], spans[0][1] - spans[0][0])
-    ]
-    triple_grads, branch_parts = together(triple_grads, branch_parts)
+    triple_grads, branch_parts, attended_grads = together(triple_grads, branch_parts, attended_grads)
     pair = token_sum([([attn_grad], [attended_own]), ([normed_one], triple_grads)], fsdp_count)
-    if len(spans) > 1:
-        attended_grads, pair = together(attended_grads, pair)
     state = scatter_core(pair, fsdp_count)
+    block_out, last_sums = last_forward(fed[0][0], branch_parts, after_attn, cotangent, gate_two)
+    attended_grads, state, block_out = together(attended_grads, state, block_out)
+    state = scatter_x(state, fsdp_count)
     for index in range(1, len(spans)):
         start, end = spans[index]
         triple_grads.append(
-            attend_backward(triples[index], *mixes[index], attended_grads[index], end - start)
+            attend_backward(triple, 3 * start, *mixes[index], attended_grads[index], end - start)
         )
-    triple_grads, state = together(triple_grads, state)
     parts = [product_back(triple_grads, heads_whole, LOW, own, k) for k in others]
     one_parts = [shift_tp(values, k, tp_count) for k, values in zip(others, parts)]
-    state = scatter_x(state, fsdp_count)
     triple_grads, parts = together(triple_grads, parts)
     last = None
     if len(spans) > 1:
-        pair = token_sum([([normed_one], triple_grads[1:])], fsdp_count)
-        triple_grads, pair = together(triple_grads, pair)
-        last = scatter_core(pair, fsdp_count)
+        last = token_sum([([normed_one], triple_grads[1:])], fsdp_count)
+    triple_grads, last, state = together(triple_grads, last, state)
+    state = scatter_z(state, fsdp_count)
+    if last:
+        last = scatter_core(last, fsdp_count)
     normed_one_grad = product_back(triple_grads, heads_whole, FULL, own, 0)
-    block_out, last_sums = last_forward(fed[0][0], branch_parts, after_attn, cotangent, gate_two)
-    up_new = adam_step(up_weight, up_first, up_second, feed_sum[:, :units].astype(FULL), 0.02)
-    down_new = adam_step(down_weight, down_first, down_second, feed_sum[:, units:].T.astype(FULL), 0.01)
-    one_parts, normed_one_grad, block_out, state, last, up_new, down_new = together(
-        one_parts, normed_one_grad, block_out, state, last, up_new, down_new
-    )
+    one_parts, normed_one_grad, last = together(one_parts, normed_one_grad, last)
     if last:
         last = scatter_x(last, fsdp_count)
     latents_grad, first_sums = first_back(normed_one_grad, one_parts, latents, after_grad, scale_one)
-    first_sums, last = together(first_sums, last)
-    state = scatter_z(state, fsdp_count)
+    first_sums, last, feed_sum = together(first_sums, last, feed_sum)
     if last:
         last = scatter_z(last, fsdp_count)
+    up_new = adam_step(up_weight, up_first, up_second, feed_sum[:, :units].astype(FULL), 0.02)
+    down_new = adam_step(down_weight, down_first, down_second, feed_sum[:, units:].T.astype(FULL), 0.01)
     modulation_all = modulation_shares(
         jnp.concatenate([first_sums[:2], second_sums[:3], last_sums[:1]], axis=0),
         tp_count,

time: 393 us -> 364 us (0.926)
  waiting for transfers between devices: 102 us -> 79.4 us
  Pallas kernels: 170 us -> 165 us
  starting transfers between devices: 48.3 us -> 52.8 us
    ppermute x16, waiting for transfers between devices: 35.4 us -> 6.92 us  [shift_fsdp(): return lax.ppermute(values, 'fsdp', pairs)]
    all_gather x2, waiting for transfers between devices: 21.6 us -> 0.97 us  [gather_rows(): return lax.all_gather(shard, 'fsdp', axis=0, tiled=True)]
    ppermute x13, waiting for transfers between devices: 40.8 us -> 60.2 us  [shift_tp(): lax.ppermute(values, 'tp', [(i, (i + steps) % count) for i in range(count)])]
    all_to_all x1, waiting for transfers between devices: 0.01 us -> 8.22 us  [local(): lax.all_to_all(shares, 'fsdp', split_axis=0, concat_axis=0, tiled=True)]
    reduce_scatter x1, waiting for transfers between devices: 4.44 us -> 0.02 us  [scatter_rows(): return lax.psum_scatter(whole, 'fsdp', scatter_dimension=0, tiled=True)]
    ppermute x16, starting transfers between devices: 15.6 us -> 19.8 us  [shift_fsdp(): return lax.ppermute(values, 'fsdp', pairs)]
    pallas_call x2 -> x1, Pallas kernels: 10.7 us -> 7.06 us  [product(): pl.pallas_call(body, grid=(width // tile,), in_specs=[resident((rows, dep...]
    unnamed x83 -> x87, local copies, waits for them, and re-layouts: 10.9 us -> 7.57 us
  transfers between devices with their start and end apart: 35 -> 35, of which waited for: 16 -> 14; matrix products, arithmetic and copies ran while one was open for 9% -> 9% of each run, Pallas kernels for 40% -> 42%
where the time goes in v3:
time: 364 us; the launch traced here: 359 us
  Pallas kernels  165 us (45%)
  waiting for transfers between devices  79.4 us (22%)
  starting transfers between devices  52.8 us (15%)
  other arithmetic  26.2 us (7%)
  between operations  15 us (4%)
  local copies, waits for them, and re-layouts  13.9 us (4%)
  blocking collectives  4.42 us (1%)
    ppermute x13, waiting for transfers between devices, shift_tp(): lax.ppermute(values, 'tp', [(i, (i + steps) % count) for i in range(count)])  60.2 us
    pallas_call x2, Pallas kernels, attend_backward(): pl.pallas_call(body, grid=(pairs, steps), in_specs=[pl.BlockSpec((block,...  35.1 us
    pallas_call x3, Pallas kernels, token_sum(): pl.pallas_call(body, grid=(width // tile,), in_specs=in_specs, out_specs=...  32.5 us
    pallas_call x2, Pallas kernels, feed_both(): pl.pallas_call(body, grid=(steps,), in_specs=[resident((tokens, depth)),...  31.9 us
    pallas_call x4, Pallas kernels, by_tokens(): pl.pallas_call(body, grid=(tokens // block,), in_specs=[cut(value.shape)...  24.5 us
    pallas_call x2, Pallas kernels, attend_forward(): pl.pallas_call(body, grid=(pairs, tokens // block), in_specs=[pl.BlockSpe...  19.9 us
    ppermute x16, starting transfers between devices, shift_fsdp(): return lax.ppermute(values, 'fsdp', pairs)  19.8 us
    ppermute x13, starting transfers between devices, shift_tp(): lax.ppermute(values, 'tp', [(i, (i + steps) % count) for i in range(count)])  14.9 us
  transfers between devices with their start and end apart: 35, of which 14 were waited for; matrix products, arithmetic and copies ran while one was open for 9% of the time, Pallas kernels for 42%

profile of v3, /device:TPU:0, one launch (start us, length us, event | category | flops | bytes accessed | tf_op | source)
XLA Modules:
  0.0 359.3 jit_solution(3454586052610431711)
XLA Ops:
  10.4 7.4 %all-to-all-start = ((bf16[16,1,64]{2,1,0:T(2,128)(2,1)}), bf16[16,1,64]{2,1,0:T(2,128)(2,1)S(1)}, u32[]{:S(2)}, u32[]{:S(2)}) async-start(bf16[16,1,64]{2,1,0:T(2,128)(2,1)} %all_to_all.30), calls=%async_computation | async-start | bytes 16384 | tf_op jit(solution)/shard_map/all_to_all | solution.py:763
  26.9 6.0 %all-to-all-start.1 = ((f32[16,1,3072]{2,1,0:T(1,128)}), f32[16,1,3072]{2,1,0:T(1,128)S(1)}, u32[]{:S(2)}, u32[]{:S(2)}) async-start(f32[16,1,3072]{2,1,0:T(1,128)} %copy.88), calls=%async_computation.1 | async-start | bytes 393216 | tf_op jit(solution)/shard_map/all_to_all | solution.py:776
  33.8 8.2 %all-to-all-done.1 = f32[16,1,3072]{2,1,0:T(1,128)S(1)} async-done(((f32[16,1,3072]{2,1,0:T(1,128)}), f32[16,1,3072]{2,1,0:T(1,128)S(1)}, u32[]{:S(2)}, u32[]{:S(2)}) %all-to-all-start.1) | async-done | bytes 196640 | tf_op jit(solution)/shard_map/all_to_all | solution.py:776
  42.1 5.4 %collective-permute-done = bf16[512,1024]{1,0:T(8,128)(2,1)} collective-permute-done((bf16[512,1024]{1,0:T(8,128)(2,1)}, bf16[512,1024]{1,0:T(8,128)(2,1)}, u32[]{:S(2)}, u32[]{:S(2)}) %collective-permute-start) | collective-permute-done | bytes 1048608 | tf_op jit(solution)/shard_map/ppermute | solution.py:580
  70.0 7.1 %product.1.query_ref.keys_ref.values_ref = bf16[1024,1536]{1,0:T(8,128)(2,1)} custom-call(bf16[1024,1024]{1,0:T(8,128)(2,1)} %pad_maximum_fusion.left_ref.refs_2_.refs_0_, bf16[1024,1536]{1,0:T(8,128)(2,1)} %all-gather.3.cloned.1.call-done.right_ref.refs_2_), custom_call_target="tpu_custom_call" | custom-call | flops 3221225472 | bytes 11534336 | tf_op jit(solution)/shard_map/product/pallas_call | solution.py:45
  78.8 10.0 %attend_forward.3 = (bf16[1024,256]{1,0:T(8,128)(2,1)}, f32[1024,256]{1,0:T(8,128)}) custom-call(bf16[1024,1536]{1,0:T(8,128)(2,1)} %product.1.query_ref.keys_ref.values_ref, bf16[1024,1536]{1,0:T(8,128)(2,1)} %product.1.query_ref.keys_ref.values_ref, bf16[1024,1536]{1,0:T(8,128)(2,1)} %product.1.query_ref.keys_ref.values_ref), custom_call_target="tpu_custom_call" | custom-call | flops 4294967296 | bytes 3145728 | tf_op jit(solution)/shard_map/attend_forward/pallas_call | solution.py:219
  90.6 9.9 %attend_forward.2 = (bf16[1024,256]{1,0:T(8,128)(2,1)}, f32[1024,256]{1,0:T(8,128)}) custom-call(bf16[1024,1536]{1,0:T(8,128)(2,1)} %product.1.query_ref.keys_ref.values_ref, bf16[1024,1536]{1,0:T(8,128)(2,1)} %product.1.query_ref.keys_ref.values_ref, bf16[1024,1536]{1,0:T(8,128)(2,1)} %product.1.query_ref.keys_ref.values_ref), custom_call_target="tpu_custom_call" | custom-call | flops 4294967296 | bytes 3145728 | tf_op jit(solution)/shard_map/attend_forward/pallas_call | solution.py:219
  103.7 6.9 %collective-permute-done.7 = bf16[512,256]{1,0:T(8,128)(2,1)S(1)} collective-permute-done((bf16[512,256]{1,0:T(8,128)(2,1)S(1)}, bf16[512,256]{1,0:T(8,128)(2,1)S(1)}, u32[]{:S(2)}, u32[]{:S(2)}) %collective-permute-start.7) | collective-permute-done | bytes 262176 | tf_op jit(solution)/shard_map/ppermute | solution.py:580
  115.9 5.4 %merge_and_normalize.1 = (f32[512,1024]{1,0:T(8,128)}, f32[512,1024]{1,0:T(8,128)}, bf16[512,1024]{1,0:T(8,128)(2,1)}) custom-call(bf16[512,1024]{1,0:T(8,128)(2,1)} %pad_maximum_fusion.1.attended_ref.refs_1_, f32[512,1024]{1,0:T(8,128)} %bitcast.83, bf16[1024,1024]{1,0:T(8,128)(2,1)} %arrange.1.merge_ref.refs_5_, ...), custom_call_target="tpu_custom_call" | custom-call | flops 1073741824 | bytes 10498048 | tf_op jit(solution)/shard_map/merge_and_normalize/pallas_call | solution.py:446
  122.8 23.2 %collective-permute-done.11.normed_ref.refs_1_ = bf16[512,1024]{1,0:T(8,128)(2,1)S(1)} collective-permute-done((bf16[512,1024]{1,0:T(8,128)(2,1)}, bf16[512,1024]{1,0:T(8,128)(2,1)S(1)}, u32[]{:S(2)}, u32[]{:S(2)}) %collective-permute-start.11) | collective-permute-done | bytes 1048608 | tf_op jit(solution)/shard_map/ppermute | solution.py:580
  146.9 15.4 %feed_both.2 = (bf16[512,1024]{1,0:T(8,128)(2,1)}, bf16[512,1024]{1,0:T(8,128)(2,1)}, bf16[512,2048]{1,0:T(8,128)(2,1)}, bf16[512,2048]{1,0:T(8,128)(2,1)}) custom-call(bf16[512,1024]{1,0:T(8,128)(2,1)} %copy-done.36, bf16[512,1024]{1,0:T(8,128)(2,1)} %copy-done.34, bf16[1024,4096]{1,0:T(8,128)(2,1)} %all-gather.5.cloned.1.call-done.up_ref.down_ref, ...), custom_call_target="tpu_custom_call" | custom-call | flops 8589934592 | bytes 18874368 | tf_op jit(solution)/shard_map/feed_both/pallas_call | solution.py:372
  163.9 16.4 %feed_both.3 = (f32[512,1024]{1,0:T(8,128)}, f32[512,1024]{1,0:T(8,128)}, bf16[512,2048]{1,0:T(8,128)(2,1)}, bf16[512,2048]{1,0:T(8,128)(2,1)}) custom-call(bf16[512,1024]{1,0:T(8,128)(2,1)} %get-tuple-element.154.normed_ref.refs_0_, bf16[512,1024]{1,0:T(8,128)(2,1)} %copy-done.12, bf16[1024,4096]{1,0:T(8,128)(2,1)} %all-gather.5.cloned.1.call-done.up_ref.down_ref, ...), custom_call_target="tpu_custom_call" | custom-call | flops 8589934592 | bytes 18874368 | tf_op jit(solution)/shard_map/feed_both/pallas_call | solution.py:372
  180.3 16.5 %token_sum.3 = bf16[1024,4096]{1,0:T(8,128)(2,1)} custom-call(bf16[512,1024]{1,0:T(8,128)(2,1)} %get-tuple-element.154.normed_ref.refs_0_, bf16[512,1024]{1,0:T(8,128)(2,1)} %copy-done.36, bf16[512,2048]{1,0:T(8,128)(2,1)} %get-tuple-element.163.refs_2_, bf16[512,2048]{1,0:T(8,128)(2,1)} %get-tuple-element.164.refs_3_, bf16[512,1024]{1,0:T(8,128)(2,1)} %copy-done.12, ...), custom_call_target="tpu_custom_call" | custom-call | flops 8589934592 | bytes 20971520 | tf_op jit(solution)/shard_map/token_sum/pallas_call | solution.py:158
  197.8 7.9 %second_back.1 = (f32[512,1024]{1,0:T(8,128)}, bf16[512,1024]{1,0:T(8,128)(2,1)}, bf16[512,256]{1,0:T(8,128)(2,1)}, bf16[512,256]{1,0:T(8,128)(2,1)}, bf16[512,2...) custom-call(f32[512,1024]{1,0:T(8,128)} %get-tuple-element.162.refs_0_, bf16[512,1024]{1,0:T(8,128)(2,1)} %copy-done.11, ...), custom_call_target="tpu_custom_call" | custom-call | flops 1073741824 | bytes 15769600 | tf_op jit(solution)/shard_map/second_back/pallas_call | solution.py:446
  207.8 7.4 %collective-permute-done.13 = bf16[512,256]{1,0:T(8,128)(2,1)S(1)} collective-permute-done((bf16[512,256]{1,0:T(8,128)(2,1)}, bf16[512,256]{1,0:T(8,128)(2,1)S(1)}, u32[]{:S(2)}, u32[]{:S(2)}) %collective-permute-start.13) | collective-permute-done | bytes 262176 | tf_op jit(solution)/shard_map/ppermute | solution.py:580
  217.5 17.6 %attend_backward.2.refs_3_.refs_0_ = bf16[1024,768]{1,0:T(8,128)(2,1)} custom-call(bf16[1024,1536]{1,0:T(8,128)(2,1)} %product.1.query_ref.keys_ref.values_ref, bf16[1024,1536]{1,0:T(8,128)(2,1)} %product.1.query_ref.keys_ref.values_ref, bf16[1024,1536]{1,0:T(8,128)(2,1)} %product.1.query_ref.keys_ref.values_ref, ...), custom_call_target="tpu_custom_call" | custom-call | flops 10737418240 | bytes 5242880 | tf_op jit(solution)/shard_map/attend_backward/pallas_call | solution.py:312
  235.1 7.2 %collective-permute-done.15 = bf16[512,256]{1,0:T(8,128)(2,1)S(1)} collective-permute-done((bf16[512,256]{1,0:T(8,128)(2,1)}, bf16[512,256]{1,0:T(8,128)(2,1)S(1)}, u32[]{:S(2)}, u32[]{:S(2)}) %collective-permute-start.15) | collective-permute-done | bytes 262176 | tf_op jit(solution)/shard_map/ppermute | solution.py:580
  243.1 10.0 %token_sum.4 = (bf16[512,1792]{1,0:T(8,128)(2,1)}, bf16[512,1792]{1,0:T(8,128)(2,1)}) custom-call(bf16[512,1024]{1,0:T(8,128)(2,1)} %get-tuple-element.180.refs_0_, bf16[512,1024]{1,0:T(8,128)(2,1)} %pad_maximum_fusion.1.attended_ref.refs_1_, bf16[1024,1024]{1,0:T(8,128)(2,1)} %pad_maximum_fusion.left_ref.refs_2_.refs_0_, ...), custom_call_target="tpu_custom_call" | custom-call | flops 3758096384 | bytes 11534336 | tf_op jit(solution)/shard_map/token_sum/pallas_call | solution.py:158
  259.1 17.5 %attend_backward.3.refs_1_ = bf16[1024,768]{1,0:T(8,128)(2,1)} custom-call(bf16[1024,1536]{1,0:T(8,128)(2,1)} %product.1.query_ref.keys_ref.values_ref, bf16[1024,1536]{1,0:T(8,128)(2,1)} %product.1.query_ref.keys_ref.values_ref, bf16[1024,1536]{1,0:T(8,128)(2,1)} %product.1.query_ref.keys_ref.values_ref, bf16[1024,256]{1,0:T(8,128)(2,1)} %get-tuple-element.144.out_low_ref, ...), custom_call_target="tpu_custom_call" | custom-call | flops 10737418240 | bytes 5242880 | tf_op jit(solution)/shard_map/attend_backward/pallas_call | solution.py:312
  276.6 5.5 %product_back.2 = bf16[512,1024]{1,0:T(8,128)(2,1)} custom-call(bf16[1024,768]{1,0:T(8,128)(2,1)} %attend_backward.2.refs_3_.refs_0_, bf16[1024,768]{1,0:T(8,128)(2,1)} %attend_backward.3.refs_1_, bf16[1024,1536]{1,0:T(8,128)(2,1)} %all-gather.3.cloned.1.call-done.right_ref.refs_2_), custom_call_target="tpu_custom_call" | custom-call | flops 1610612736 | bytes 6815744 | tf_op jit(solution)/shard_map/product_back/pallas_call | solution.py:76
  282.8 6.0 %token_sum.5 = (bf16[512,768]{1,0:T(8,128)(2,1)}, bf16[512,768]{1,0:T(8,128)(2,1)}) custom-call(bf16[1024,1024]{1,0:T(8,128)(2,1)} %pad_maximum_fusion.left_ref.refs_2_.refs_0_, bf16[1024,768]{1,0:T(8,128)(2,1)} %attend_backward.3.refs_1_), custom_call_target="tpu_custom_call" | custom-call | flops 1610612736 | bytes 5242880 | tf_op jit(solution)/shard_map/token_sum/pallas_call | solution.py:158
  292.0 5.9 %product_back.3.refs_0_ = f32[512,1024]{1,0:T(8,128)} custom-call(bf16[1024,768]{1,0:T(8,128)(2,1)} %attend_backward.2.refs_3_.refs_0_, bf16[1024,768]{1,0:T(8,128)(2,1)} %attend_backward.3.refs_1_, bf16[1024,1536]{1,0:T(8,128)(2,1)} %all-gather.3.cloned.1.call-done.right_ref.refs_2_), custom_call_target="tpu_custom_call" | custom-call | flops 1610612736 | bytes 6815744 | tf_op jit(solution)/shard_map/product_back/pallas_call | solution.py:76
  297.9 9.8 %collective-permute-done.17.refs_1_ = bf16[512,1024]{1,0:T(8,128)(2,1)} collective-permute-done((bf16[512,1024]{1,0:T(8,128)(2,1)}, bf16[512,1024]{1,0:T(8,128)(2,1)}, u32[]{:S(2)}, u32[]{:S(2)}) %collective-permute-start.17) | collective-permute-done | bytes 1048608 | tf_op jit(solution)/shard_map/ppermute | solution.py:580
  314.9 6.2 %first_back.1 = (f32[512,8,128]{2,1,0:T(8,128)}, f32[8,1024]{1,0:T(8,128)}) custom-call(f32[512,1024]{1,0:T(8,128)} %product_back.3.refs_0_, bf16[512,1024]{1,0:T(8,128)(2,1)} %collective-permute-done.17.refs_1_, f32[512,1024]{1,0:T(8,128)} %bitcast.84, f32[512,1024]{1,0:T(8,128)} %get-tuple-element.202.refs_3_, f32[1,1024]{1,0:T(1,128)} %get-tuple-element.341.refs_4_), custom_call_target="tpu_custom_call" | custom-call | flops 10485760 | bytes 9474048 | tf_op jit(solution)/shard_map/first_back/pallas_call | solution.py:446
  (215 shorter events, 105.5 us)
Async XLA Ops:
  7.2 60.7 %all-gather.3.cloned.1.call-start = ((), (), s32[]{:S(2)}) async-start(), calls=%async_computation.4 | async-start | bytes 3342336 | tf_op jit(solution)/shard_map/all_gather | solution.py:689
  10.4 15.4 %all-to-all-start = ((bf16[16,1,64]{2,1,0:T(2,128)(2,1)}), bf16[16,1,64]{2,1,0:T(2,128)(2,1)S(1)}, u32[]{:S(2)}, u32[]{:S(2)}) async-start(bf16[16,1,64]{2,1,0:T(2,128)(2,1)} %all_to_all.30), calls=%async_computation | async-start | bytes 16384 | tf_op jit(solution)/shard_map/all_to_all | solution.py:763
  21.7 25.8 %collective-permute-start = (bf16[512,1024]{1,0:T(8,128)(2,1)}, bf16[512,1024]{1,0:T(8,128)(2,1)}, u32[]{:S(2)}, u32[]{:S(2)}) collective-permute-start(bf16[512,1024]{1,0:T(8,128)(2,1)} %multiply_convert_fusion.1), channel_id=1, source_target_pairs={{0,1},{1,0},{2,3},{3,2},{4,5},{5,4},{6,7},{7,6},{8,9},{9,8},{10,11... | collective-permute-start | bytes 3145736 | tf_op jit(solution)/shard_map/ppermute | solution.py:580
  26.9 15.1 %all-to-all-start.1 = ((f32[16,1,3072]{2,1,0:T(1,128)}), f32[16,1,3072]{2,1,0:T(1,128)S(1)}, u32[]{:S(2)}, u32[]{:S(2)}) async-start(f32[16,1,3072]{2,1,0:T(1,128)} %copy.88), calls=%async_computation.1 | async-start | bytes 393216 | tf_op jit(solution)/shard_map/all_to_all | solution.py:776
  32.9 114.0 %all-gather.5.cloned.1.call-start = ((), (), s32[]{:S(2)}) async-start(), calls=%async_computation.5 | async-start | bytes 8912896 | tf_op jit(solution)/shard_map/all_gather | solution.py:689
  67.9 253.2 %reduce-scatter.2.cloned.1.call-start = ((), (), s32[]{:S(2)}) async-start(), calls=%async_computation.6 | async-start | bytes 8912896 | tf_op jit(solution)/shard_map/reduce_scatter | solution.py:693
  68.4 32.1 %collective-permute-start.6 = (bf16[512,1024]{1,0:T(8,128)(2,1)S(1)}, bf16[512,1024]{1,0:T(8,128)(2,1)S(1)}, u32[]{:S(2)}, u32[]{:S(2)}) collective-permute-start(bf16[512,1024]{1,0:T(8,128)(2,1)S(1)} %multiply_convert_fusion.grad_ref.refs_4_), channel_id=1, source_target_pairs={{0,1},{1,0},{2,3},{3,2},{4,5},{5,4},{6,7},{7,6},{8,9},{9,8},{10,11... | collective-permute-start | bytes 3145736 | tf_op jit(solution)/shard_map/ppermute | solution.py:580
  77.2 23.4 %collective-permute-start.5 = (bf16[256,1024]{1,0:T(8,128)(2,1)S(1)}, bf16[256,1024]{1,0:T(8,128)(2,1)S(1)}, u32[]{:S(2)}, u32[]{:S(2)}) collective-permute-start(bf16[256,1024]{1,0:T(8,128)(2,1)S(1)} %constant_dynamic-update-slice_fusion.2.refs_0_), channel_id=1, source_target_pairs={{0,4},{2,6},{4,0},{6,2},{8,12},{10,14},{12,8},{14,10},{16,20},{18,... | collective-permute-start | bytes 1572872 | tf_op jit(solution)/shard_map/ppermute | solution.py:597
  89.9 13.8 %collective-permute-start.8 = (bf16[512,256]{1,0:T(8,128)(2,1)S(1)}, bf16[512,256]{1,0:T(8,128)(2,1)S(1)}, u32[]{:S(2)}, u32[]{:S(2)}) collective-permute-start(bf16[512,256]{1,0:T(8,128)(2,1)S(1)} %get-tuple-element.338), channel_id=1, source_target_pairs={{0,1},{1,0},{2,3},{3,2},{4,5},{5,4},{6,7},{7,6},{8,9},{9,8},{10,11... | collective-permute-start | bytes 786440 | tf_op jit(solution)/shard_map/ppermute | solution.py:580
  100.6 11.1 %collective-permute-start.9 = (bf16[256,1024]{1,0:T(8,128)(2,1)S(1)}, bf16[256,1024]{1,0:T(8,128)(2,1)S(1)}, u32[]{:S(2)}, u32[]{:S(2)}) collective-permute-start(bf16[256,1024]{1,0:T(8,128)(2,1)S(1)} %constant_dynamic-update-slice_fusion.2.refs_0_), channel_id=1, source_target_pairs={{0,2},{2,0},{4,6},{6,4},{8,10},{10,8},{12,14},{14,12},{16,18},{18,... | collective-permute-start | bytes 1572872 | tf_op jit(solution)/shard_map/ppermute | solution.py:597
  121.3 24.6 %collective-permute-start.11 = (bf16[512,1024]{1,0:T(8,128)(2,1)}, bf16[512,1024]{1,0:T(8,128)(2,1)S(1)}, u32[]{:S(2)}, u32[]{:S(2)}) collective-permute-start(bf16[512,1024]{1,0:T(8,128)(2,1)} %get-tuple-element.154.normed_ref.refs_0_), channel_id=1, source_target_pairs={{0,1},{1,0},{2,3},{3,2},{4,5},{5,4},{6,7},{7,6},{8,9},{9,8},{10,11... | collective-permute-start | bytes 3145736 | tf_op jit(solution)/shard_map/ppermute | solution.py:580
  162.4 34.4 %collective-permute-start.12 = (bf16[512,1024]{1,0:T(8,128)(2,1)}, bf16[512,1024]{1,0:T(8,128)(2,1)S(1)}, u32[]{:S(2)}, u32[]{:S(2)}) collective-permute-start(bf16[512,1024]{1,0:T(8,128)(2,1)} %get-tuple-element.151), channel_id=1, source_target_pairs={{0,1},{1,0},{2,3},{3,2},{4,5},{5,4},{6,7},{7,6},{8,9},{9,8},{10,11... | collective-permute-start | bytes 3145736 | tf_op jit(solution)/shard_map/ppermute | solution.py:580
  206.3 36.8 %collective-permute-start.14 = (bf16[512,1024]{1,0:T(8,128)(2,1)S(1)}, bf16[512,1024]{1,0:T(8,128)(2,1)S(1)}, u32[]{:S(2)}, u32[]{:S(2)}) collective-permute-start(bf16[512,1024]{1,0:T(8,128)(2,1)S(1)} %copy-done.35), channel_id=1, source_target_pairs={{0,1},{1,0},{2,3},{3,2},{4,5},{5,4},{6,7},{7,6},{8,9},{9,8},{10,11... | collective-permute-start | bytes 3145736 | tf_op jit(solution)/shard_map/ppermute | solution.py:580
  217.0 25.3 %collective-permute-start.15 = (bf16[512,256]{1,0:T(8,128)(2,1)}, bf16[512,256]{1,0:T(8,128)(2,1)S(1)}, u32[]{:S(2)}, u32[]{:S(2)}) collective-permute-start(bf16[512,256]{1,0:T(8,128)(2,1)} %get-tuple-element.178), channel_id=1, source_target_pairs={{0,1},{1,0},{2,3},{3,2},{4,5},{5,4},{6,7},{7,6},{8,9},{9,8},{10,11... | collective-permute-start | bytes 786440 | tf_op jit(solution)/shard_map/ppermute | solution.py:580
  258.4 31.8 %collective-permute-start.18 = (bf16[256,1792]{1,0:T(8,128)(2,1)S(1)}, bf16[256,1792]{1,0:T(8,128)(2,1)S(1)}, u32[]{:S(2)}, u32[]{:S(2)}) collective-permute-start(bf16[256,1792]{1,0:T(8,128)(2,1)S(1)} %add_convert_fusion.2), channel_id=1, source_target_pairs={{0,4},{2,6},{4,0},{6,2},{8,12},{10,14},{12,8},{14,10},{16,20},{18,... | collective-permute-start | bytes 2752520 | tf_op jit(solution)/shard_map/ppermute | solution.py:597
  282.1 25.6 %collective-permute-start.17 = (bf16[512,1024]{1,0:T(8,128)(2,1)}, bf16[512,1024]{1,0:T(8,128)(2,1)}, u32[]{:S(2)}, u32[]{:S(2)}) collective-permute-start(bf16[512,1024]{1,0:T(8,128)(2,1)} %product_back.2), channel_id=1, source_target_pairs={{0,1},{1,0},{2,3},{3,2},{4,5},{5,4},{6,7},{7,6},{8,9},{9,8},{10,11... | collective-permute-start | bytes 3145736 | tf_op jit(solution)/shard_map/ppermute | solution.py:580
  291.2 16.5 %collective-permute-start.19 = (bf16[512,768]{1,0:T(8,128)(2,1)}, bf16[512,768]{1,0:T(8,128)(2,1)S(1)}, u32[]{:S(2)}, u32[]{:S(2)}) collective-permute-start(bf16[512,768]{1,0:T(8,128)(2,1)} %get-tuple-element.199), channel_id=1, source_target_pairs={{0,2},{2,0},{4,6},{6,4},{8,10},{10,8},{12,14},{14,12},{16,18},{18,... | collective-permute-start | bytes 2359304 | tf_op jit(solution)/shard_map/ppermute | solution.py:597
  307.8 13.3 %collective-permute-start.20 = (bf16[256,768]{1,0:T(8,128)(2,1)S(1)}, bf16[256,768]{1,0:T(8,128)(2,1)}, u32[]{:S(2)}, u32[]{:S(2)}) collective-permute-start(bf16[256,768]{1,0:T(8,128)(2,1)S(1)} %add_convert_fusion.3), channel_id=1, source_target_pairs={{0,4},{2,6},{4,0},{6,2},{8,12},{10,14},{12,8},{14,10},{16,20},{18,... | collective-permute-start | bytes 1179656 | tf_op jit(solution)/shard_map/ppermute | solution.py:597
  310.4 23.3 %collective-permute-start.22 = (bf16[64,1792]{1,0:T(8,128)(2,1)}, bf16[64,1792]{1,0:T(8,128)(2,1)S(1)}, u32[]{:S(2)}, u32[]{:S(2)}) collective-permute-start(bf16[64,1792]{1,0:T(8,128)(2,1)} %get-tuple-element.329), channel_id=1, source_target_pairs={{0,8},{2,10},{4,12},{6,14},{8,16},{10,18},{12,20},{14,22},{16,24},... | collective-permute-start | bytes 688136 | tf_op jit(solution)/shard_map/ppermute | solution.py:597
  311.3 31.9 %collective-permute-start.23 = (bf16[64,1792]{1,0:T(8,128)(2,1)}, bf16[64,1792]{1,0:T(8,128)(2,1)}, u32[]{:S(2)}, u32[]{:S(2)}) collective-permute-start(bf16[64,1792]{1,0:T(8,128)(2,1)} %get-tuple-element.328), channel_id=1, source_target_pairs={{0,16},{2,18},{4,20},{6,22},{8,24},{10,26},{12,28},{14,30},{16,0},... | collective-permute-start | bytes 688136 | tf_op jit(solution)/shard_map/ppermute | solution.py:597
  312.5 30.7 %collective-permute-start.24 = (bf16[64,1792]{1,0:T(8,128)(2,1)}, bf16[64,1792]{1,0:T(8,128)(2,1)}, u32[]{:S(2)}, u32[]{:S(2)}) collective-permute-start(bf16[64,1792]{1,0:T(8,128)(2,1)} %get-tuple-element.327), channel_id=1, source_target_pairs={{0,24},{2,26},{4,28},{6,30},{8,0},{10,2},{12,4},{14,6},{16,8},{18,... | collective-permute-start | bytes 688136 | tf_op jit(solution)/shard_map/ppermute | solution.py:597
  324.4 18.8 %collective-permute-start.25 = (bf16[64,768]{1,0:T(8,128)(2,1)}, bf16[64,768]{1,0:T(8,128)(2,1)}, u32[]{:S(2)}, u32[]{:S(2)}) collective-permute-start(bf16[64,768]{1,0:T(8,128)(2,1)} %get-tuple-element.333), channel_id=1, source_target_pairs={{0,8},{2,10},{4,12},{6,14},{8,16},{10,18},{12,20},{14,22},{16,24},... | collective-permute-start | bytes 294920 | tf_op jit(solution)/shard_map/ppermute | solution.py:597
  327.1 16.1 %collective-permute-start.26 = (bf16[64,768]{1,0:T(8,128)(2,1)S(1)}, bf16[64,768]{1,0:T(8,128)(2,1)S(1)}, u32[]{:S(2)}, u32[]{:S(2)}) collective-permute-start(bf16[64,768]{1,0:T(8,128)(2,1)S(1)} %get-tuple-element.332), channel_id=1, source_target_pairs={{0,16},{2,18},{4,20},{6,22},{8,24},{10,26},{12,28},{14,30},{16,0},... | collective-permute-start | bytes 294920 | tf_op jit(solution)/shard_map/ppermute | solution.py:597
  329.2 13.9 %all-to-all-start.2 = ((f32[16,1,3072]{2,1,0:T(1,128)}), f32[16,1,3072]{2,1,0:T(1,128)S(1)}, u32[]{:S(2)}, u32[]{:S(2)}) async-start(f32[16,1,3072]{2,1,0:T(1,128)} %broadcast_in_dim.10), calls=%async_computation.3 | async-start | bytes 393216 | tf_op jit(solution)/shard_map/all_to_all | solution.py:709
  (52 other events, 414.4 us)
Sparse Core Ops, SparseCore 0:
  10.9 47.8 all-gather.2
  68.0 78.8 all-gather.4
  196.9 115.1 reduce-scatter.1

commit v4 on v3

--- a/solution.py
+++ b/solution.py
@@ -21,7 +21,9 @@
 
 
 def cost(flops, moved, raised=0):
-    return pl.CostEstimate(flops=int(flops), bytes_accessed=int(moved), transcendentals=int(raised))
+    return pl.CostEstimate(
+        flops=int(flops) // 4, bytes_accessed=int(moved) // 4, transcendentals=int(raised) // 4
+    )
 
 
 def resident(shape):
@@ -235,7 +237,46 @@
     )(triple, triple, triple)
 
 
-def attend_backward(triple, start, attended, level, grads, width):
+def probabilities(triple, start, level, width):
+    tokens = triple.shape[0]
+    pairs = width // PAIR
+    first = start // PAIR
+    block = min(512, tokens)
+    scaling = HEAD ** (-0.5)
+
+    def body(query_ref, keys_ref, level_ref, out_ref):
+        lane, heads = head_lanes()
+        keys = keys_ref[...]
+        query = query_ref[...].astype(FULL)
+        for index, (mask, free) in enumerate(heads):
+            own = HEAD * index
+            scores = lax.dot_general(
+                ones_in_lanes(lane, free, keys),
+                (
+                    query * (mask * scaling) - in_lanes(lane, free, level_ref[:, own : own + 1])
+                ).astype(LOW),
+                NT,
+                preferred_element_type=FULL,
+            )
+            out_ref[0, index] = jnp.exp(scores).astype(LOW)
+
+    return pl.pallas_call(
+        body,
+        grid=(pairs, tokens // block),
+        in_specs=[
+            pl.BlockSpec((block, PAIR), lambda h, i: (i, first + h)),
+            pl.BlockSpec((tokens, PAIR), lambda h, i: (0, first + pairs + h)),
+            pl.BlockSpec((block, PAIR), lambda h, i: (i, h)),
+        ],
+        out_specs=pl.BlockSpec((1, 2, tokens, block), lambda h, i: (h, 0, 0, i)),
+        out_shape=jax.ShapeDtypeStruct((pairs, 2, tokens, tokens), LOW),
+        compiler_params=params(),
+        cost_estimate=cost(4 * tokens * tokens * width, 4 * pairs * tokens * tokens, tokens * tokens * width // HEAD),
+        name="probabilities",
+    )(triple, triple, level)
+
+
+def attend_backward(triple, start, attended, probs, grads, width):
     tokens = triple.shape[0]
     pairs = width // PAIR
     first = start // PAIR
@@ -243,7 +284,7 @@
     steps = tokens // block
     scaling = HEAD ** (-0.5)
 
-    def body(query_ref, keys_ref, values_ref, out_low_ref, level_ref, grad_ref, out_ref, key_sum, value_sum):
+    def body(query_ref, keys_ref, values_ref, out_low_ref, probs_ref, grad_ref, out_ref, key_sum, value_sum):
         pair = pl.program_id(0)
         step = pl.program_id(1)
         lane, heads = head_lanes()
@@ -254,17 +295,9 @@
         inner = grad * out_low_ref[...].astype(FULL)
         query_grad = key_grad = value_grad = None
         for index, (mask, free) in enumerate(heads):
-            own = HEAD * index
-            query_part = query * (mask * scaling)
+            query_part = (query * (mask * scaling)).astype(LOW)
             grad_part = grad * mask
-            probs = jnp.exp(
-                lax.dot_general(
-                    ones_in_lanes(lane, free, keys),
-                    (query_part - in_lanes(lane, free, level_ref[:, own : own + 1])).astype(LOW),
-                    NT,
-                    preferred_element_type=FULL,
-                )
-            )
+            probs = probs_ref[0, index]
             prob_grad = lax.dot_general(
                 ones_in_lanes(lane, free, values),
                 (
@@ -273,9 +306,9 @@
                 NT,
                 preferred_element_type=FULL,
             )
-            score_grad = (probs * prob_grad).astype(LOW)
-            value_part = jnp.dot(probs.astype(LOW), grad_part.astype(LOW), preferred_element_type=FULL)
-            key_part = jnp.dot(score_grad, query_part.astype(LOW), preferred_element_type=FULL)
+            score_grad = (probs.astype(FULL) * prob_grad).astype(LOW)
+            value_part = jnp.dot(probs, grad_part.astype(LOW), preferred_element_type=FULL)
+            key_part = jnp.dot(score_grad, query_part, preferred_element_type=FULL)
             asked_part = lax.dot_general(
                 score_grad, keys * (mask * scaling).astype(LOW), TN, preferred_element_type=FULL
             )
@@ -317,16 +350,16 @@
             pl.BlockSpec((tokens, PAIR), lambda h, i: (0, first + pairs + h)),
             pl.BlockSpec((tokens, PAIR), lambda h, i: (0, first + 2 * pairs + h)),
             rows_of_pair,
-            rows_of_pair,
+            pl.BlockSpec((1, 2, tokens, block), lambda h, i: (h, 0, 0, i)),
             rows_of_pair,
         ],
         out_specs=resident((tokens, 3 * width)),
         out_shape=jax.ShapeDtypeStruct((tokens, 3 * width), LOW),
         scratch_shapes=[pltpu.VMEM((tokens, PAIR), FULL), pltpu.VMEM((tokens, PAIR), FULL)],
         compiler_params=params(),
-        cost_estimate=cost(40 * tokens * tokens * width, 20 * tokens * width, tokens * tokens * width // HEAD),
+        cost_estimate=cost(32 * tokens * tokens * width, 20 * tokens * width + 4 * pairs * tokens * tokens),
         name="attend_backward",
-    )(triple, triple, triple, attended, level, grads)
+    )(triple, triple, triple, attended, probs, grads)
 
 
 def feed_both(normed, branch_grad, weights, out_type):
@@ -817,6 +850,11 @@
     )
     normed_two_blocks = blocks_of_tokens(normed_two)
 
+    mixes = [
+        (mixed, probabilities(triple, 3 * start, level, end - start))
+        for (mixed, level), (start, end) in zip(mixes, spans)
+    ]
+    normed_two_blocks, mixes = together(normed_two_blocks, mixes)
     fed = [None] + [feed_both(normed_two_blocks[k], branch_grad_blocks[k], feed_whole, LOW) for k in others]
     back_parts = [shift_tp(fed[k][1], k, tp_count) for k in others]
     normed_two, fed = together(normed_two, fed)
@@ -848,7 +886,7 @@
     triple_grads = [
         attend_backward(triple, 0, *mixes[0], attended_grads[0], spans[0][1])
     ]
-    triple_grads, branch_parts, attended_grads = together(triple_grads, branch_parts, attended_grads)
+    triple_grads, branch_parts = together(triple_grads, branch_parts)
     pair = token_sum([([attn_grad], [attended_own]), ([normed_one], triple_grads)], fsdp_count)
     state = scatter_core(pair, fsdp_count)
     block_out, last_sums = last_forward(fed[0][0], branch_parts, after_attn, cotangent, gate_two)

time: 364 us -> 367 us (level)
  Pallas kernels: 165 us -> 176 us
  starting transfers between devices: 52.8 us -> 46.5 us
    pallas_call x0 -> x2, Pallas kernels: none -> 14.4 us  [probabilities(): pl.pallas_call(body, grid=(pairs, tokens // block), in_specs=[pl.BlockSpe...]
    ppermute x13, waiting for transfers between devices: 60.2 us -> 51.3 us  [shift_tp(): lax.ppermute(values, 'tp', [(i, (i + steps) % count) for i in range(count)])]
    pallas_call x2, Pallas kernels: 35.1 us -> 30.7 us  [attend_backward(): pl.pallas_call(body, grid=(pairs, steps), in_specs=[pl.BlockSpec((block,...]
    unnamed x87 -> x93, local copies, waits for them, and re-layouts: 7.57 us -> 8.55 us
  transfers between devices with their start and end apart: 35 -> 35, of which waited for: 14 -> 15; matrix products, arithmetic and copies ran while one was open for 9% -> 10% of each run, Pallas kernels for 42% -> 44%
where the time goes in v4:
time: 367 us; the launch traced here: 362 us
  Pallas kernels  176 us (48%)
  waiting for transfers between devices  76.4 us (21%)
  starting transfers between devices  46.5 us (13%)
  other arithmetic  27 us (7%)
  local copies, waits for them, and re-layouts  14.8 us (4%)
  between operations  14.7 us (4%)
  blocking collectives  4.42 us (1%)
    ppermute x13, waiting for transfers between devices, shift_tp(): lax.ppermute(values, 'tp', [(i, (i + steps) % count) for i in range(count)])  51.3 us
    pallas_call x3, Pallas kernels, token_sum(): pl.pallas_call(body, grid=(width // tile,), in_specs=in_specs, out_specs=...  32.5 us
    pallas_call x2, Pallas kernels, feed_both(): pl.pallas_call(body, grid=(steps,), in_specs=[resident((tokens, depth)),...  32 us
    pallas_call x2, Pallas kernels, attend_backward(): pl.pallas_call(body, grid=(pairs, steps), in_specs=[pl.BlockSpec((block,...  30.7 us
    pallas_call x4, Pallas kernels, by_tokens(): pl.pallas_call(body, grid=(tokens // block,), in_specs=[cut(value.shape)...  24.9 us
    pallas_call x2, Pallas kernels, attend_forward(): pl.pallas_call(body, grid=(pairs, tokens // block), in_specs=[pl.BlockSpe...  19.9 us
    ppermute x16, starting transfers between devices, shift_fsdp(): return lax.ppermute(values, 'fsdp', pairs)  16.9 us
    ppermute x13, starting transfers between devices, shift_tp(): lax.ppermute(values, 'tp', [(i, (i + steps) % count) for i in range(count)])  15.4 us
  transfers between devices with their start and end apart: 35, of which 15 were waited for; matrix products, arithmetic and copies ran while one was open for 10% of the time, Pallas kernels for 44%

profile of v4, /device:TPU:0, one launch (start us, length us, event | category | flops | bytes accessed | tf_op | source)
XLA Modules:
  0.0 362.0 jit_solution(3330917262208051193)
XLA Ops:
  17.3 5.9 %all-to-all-start = ((bf16[16,1,64]{2,1,0:T(2,128)(2,1)}), bf16[16,1,64]{2,1,0:T(2,128)(2,1)S(1)}, u32[]{:S(2)}, u32[]{:S(2)}) async-start(bf16[16,1,64]{2,1,0:T(2,128)(2,1)} %all_to_all.30), calls=%async_computation | async-start | bytes 16384 | tf_op jit(solution)/shard_map/all_to_all | solution.py:796
  35.0 8.1 %all-to-all-done.1 = f32[16,1,3072]{2,1,0:T(1,128)S(1)} async-done(((f32[16,1,3072]{2,1,0:T(1,128)}), f32[16,1,3072]{2,1,0:T(1,128)S(1)}, u32[]{:S(2)}, u32[]{:S(2)}) %all-to-all-start.1) | async-done | bytes 196640 | tf_op jit(solution)/shard_map/all_to_all | solution.py:809
  69.5 7.1 %product.1.query_ref.keys_ref.values_ref = bf16[1024,1536]{1,0:T(8,128)(2,1)} custom-call(bf16[1024,1024]{1,0:T(8,128)(2,1)} %pad_maximum_fusion.left_ref.refs_2_.refs_0_, bf16[1024,1536]{1,0:T(8,128)(2,1)} %all-gather.3.cloned.1.call-done.right_ref.refs_2_), custom_call_target="tpu_custom_call" | custom-call | flops 805306368 | bytes 2883584 | tf_op jit(solution)/shard_map/product/pallas_call | solution.py:47
  77.1 10.0 %attend_forward.3 = (bf16[1024,256]{1,0:T(8,128)(2,1)}, f32[1024,256]{1,0:T(8,128)}) custom-call(bf16[1024,1536]{1,0:T(8,128)(2,1)} %product.1.query_ref.keys_ref.values_ref, bf16[1024,1536]{1,0:T(8,128)(2,1)} %product.1.query_ref.keys_ref.values_ref, bf16[1024,1536]{1,0:T(8,128)(2,1)} %product.1.query_ref.keys_ref.values_ref), custom_call_target="tpu_custom_call" | custom-call | flops 1073741824 | bytes 786432 | tf_op jit(solution)/shard_map/attend_forward/pallas_call | solution.py:221
  88.7 9.9 %attend_forward.2 = (bf16[1024,256]{1,0:T(8,128)(2,1)}, f32[1024,256]{1,0:T(8,128)}) custom-call(bf16[1024,1536]{1,0:T(8,128)(2,1)} %product.1.query_ref.keys_ref.values_ref, bf16[1024,1536]{1,0:T(8,128)(2,1)} %product.1.query_ref.keys_ref.values_ref, bf16[1024,1536]{1,0:T(8,128)(2,1)} %product.1.query_ref.keys_ref.values_ref), custom_call_target="tpu_custom_call" | custom-call | flops 1073741824 | bytes 786432 | tf_op jit(solution)/shard_map/attend_forward/pallas_call | solution.py:221
  101.9 6.8 %collective-permute-done.7 = bf16[512,256]{1,0:T(8,128)(2,1)S(1)} collective-permute-done((bf16[512,256]{1,0:T(8,128)(2,1)S(1)}, bf16[512,256]{1,0:T(8,128)(2,1)S(1)}, u32[]{:S(2)}, u32[]{:S(2)}) %collective-permute-start.7) | collective-permute-done | bytes 262176 | tf_op jit(solution)/shard_map/ppermute | solution.py:613
  114.1 5.4 %merge_and_normalize.1 = (f32[512,1024]{1,0:T(8,128)}, f32[512,1024]{1,0:T(8,128)}, bf16[512,1024]{1,0:T(8,128)(2,1)}) custom-call(bf16[512,1024]{1,0:T(8,128)(2,1)} %pad_maximum_fusion.1.attended_ref.refs_1_, f32[512,1024]{1,0:T(8,128)} %bitcast.83, bf16[1024,1024]{1,0:T(8,128)(2,1)} %arrange.1.merge_ref.refs_5_, ...), custom_call_target="tpu_custom_call" | custom-call | flops 268435456 | bytes 2624512 | tf_op jit(solution)/shard_map/merge_and_normalize/pallas_call | solution.py:479
  120.9 7.2 %probabilities.2.probs_ref = bf16[2,2,1024,1024]{3,2,1,0:T(8,128)(2,1)} custom-call(bf16[1024,1536]{1,0:T(8,128)(2,1)} %product.1.query_ref.keys_ref.values_ref, bf16[1024,1536]{1,0:T(8,128)(2,1)} %product.1.query_ref.keys_ref.values_ref, f32[1024,256]{1,0:T(8,128)} %get-tuple-element.152.level_ref), custom_call_target="tpu_custom_call" | custom-call | flops 268435456 | bytes 2097152 | tf_op jit(solution)/shard_map/probabilities/pallas_call | solution.py:263
  128.1 7.2 %probabilities.3.probs_ref = bf16[2,2,1024,1024]{3,2,1,0:T(8,128)(2,1)} custom-call(bf16[1024,1536]{1,0:T(8,128)(2,1)} %product.1.query_ref.keys_ref.values_ref, bf16[1024,1536]{1,0:T(8,128)(2,1)} %product.1.query_ref.keys_ref.values_ref, f32[1024,256]{1,0:T(8,128)} %get-tuple-element.153.level_ref), custom_call_target="tpu_custom_call" | custom-call | flops 268435456 | bytes 2097152 | tf_op jit(solution)/shard_map/probabilities/pallas_call | solution.py:263
  135.3 8.8 %collective-permute-done.11.normed_ref.refs_1_ = bf16[512,1024]{1,0:T(8,128)(2,1)S(1)} collective-permute-done((bf16[512,1024]{1,0:T(8,128)(2,1)}, bf16[512,1024]{1,0:T(8,128)(2,1)S(1)}, u32[]{:S(2)}, u32[]{:S(2)}) %collective-permute-start.11) | collective-permute-done | bytes 1048608 | tf_op jit(solution)/shard_map/ppermute | solution.py:613
  145.1 15.5 %feed_both.2 = (bf16[512,1024]{1,0:T(8,128)(2,1)}, bf16[512,1024]{1,0:T(8,128)(2,1)}, bf16[512,2048]{1,0:T(8,128)(2,1)}, bf16[512,2048]{1,0:T(8,128)(2,1)}) custom-call(bf16[512,1024]{1,0:T(8,128)(2,1)} %copy-done.4, bf16[512,1024]{1,0:T(8,128)(2,1)} %copy-done.3, bf16[1024,4096]{1,0:T(8,128)(2,1)} %all-gather.5.cloned.1.call-done.up_ref.down_ref, ...), custom_call_target="tpu_custom_call" | custom-call | flops 2147483648 | bytes 4718592 | tf_op jit(solution)/shard_map/feed_both/pallas_call | solution.py:405
  162.2 16.4 %feed_both.3 = (f32[512,1024]{1,0:T(8,128)}, f32[512,1024]{1,0:T(8,128)}, bf16[512,2048]{1,0:T(8,128)(2,1)}, bf16[512,2048]{1,0:T(8,128)(2,1)}) custom-call(bf16[512,1024]{1,0:T(8,128)(2,1)} %get-tuple-element.170.normed_ref.refs_0_, bf16[512,1024]{1,0:T(8,128)(2,1)} %copy-done.2, bf16[1024,4096]{1,0:T(8,128)(2,1)} %all-gather.5.cloned.1.call-done.up_ref.down_ref, ...), custom_call_target="tpu_custom_call" | custom-call | flops 2147483648 | bytes 4718592 | tf_op jit(solution)/shard_map/feed_both/pallas_call | solution.py:405
  178.6 16.4 %token_sum.3 = bf16[1024,4096]{1,0:T(8,128)(2,1)} custom-call(bf16[512,1024]{1,0:T(8,128)(2,1)} %get-tuple-element.170.normed_ref.refs_0_, bf16[512,1024]{1,0:T(8,128)(2,1)} %copy-done.4, bf16[512,2048]{1,0:T(8,128)(2,1)} %get-tuple-element.171.refs_2_, bf16[512,2048]{1,0:T(8,128)(2,1)} %get-tuple-element.172.refs_3_, bf16[512,1024]{1,0:T(8,128)(2,1)} %copy-done.2, ...), custom_call_target="tpu_custom_call" | custom-call | flops 2147483648 | bytes 5242880 | tf_op jit(solution)/shard_map/token_sum/pallas_call | solution.py:160
  197.2 7.9 %second_back.1 = (f32[512,1024]{1,0:T(8,128)}, bf16[512,1024]{1,0:T(8,128)(2,1)}, bf16[512,256]{1,0:T(8,128)(2,1)}, bf16[512,256]{1,0:T(8,128)(2,1)}, bf16[512,2...) custom-call(f32[512,1024]{1,0:T(8,128)} %get-tuple-element.169.refs_0_, bf16[512,1024]{1,0:T(8,128)(2,1)} %copy-done.15, ...), custom_call_target="tpu_custom_call" | custom-call | flops 268435456 | bytes 3942400 | tf_op jit(solution)/shard_map/second_back/pallas_call | solution.py:479
  206.6 20.7 %collective-permute-done.13 = bf16[512,256]{1,0:T(8,128)(2,1)S(1)} collective-permute-done((bf16[512,256]{1,0:T(8,128)(2,1)}, bf16[512,256]{1,0:T(8,128)(2,1)S(1)}, u32[]{:S(2)}, u32[]{:S(2)}) %collective-permute-start.13) | collective-permute-done | bytes 262176 | tf_op jit(solution)/shard_map/ppermute | solution.py:613
  229.1 15.3 %attend_backward.2.refs_3_.refs_0_ = bf16[1024,768]{1,0:T(8,128)(2,1)} custom-call(bf16[1024,1536]{1,0:T(8,128)(2,1)} %product.1.query_ref.keys_ref.values_ref, bf16[1024,1536]{1,0:T(8,128)(2,1)} %product.1.query_ref.keys_ref.values_ref, bf16[1024,1536]{1,0:T(8,128)(2,1)} %product.1.query_ref.keys_ref.values_ref, ...), custom_call_target="tpu_custom_call" | custom-call | flops 2147483648 | bytes 3407872 | tf_op jit(solution)/shard_map/attend_backward/pallas_call | solution.py:345
  244.4 10.1 %token_sum.4 = (bf16[512,1792]{1,0:T(8,128)(2,1)}, bf16[512,1792]{1,0:T(8,128)(2,1)}) custom-call(bf16[512,1024]{1,0:T(8,128)(2,1)} %get-tuple-element.186.refs_0_, bf16[512,1024]{1,0:T(8,128)(2,1)} %pad_maximum_fusion.1.attended_ref.refs_1_, bf16[1024,1024]{1,0:T(8,128)(2,1)} %pad_maximum_fusion.left_ref.refs_2_.refs_0_, ...), custom_call_target="tpu_custom_call" | custom-call | flops 939524096 | bytes 2883584 | tf_op jit(solution)/shard_map/token_sum/pallas_call | solution.py:160
  255.3 5.4 %last_forward.1 = (f32[512,8,128]{2,1,0:T(8,128)}, f32[8,1024]{1,0:T(8,128)}) custom-call(f32[512,1024]{1,0:T(8,128)} %get-tuple-element.193.refs_0_, bf16[512,1024]{1,0:T(8,128)(2,1)} %copy-done.14, f32[512,1024]{1,0:T(8,128)} %get-tuple-element.177.refs_2_, f32[512,1024]{1,0:T(8,128)} %bitcast.86, f32[1,1024]{1,0:T(1,128)} %copy-done.36), custom_call_target="tpu_custom_call" | custom-call | flops 786432 | bytes 2368512 | tf_op jit(solution)/shard_map/last_forward/pallas_call | solution.py:479
  265.1 15.4 %attend_backward.3.refs_1_ = bf16[1024,768]{1,0:T(8,128)(2,1)} custom-call(bf16[1024,1536]{1,0:T(8,128)(2,1)} %product.1.query_ref.keys_ref.values_ref, bf16[1024,1536]{1,0:T(8,128)(2,1)} %product.1.query_ref.keys_ref.values_ref, bf16[1024,1536]{1,0:T(8,128)(2,1)} %product.1.query_ref.keys_ref.values_ref, bf16[1024,256]{1,0:T(8,128)(2,1)} %get-tuple-element.197.out_low_ref, ...), custom_call_target="tpu_custom_call" | custom-call | flops 2147483648 | bytes 3407872 | tf_op jit(solution)/shard_map/attend_backward/pallas_call | solution.py:345
  280.5 5.8 %product_back.2 = bf16[512,1024]{1,0:T(8,128)(2,1)} custom-call(bf16[1024,768]{1,0:T(8,128)(2,1)} %attend_backward.2.refs_3_.refs_0_, bf16[1024,768]{1,0:T(8,128)(2,1)} %attend_backward.3.refs_1_, bf16[1024,1536]{1,0:T(8,128)(2,1)} %all-gather.3.cloned.1.call-done.right_ref.refs_2_), custom_call_target="tpu_custom_call" | custom-call | flops 402653184 | bytes 1703936 | tf_op jit(solution)/shard_map/product_back/pallas_call | solution.py:78
  286.7 6.0 %token_sum.5 = (bf16[512,768]{1,0:T(8,128)(2,1)}, bf16[512,768]{1,0:T(8,128)(2,1)}) custom-call(bf16[1024,1024]{1,0:T(8,128)(2,1)} %pad_maximum_fusion.left_ref.refs_2_.refs_0_, bf16[1024,768]{1,0:T(8,128)(2,1)} %attend_backward.3.refs_1_), custom_call_target="tpu_custom_call" | custom-call | flops 402653184 | bytes 1310720 | tf_op jit(solution)/shard_map/token_sum/pallas_call | solution.py:160
  294.4 5.9 %product_back.3.refs_0_ = f32[512,1024]{1,0:T(8,128)} custom-call(bf16[1024,768]{1,0:T(8,128)(2,1)} %attend_backward.2.refs_3_.refs_0_, bf16[1024,768]{1,0:T(8,128)(2,1)} %attend_backward.3.refs_1_, bf16[1024,1536]{1,0:T(8,128)(2,1)} %all-gather.3.cloned.1.call-done.right_ref.refs_2_), custom_call_target="tpu_custom_call" | custom-call | flops 402653184 | bytes 1703936 | tf_op jit(solution)/shard_map/product_back/pallas_call | solution.py:78
  300.3 10.7 %collective-permute-done.17.refs_1_ = bf16[512,1024]{1,0:T(8,128)(2,1)} collective-permute-done((bf16[512,1024]{1,0:T(8,128)(2,1)}, bf16[512,1024]{1,0:T(8,128)(2,1)}, u32[]{:S(2)}, u32[]{:S(2)}) %collective-permute-start.17) | collective-permute-done | bytes 1048608 | tf_op jit(solution)/shard_map/ppermute | solution.py:613
  318.2 6.2 %first_back.1 = (f32[512,8,128]{2,1,0:T(8,128)}, f32[8,1024]{1,0:T(8,128)}) custom-call(f32[512,1024]{1,0:T(8,128)} %product_back.3.refs_0_, bf16[512,1024]{1,0:T(8,128)(2,1)} %collective-permute-done.17.refs_1_, f32[512,1024]{1,0:T(8,128)} %bitcast.84, f32[512,1024]{1,0:T(8,128)} %get-tuple-element.212.refs_3_, f32[1,1024]{1,0:T(1,128)} %get-tuple-element.351.refs_4_), custom_call_target="tpu_custom_call" | custom-call | flops 2621440 | bytes 2368512 | tf_op jit(solution)/shard_map/first_back/pallas_call | solution.py:479
  (223 shorter events, 113.2 us)
Async XLA Ops:
  7.2 60.0 %all-gather.3.cloned.1.call-start = ((), (), s32[]{:S(2)}) async-start(), calls=%async_computation.4 | async-start | bytes 3342336 | tf_op jit(solution)/shard_map/all_gather | solution.py:722
  13.6 29.5 %collective-permute-start = (bf16[512,1024]{1,0:T(8,128)(2,1)}, bf16[512,1024]{1,0:T(8,128)(2,1)}, u32[]{:S(2)}, u32[]{:S(2)}) collective-permute-start(bf16[512,1024]{1,0:T(8,128)(2,1)} %multiply_convert_fusion.1), channel_id=1, source_target_pairs={{0,1},{1,0},{2,3},{3,2},{4,5},{5,4},{6,7},{7,6},{8,9},{9,8},{10,11... | collective-permute-start | bytes 3145736 | tf_op jit(solution)/shard_map/ppermute | solution.py:613
  30.6 12.5 %all-to-all-start.1 = ((f32[16,1,3072]{2,1,0:T(1,128)}), f32[16,1,3072]{2,1,0:T(1,128)S(1)}, u32[]{:S(2)}, u32[]{:S(2)}) async-start(f32[16,1,3072]{2,1,0:T(1,128)} %copy.88), calls=%async_computation.1 | async-start | bytes 393216 | tf_op jit(solution)/shard_map/all_to_all | solution.py:809
  34.1 111.0 %all-gather.5.cloned.1.call-start = ((), (), s32[]{:S(2)}) async-start(), calls=%async_computation.5 | async-start | bytes 8912896 | tf_op jit(solution)/shard_map/all_gather | solution.py:722
  51.9 14.6 %collective-permute-start.3 = (bf16[64,1024]{1,0:T(8,128)(2,1)S(1)}, bf16[64,1024]{1,0:T(8,128)(2,1)S(1)}, u32[]{:S(2)}, u32[]{:S(2)}) collective-permute-start(bf16[64,1024]{1,0:T(8,128)(2,1)S(1)} %constant_dynamic-update-slice_fusion), channel_id=1, source_target_pairs={{0,16},{2,18},{4,20},{6,22},{8,24},{10,26},{12,28},{14,30},{16,0},... | collective-permute-start | bytes 393224 | tf_op jit(solution)/shard_map/ppermute | solution.py:630
  53.3 13.2 %collective-permute-start.4 = (bf16[64,1024]{1,0:T(8,128)(2,1)S(1)}, bf16[64,1024]{1,0:T(8,128)(2,1)S(1)}, u32[]{:S(2)}, u32[]{:S(2)}) collective-permute-start(bf16[64,1024]{1,0:T(8,128)(2,1)S(1)} %constant_dynamic-update-slice_fusion), channel_id=1, source_target_pairs={{0,24},{2,26},{4,28},{6,30},{8,0},{10,2},{12,4},{14,6},{16,8},{18,... | collective-permute-start | bytes 393224 | tf_op jit(solution)/shard_map/ppermute | solution.py:630
  67.2 257.2 %reduce-scatter.2.cloned.1.call-start = ((), (), s32[]{:S(2)}) async-start(), calls=%async_computation.6 | async-start | bytes 8912896 | tf_op jit(solution)/shard_map/reduce_scatter | solution.py:726
  67.8 30.9 %collective-permute-start.6 = (bf16[512,1024]{1,0:T(8,128)(2,1)S(1)}, bf16[512,1024]{1,0:T(8,128)(2,1)S(1)}, u32[]{:S(2)}, u32[]{:S(2)}) collective-permute-start(bf16[512,1024]{1,0:T(8,128)(2,1)S(1)} %multiply_convert_fusion.grad_ref.refs_4_), channel_id=1, source_target_pairs={{0,1},{1,0},{2,3},{3,2},{4,5},{5,4},{6,7},{7,6},{8,9},{9,8},{10,11... | collective-permute-start | bytes 3145736 | tf_op jit(solution)/shard_map/ppermute | solution.py:613
  76.7 22.0 %collective-permute-start.5 = (bf16[256,1024]{1,0:T(8,128)(2,1)S(1)}, bf16[256,1024]{1,0:T(8,128)(2,1)S(1)}, u32[]{:S(2)}, u32[]{:S(2)}) collective-permute-start(bf16[256,1024]{1,0:T(8,128)(2,1)S(1)} %constant_dynamic-update-slice_fusion.2.refs_0_), channel_id=1, source_target_pairs={{0,4},{2,6},{4,0},{6,2},{8,12},{10,14},{12,8},{14,10},{16,20},{18,... | collective-permute-start | bytes 1572872 | tf_op jit(solution)/shard_map/ppermute | solution.py:630
  88.1 13.8 %collective-permute-start.8 = (bf16[512,256]{1,0:T(8,128)(2,1)S(1)}, bf16[512,256]{1,0:T(8,128)(2,1)S(1)}, u32[]{:S(2)}, u32[]{:S(2)}) collective-permute-start(bf16[512,256]{1,0:T(8,128)(2,1)S(1)} %get-tuple-element.348), channel_id=1, source_target_pairs={{0,1},{1,0},{2,3},{3,2},{4,5},{5,4},{6,7},{7,6},{8,9},{9,8},{10,11... | collective-permute-start | bytes 786440 | tf_op jit(solution)/shard_map/ppermute | solution.py:613
  119.5 24.6 %collective-permute-start.11 = (bf16[512,1024]{1,0:T(8,128)(2,1)}, bf16[512,1024]{1,0:T(8,128)(2,1)S(1)}, u32[]{:S(2)}, u32[]{:S(2)}) collective-permute-start(bf16[512,1024]{1,0:T(8,128)(2,1)} %get-tuple-element.170.normed_ref.refs_0_), channel_id=1, source_target_pairs={{0,1},{1,0},{2,3},{3,2},{4,5},{5,4},{6,7},{7,6},{8,9},{9,8},{10,11... | collective-permute-start | bytes 3145736 | tf_op jit(solution)/shard_map/ppermute | solution.py:613
  160.7 34.4 %collective-permute-start.12 = (bf16[512,1024]{1,0:T(8,128)(2,1)}, bf16[512,1024]{1,0:T(8,128)(2,1)S(1)}, u32[]{:S(2)}, u32[]{:S(2)}) collective-permute-start(bf16[512,1024]{1,0:T(8,128)(2,1)} %get-tuple-element.158), channel_id=1, source_target_pairs={{0,1},{1,0},{2,3},{3,2},{4,5},{5,4},{6,7},{7,6},{8,9},{9,8},{10,11... | collective-permute-start | bytes 3145736 | tf_op jit(solution)/shard_map/ppermute | solution.py:613
  196.6 47.8 %collective-permute-start.15 = (bf16[512,1024]{1,0:T(8,128)(2,1)S(1)}, bf16[512,1024]{1,0:T(8,128)(2,1)S(1)}, u32[]{:S(2)}, u32[]{:S(2)}) collective-permute-start(bf16[512,1024]{1,0:T(8,128)(2,1)S(1)} %copy-done.38), channel_id=1, source_target_pairs={{0,1},{1,0},{2,3},{3,2},{4,5},{5,4},{6,7},{7,6},{8,9},{9,8},{10,11... | collective-permute-start | bytes 3145736 | tf_op jit(solution)/shard_map/ppermute | solution.py:613
  205.1 22.2 %collective-permute-start.13 = (bf16[512,256]{1,0:T(8,128)(2,1)}, bf16[512,256]{1,0:T(8,128)(2,1)S(1)}, u32[]{:S(2)}, u32[]{:S(2)}) collective-permute-start(bf16[512,256]{1,0:T(8,128)(2,1)} %get-tuple-element.180), channel_id=1, source_target_pairs={{0,1},{1,0},{2,3},{3,2},{4,5},{5,4},{6,7},{7,6},{8,9},{9,8},{10,11... | collective-permute-start | bytes 786440 | tf_op jit(solution)/shard_map/ppermute | solution.py:613
  264.4 28.3 %collective-permute-start.18 = (bf16[256,1792]{1,0:T(8,128)(2,1)S(1)}, bf16[256,1792]{1,0:T(8,128)(2,1)S(1)}, u32[]{:S(2)}, u32[]{:S(2)}) collective-permute-start(bf16[256,1792]{1,0:T(8,128)(2,1)S(1)} %add_convert_fusion.2), channel_id=1, source_target_pairs={{0,4},{2,6},{4,0},{6,2},{8,12},{10,14},{12,8},{14,10},{16,20},{18,... | collective-permute-start | bytes 2752520 | tf_op jit(solution)/shard_map/ppermute | solution.py:630
  286.3 24.7 %collective-permute-start.17 = (bf16[512,1024]{1,0:T(8,128)(2,1)}, bf16[512,1024]{1,0:T(8,128)(2,1)}, u32[]{:S(2)}, u32[]{:S(2)}) collective-permute-start(bf16[512,1024]{1,0:T(8,128)(2,1)} %product_back.2), channel_id=1, source_target_pairs={{0,1},{1,0},{2,3},{3,2},{4,5},{5,4},{6,7},{7,6},{8,9},{9,8},{10,11... | collective-permute-start | bytes 3145736 | tf_op jit(solution)/shard_map/ppermute | solution.py:613
  293.6 17.3 %collective-permute-start.19 = (bf16[512,768]{1,0:T(8,128)(2,1)}, bf16[512,768]{1,0:T(8,128)(2,1)S(1)}, u32[]{:S(2)}, u32[]{:S(2)}) collective-permute-start(bf16[512,768]{1,0:T(8,128)(2,1)} %get-tuple-element.209), channel_id=1, source_target_pairs={{0,2},{2,0},{4,6},{6,4},{8,10},{10,8},{12,14},{14,12},{16,18},{18,... | collective-permute-start | bytes 2359304 | tf_op jit(solution)/shard_map/ppermute | solution.py:630
  311.1 13.3 %collective-permute-start.20 = (bf16[256,768]{1,0:T(8,128)(2,1)S(1)}, bf16[256,768]{1,0:T(8,128)(2,1)}, u32[]{:S(2)}, u32[]{:S(2)}) collective-permute-start(bf16[256,768]{1,0:T(8,128)(2,1)S(1)} %add_convert_fusion.3), channel_id=1, source_target_pairs={{0,4},{2,6},{4,0},{6,2},{8,12},{10,14},{12,8},{14,10},{16,20},{18,... | collective-permute-start | bytes 1179656 | tf_op jit(solution)/shard_map/ppermute | solution.py:630
  313.6 24.0 %collective-permute-start.22 = (bf16[64,1792]{1,0:T(8,128)(2,1)}, bf16[64,1792]{1,0:T(8,128)(2,1)S(1)}, u32[]{:S(2)}, u32[]{:S(2)}) collective-permute-start(bf16[64,1792]{1,0:T(8,128)(2,1)} %get-tuple-element.339), channel_id=1, source_target_pairs={{0,8},{2,10},{4,12},{6,14},{8,16},{10,18},{12,20},{14,22},{16,24},... | collective-permute-start | bytes 688136 | tf_op jit(solution)/shard_map/ppermute | solution.py:630
  314.6 32.6 %collective-permute-start.23 = (bf16[64,1792]{1,0:T(8,128)(2,1)}, bf16[64,1792]{1,0:T(8,128)(2,1)}, u32[]{:S(2)}, u32[]{:S(2)}) collective-permute-start(bf16[64,1792]{1,0:T(8,128)(2,1)} %get-tuple-element.338), channel_id=1, source_target_pairs={{0,16},{2,18},{4,20},{6,22},{8,24},{10,26},{12,28},{14,30},{16,0},... | collective-permute-start | bytes 688136 | tf_op jit(solution)/shard_map/ppermute | solution.py:630
  315.8 31.4 %collective-permute-start.24 = (bf16[64,1792]{1,0:T(8,128)(2,1)}, bf16[64,1792]{1,0:T(8,128)(2,1)}, u32[]{:S(2)}, u32[]{:S(2)}) collective-permute-start(bf16[64,1792]{1,0:T(8,128)(2,1)} %get-tuple-element.337), channel_id=1, source_target_pairs={{0,24},{2,26},{4,28},{6,30},{8,0},{10,2},{12,4},{14,6},{16,8},{18,... | collective-permute-start | bytes 688136 | tf_op jit(solution)/shard_map/ppermute | solution.py:630
  326.4 20.8 %collective-permute-start.25 = (bf16[64,768]{1,0:T(8,128)(2,1)}, bf16[64,768]{1,0:T(8,128)(2,1)}, u32[]{:S(2)}, u32[]{:S(2)}) collective-permute-start(bf16[64,768]{1,0:T(8,128)(2,1)} %get-tuple-element.343), channel_id=1, source_target_pairs={{0,8},{2,10},{4,12},{6,14},{8,16},{10,18},{12,20},{14,22},{16,24},... | collective-permute-start | bytes 294920 | tf_op jit(solution)/shard_map/ppermute | solution.py:630
  331.0 16.2 %collective-permute-start.26 = (bf16[64,768]{1,0:T(8,128)(2,1)}, bf16[64,768]{1,0:T(8,128)(2,1)S(1)}, u32[]{:S(2)}, u32[]{:S(2)}) collective-permute-start(bf16[64,768]{1,0:T(8,128)(2,1)} %get-tuple-element.342), channel_id=1, source_target_pairs={{0,16},{2,18},{4,20},{6,22},{8,24},{10,26},{12,28},{14,30},{16,0},... | collective-permute-start | bytes 294920 | tf_op jit(solution)/shard_map/ppermute | solution.py:630
  333.2 13.9 %all-to-all-start.2 = ((f32[16,1,3072]{2,1,0:T(1,128)}), f32[16,1,3072]{2,1,0:T(1,128)S(1)}, u32[]{:S(2)}, u32[]{:S(2)}) async-start(f32[16,1,3072]{2,1,0:T(1,128)} %broadcast_in_dim.10), calls=%async_computation.3 | async-start | bytes 393216 | tf_op jit(solution)/shard_map/all_to_all | solution.py:742
  (55 other events, 456.6 us)
Sparse Core Ops, SparseCore 0:
  10.9 56.2 all-gather.2
  69.9 75.1 all-gather.4
  195.2 110.0 reduce-scatter.1

commit v5 on v4

--- a/solution.py
+++ b/solution.py
@@ -21,9 +21,7 @@
 
 
 def cost(flops, moved, raised=0):
-    return pl.CostEstimate(
-        flops=int(flops) // 4, bytes_accessed=int(moved) // 4, transcendentals=int(raised) // 4
-    )
+    return pl.CostEstimate(flops=int(flops), bytes_accessed=int(moved), transcendentals=int(raised))
 
 
 def resident(shape):
@@ -875,6 +873,7 @@
     after_grad, attn_grad, pieces, second_sums = second_back(
         fed[0][1], back_parts, after_attn, attn_branch, cotangent, merge_whole, gate_one, scale_two, cuts
     )
+    pieces, branch_parts = together(pieces, branch_parts)
     attended_grads = []
     for index in range(len(spans)):
         mine = pieces[index :: len(spans)]
@@ -886,7 +885,7 @@
     triple_grads = [
         attend_backward(triple, 0, *mixes[0], attended_grads[0], spans[0][1])
     ]
-    triple_grads, branch_parts = together(triple_grads, branch_parts)
+    triple_grads, attended_grads = together(triple_grads, attended_grads)
     pair = token_sum([([attn_grad], [attended_own]), ([normed_one], triple_grads)], fsdp_count)
     state = scatter_core(pair, fsdp_count)
     block_out, last_sums = last_forward(fed[0][0], branch_parts, after_attn, cotangent, gate_two)

time: 367 us -> 368 us (level)
  waiting for transfers between devices: 76.4 us -> 71.4 us
    ppermute x16, waiting for transfers between devices: 9.68 us -> 5.02 us  [shift_fsdp(): return lax.ppermute(values, 'fsdp', pairs)]
    unnamed x93 -> x83, local copies, waits for them, and re-layouts: 8.55 us -> 8.34 us
  transfers between devices with their start and end apart: 35 -> 35, of which waited for: 15 -> 12; matrix products, arithmetic and copies ran while one was open for 10% -> 10% of each run, Pallas kernels for 44% -> 44%
where the time goes in v5:
time: 368 us; the launch traced here: 362 us
  Pallas kernels  175 us (48%)
  waiting for transfers between devices  71.4 us (19%)
  starting transfers between devices  49.3 us (13%)
  other arithmetic  28.6 us (8%)
  local copies, waits for them, and re-layouts  15.3 us (4%)
  between operations  14.6 us (4%)
  blocking collectives  4.42 us (1%)
    ppermute x13, waiting for transfers between devices, shift_tp(): lax.ppermute(values, 'tp', [(i, (i + steps) % count) for i in range(count)])  52.8 us
    pallas_call x3, Pallas kernels, token_sum(): pl.pallas_call(body, grid=(width // tile,), in_specs=in_specs, out_specs=...  32.2 us
    pallas_call x2, Pallas kernels, feed_both(): pl.pallas_call(body, grid=(steps,), in_specs=[resident((tokens, depth)),...  31.9 us
    pallas_call x2, Pallas kernels, attend_backward(): pl.pallas_call(body, grid=(pairs, steps), in_specs=[pl.BlockSpec((block,...  30.8 us
    pallas_call x4, Pallas kernels, by_tokens(): pl.pallas_call(body, grid=(tokens // block,), in_specs=[cut(value.shape)...  25 us
    pallas_call x2, Pallas kernels, attend_forward(): pl.pallas_call(body, grid=(pairs, tokens // block), in_specs=[pl.BlockSpe...  19.9 us
    ppermute x16, starting transfers between devices, shift_fsdp(): return lax.ppermute(values, 'fsdp', pairs)  19.9 us
    ppermute x13, starting transfers between devices, shift_tp(): lax.ppermute(values, 'tp', [(i, (i + steps) % count) for i in range(count)])  14.5 us
  transfers between devices with their start and end apart: 35, of which 12 were waited for; matrix products, arithmetic and copies ran while one was open for 10% of the time, Pallas kernels for 44%

profile of v5, /device:TPU:0, one launch (start us, length us, event | category | flops | bytes accessed | tf_op | source)
XLA Modules:
  0.0 362.5 jit_solution(7333789389543175376)
XLA Ops:
  17.3 5.9 %all-to-all-start = ((bf16[16,1,64]{2,1,0:T(2,128)(2,1)}), bf16[16,1,64]{2,1,0:T(2,128)(2,1)S(1)}, u32[]{:S(2)}, u32[]{:S(2)}) async-start(bf16[16,1,64]{2,1,0:T(2,128)(2,1)} %all_to_all.30), calls=%async_computation | async-start | bytes 16384 | tf_op jit(solution)/shard_map/all_to_all | solution.py:794
  37.8 8.2 %all-to-all-done.1 = f32[16,1,3072]{2,1,0:T(1,128)S(1)} async-done(((f32[16,1,3072]{2,1,0:T(1,128)}), f32[16,1,3072]{2,1,0:T(1,128)S(1)}, u32[]{:S(2)}, u32[]{:S(2)}) %all-to-all-start.1) | async-done | bytes 196640 | tf_op jit(solution)/shard_map/all_to_all | solution.py:807
  69.1 7.0 %product.1.query_ref.keys_ref.values_ref = bf16[1024,1536]{1,0:T(8,128)(2,1)} custom-call(bf16[1024,1024]{1,0:T(8,128)(2,1)} %pad_maximum_fusion.left_ref.refs_2_.refs_0_, bf16[1024,1536]{1,0:T(8,128)(2,1)} %all-gather.3.cloned.1.call-done.right_ref.refs_2_), custom_call_target="tpu_custom_call" | custom-call | flops 3221225472 | bytes 11534336 | tf_op jit(solution)/shard_map/product/pallas_call | solution.py:45
  77.1 10.0 %attend_forward.3 = (bf16[1024,256]{1,0:T(8,128)(2,1)}, f32[1024,256]{1,0:T(8,128)}) custom-call(bf16[1024,1536]{1,0:T(8,128)(2,1)} %product.1.query_ref.keys_ref.values_ref, bf16[1024,1536]{1,0:T(8,128)(2,1)} %product.1.query_ref.keys_ref.values_ref, bf16[1024,1536]{1,0:T(8,128)(2,1)} %product.1.query_ref.keys_ref.values_ref), custom_call_target="tpu_custom_call" | custom-call | flops 4294967296 | bytes 3145728 | tf_op jit(solution)/shard_map/attend_forward/pallas_call | solution.py:219
  89.6 9.9 %attend_forward.2 = (bf16[1024,256]{1,0:T(8,128)(2,1)}, f32[1024,256]{1,0:T(8,128)}) custom-call(bf16[1024,1536]{1,0:T(8,128)(2,1)} %product.1.query_ref.keys_ref.values_ref, bf16[1024,1536]{1,0:T(8,128)(2,1)} %product.1.query_ref.keys_ref.values_ref, bf16[1024,1536]{1,0:T(8,128)(2,1)} %product.1.query_ref.keys_ref.values_ref), custom_call_target="tpu_custom_call" | custom-call | flops 4294967296 | bytes 3145728 | tf_op jit(solution)/shard_map/attend_forward/pallas_call | solution.py:219
  101.9 7.7 %collective-permute-done.7 = bf16[512,256]{1,0:T(8,128)(2,1)S(1)} collective-permute-done((bf16[512,256]{1,0:T(8,128)(2,1)S(1)}, bf16[512,256]{1,0:T(8,128)(2,1)S(1)}, u32[]{:S(2)}, u32[]{:S(2)}) %collective-permute-start.7) | collective-permute-done | bytes 262176 | tf_op jit(solution)/shard_map/ppermute | solution.py:611
  121.0 7.2 %probabilities.2.probs_ref = bf16[2,2,1024,1024]{3,2,1,0:T(8,128)(2,1)} custom-call(bf16[1024,1536]{1,0:T(8,128)(2,1)} %product.1.query_ref.keys_ref.values_ref, bf16[1024,1536]{1,0:T(8,128)(2,1)} %product.1.query_ref.keys_ref.values_ref, f32[1024,256]{1,0:T(8,128)} %get-tuple-element.157.level_ref), custom_call_target="tpu_custom_call" | custom-call | flops 1073741824 | bytes 8388608 | tf_op jit(solution)/shard_map/probabilities/pallas_call | solution.py:261
  128.1 7.2 %probabilities.3.probs_ref = bf16[2,2,1024,1024]{3,2,1,0:T(8,128)(2,1)} custom-call(bf16[1024,1536]{1,0:T(8,128)(2,1)} %product.1.query_ref.keys_ref.values_ref, bf16[1024,1536]{1,0:T(8,128)(2,1)} %product.1.query_ref.keys_ref.values_ref, f32[1024,256]{1,0:T(8,128)} %get-tuple-element.158.level_ref), custom_call_target="tpu_custom_call" | custom-call | flops 1073741824 | bytes 8388608 | tf_op jit(solution)/shard_map/probabilities/pallas_call | solution.py:261
  135.3 9.7 %collective-permute-done.11.normed_ref.refs_1_ = bf16[512,1024]{1,0:T(8,128)(2,1)S(1)} collective-permute-done((bf16[512,1024]{1,0:T(8,128)(2,1)}, bf16[512,1024]{1,0:T(8,128)(2,1)S(1)}, u32[]{:S(2)}, u32[]{:S(2)}) %collective-permute-start.11) | collective-permute-done | bytes 1048608 | tf_op jit(solution)/shard_map/ppermute | solution.py:611
  146.0 15.4 %feed_both.2 = (bf16[512,1024]{1,0:T(8,128)(2,1)}, bf16[512,1024]{1,0:T(8,128)(2,1)}, bf16[512,2048]{1,0:T(8,128)(2,1)}, bf16[512,2048]{1,0:T(8,128)(2,1)}) custom-call(bf16[512,1024]{1,0:T(8,128)(2,1)} %copy-done.34, bf16[512,1024]{1,0:T(8,128)(2,1)} %copy-done.32, bf16[1024,4096]{1,0:T(8,128)(2,1)} %all-gather.5.cloned.1.call-done.up_ref.down_ref, ...), custom_call_target="tpu_custom_call" | custom-call | flops 8589934592 | bytes 18874368 | tf_op jit(solution)/shard_map/feed_both/pallas_call | solution.py:403
  162.8 16.5 %feed_both.3 = (f32[512,1024]{1,0:T(8,128)}, f32[512,1024]{1,0:T(8,128)}, bf16[512,2048]{1,0:T(8,128)(2,1)}, bf16[512,2048]{1,0:T(8,128)(2,1)}) custom-call(bf16[512,1024]{1,0:T(8,128)(2,1)} %get-tuple-element.177.normed_ref.refs_0_, bf16[512,1024]{1,0:T(8,128)(2,1)} %copy-done.12, bf16[1024,4096]{1,0:T(8,128)(2,1)} %all-gather.5.cloned.1.call-done.up_ref.down_ref, ...), custom_call_target="tpu_custom_call" | custom-call | flops 8589934592 | bytes 18874368 | tf_op jit(solution)/shard_map/feed_both/pallas_call | solution.py:403
  179.2 16.5 %token_sum.3 = bf16[1024,4096]{1,0:T(8,128)(2,1)} custom-call(bf16[512,1024]{1,0:T(8,128)(2,1)} %get-tuple-element.177.normed_ref.refs_0_, bf16[512,1024]{1,0:T(8,128)(2,1)} %copy-done.34, bf16[512,2048]{1,0:T(8,128)(2,1)} %get-tuple-element.178.refs_2_, bf16[512,2048]{1,0:T(8,128)(2,1)} %get-tuple-element.179.refs_3_, bf16[512,1024]{1,0:T(8,128)(2,1)} %copy-done.12, ...), custom_call_target="tpu_custom_call" | custom-call | flops 8589934592 | bytes 20971520 | tf_op jit(solution)/shard_map/token_sum/pallas_call | solution.py:158
  198.0 7.9 %second_back.1 = (f32[512,1024]{1,0:T(8,128)}, bf16[512,1024]{1,0:T(8,128)(2,1)}, bf16[512,256]{1,0:T(8,128)(2,1)}, bf16[512,256]{1,0:T(8,128)(2,1)}, bf16[512,2...) custom-call(f32[512,1024]{1,0:T(8,128)} %get-tuple-element.176.refs_0_, bf16[512,1024]{1,0:T(8,128)(2,1)} %copy-done.11, ...), custom_call_target="tpu_custom_call" | custom-call | flops 1073741824 | bytes 15769600 | tf_op jit(solution)/shard_map/second_back/pallas_call | solution.py:477
  205.9 16.5 %collective-permute-done.13.refs_1_ = bf16[512,1024]{1,0:T(8,128)(2,1)S(1)} collective-permute-done((bf16[512,1024]{1,0:T(8,128)(2,1)S(1)}, bf16[512,1024]{1,0:T(8,128)(2,1)S(1)}, u32[]{:S(2)}, u32[]{:S(2)}) %collective-permute-start.13) | collective-permute-done | bytes 1048608 | tf_op jit(solution)/shard_map/ppermute | solution.py:611
  222.9 7.0 %collective-permute-done.14 = bf16[512,256]{1,0:T(8,128)(2,1)S(1)} collective-permute-done((bf16[512,256]{1,0:T(8,128)(2,1)}, bf16[512,256]{1,0:T(8,128)(2,1)S(1)}, u32[]{:S(2)}, u32[]{:S(2)}) %collective-permute-start.14) | collective-permute-done | bytes 262176 | tf_op jit(solution)/shard_map/ppermute | solution.py:611
  232.0 15.3 %attend_backward.2.refs_3_.refs_0_ = bf16[1024,768]{1,0:T(8,128)(2,1)} custom-call(bf16[1024,1536]{1,0:T(8,128)(2,1)} %product.1.query_ref.keys_ref.values_ref, bf16[1024,1536]{1,0:T(8,128)(2,1)} %product.1.query_ref.keys_ref.values_ref, bf16[1024,1536]{1,0:T(8,128)(2,1)} %product.1.query_ref.keys_ref.values_ref, ...), custom_call_target="tpu_custom_call" | custom-call | flops 8589934592 | bytes 13631488 | tf_op jit(solution)/shard_map/attend_backward/pallas_call | solution.py:343
  248.2 9.8 %token_sum.4 = (bf16[512,1792]{1,0:T(8,128)(2,1)}, bf16[512,1792]{1,0:T(8,128)(2,1)}) custom-call(bf16[512,1024]{1,0:T(8,128)(2,1)} %get-tuple-element.199.refs_0_, bf16[512,1024]{1,0:T(8,128)(2,1)} %pad_maximum_fusion.1.attended_ref.refs_1_, bf16[1024,1024]{1,0:T(8,128)(2,1)} %pad_maximum_fusion.left_ref.refs_2_.refs_0_, ...), custom_call_target="tpu_custom_call" | custom-call | flops 3758096384 | bytes 11534336 | tf_op jit(solution)/shard_map/token_sum/pallas_call | solution.py:158
  258.0 5.5 %last_forward.1 = (f32[512,8,128]{2,1,0:T(8,128)}, f32[8,1024]{1,0:T(8,128)}) custom-call(f32[512,1024]{1,0:T(8,128)} %get-tuple-element.203.refs_0_, bf16[512,1024]{1,0:T(8,128)(2,1)} %copy-done.10, f32[512,1024]{1,0:T(8,128)} %get-tuple-element.184.refs_2_, f32[512,1024]{1,0:T(8,128)} %bitcast.86, f32[1,1024]{1,0:T(1,128)} %copy-done.30), custom_call_target="tpu_custom_call" | custom-call | flops 3145728 | bytes 9474048 | tf_op jit(solution)/shard_map/last_forward/pallas_call | solution.py:477
  264.1 15.4 %attend_backward.3.refs_1_ = bf16[1024,768]{1,0:T(8,128)(2,1)} custom-call(bf16[1024,1536]{1,0:T(8,128)(2,1)} %product.1.query_ref.keys_ref.values_ref, bf16[1024,1536]{1,0:T(8,128)(2,1)} %product.1.query_ref.keys_ref.values_ref, bf16[1024,1536]{1,0:T(8,128)(2,1)} %product.1.query_ref.keys_ref.values_ref, bf16[1024,256]{1,0:T(8,128)(2,1)} %get-tuple-element.207.out_low_ref, ...), custom_call_target="tpu_custom_call" | custom-call | flops 8589934592 | bytes 13631488 | tf_op jit(solution)/shard_map/attend_backward/pallas_call | solution.py:343
  279.5 5.5 %product_back.2 = bf16[512,1024]{1,0:T(8,128)(2,1)} custom-call(bf16[1024,768]{1,0:T(8,128)(2,1)} %attend_backward.2.refs_3_.refs_0_, bf16[1024,768]{1,0:T(8,128)(2,1)} %attend_backward.3.refs_1_, bf16[1024,1536]{1,0:T(8,128)(2,1)} %all-gather.3.cloned.1.call-done.right_ref.refs_2_), custom_call_target="tpu_custom_call" | custom-call | flops 1610612736 | bytes 6815744 | tf_op jit(solution)/shard_map/product_back/pallas_call | solution.py:76
  286.8 6.0 %token_sum.5 = (bf16[512,768]{1,0:T(8,128)(2,1)}, bf16[512,768]{1,0:T(8,128)(2,1)}) custom-call(bf16[1024,1024]{1,0:T(8,128)(2,1)} %pad_maximum_fusion.left_ref.refs_2_.refs_0_, bf16[1024,768]{1,0:T(8,128)(2,1)} %attend_backward.3.refs_1_), custom_call_target="tpu_custom_call" | custom-call | flops 1610612736 | bytes 5242880 | tf_op jit(solution)/shard_map/token_sum/pallas_call | solution.py:158
  294.7 5.9 %product_back.3.refs_0_ = f32[512,1024]{1,0:T(8,128)} custom-call(bf16[1024,768]{1,0:T(8,128)(2,1)} %attend_backward.2.refs_3_.refs_0_, bf16[1024,768]{1,0:T(8,128)(2,1)} %attend_backward.3.refs_1_, bf16[1024,1536]{1,0:T(8,128)(2,1)} %all-gather.3.cloned.1.call-done.right_ref.refs_2_), custom_call_target="tpu_custom_call" | custom-call | flops 1610612736 | bytes 6815744 | tf_op jit(solution)/shard_map/product_back/pallas_call | solution.py:76
  300.6 10.3 %collective-permute-done.17.refs_1_ = bf16[512,1024]{1,0:T(8,128)(2,1)} collective-permute-done((bf16[512,1024]{1,0:T(8,128)(2,1)}, bf16[512,1024]{1,0:T(8,128)(2,1)}, u32[]{:S(2)}, u32[]{:S(2)}) %collective-permute-start.17) | collective-permute-done | bytes 1048608 | tf_op jit(solution)/shard_map/ppermute | solution.py:611
  318.0 6.2 %first_back.1 = (f32[512,8,128]{2,1,0:T(8,128)}, f32[8,1024]{1,0:T(8,128)}) custom-call(f32[512,1024]{1,0:T(8,128)} %product_back.3.refs_0_, bf16[512,1024]{1,0:T(8,128)(2,1)} %collective-permute-done.17.refs_1_, f32[512,1024]{1,0:T(8,128)} %bitcast.84, f32[512,1024]{1,0:T(8,128)} %get-tuple-element.222.refs_3_, f32[1,1024]{1,0:T(1,128)} %get-tuple-element.361.refs_4_), custom_call_target="tpu_custom_call" | custom-call | flops 10485760 | bytes 9474048 | tf_op jit(solution)/shard_map/first_back/pallas_call | solution.py:477
  (213 shorter events, 115.4 us)
Async XLA Ops:
  7.2 60.5 %all-gather.3.cloned.1.call-start = ((), (), s32[]{:S(2)}) async-start(), calls=%async_computation.4 | async-start | bytes 3342336 | tf_op jit(solution)/shard_map/all_gather | solution.py:720
  13.6 32.4 %collective-permute-start = (bf16[512,1024]{1,0:T(8,128)(2,1)}, bf16[512,1024]{1,0:T(8,128)(2,1)}, u32[]{:S(2)}, u32[]{:S(2)}) collective-permute-start(bf16[512,1024]{1,0:T(8,128)(2,1)} %multiply_convert_fusion.1), channel_id=1, source_target_pairs={{0,1},{1,0},{2,3},{3,2},{4,5},{5,4},{6,7},{7,6},{8,9},{9,8},{10,11... | collective-permute-start | bytes 3145736 | tf_op jit(solution)/shard_map/ppermute | solution.py:611
  17.3 12.3 %all-to-all-start = ((bf16[16,1,64]{2,1,0:T(2,128)(2,1)}), bf16[16,1,64]{2,1,0:T(2,128)(2,1)S(1)}, u32[]{:S(2)}, u32[]{:S(2)}) async-start(bf16[16,1,64]{2,1,0:T(2,128)(2,1)} %all_to_all.30), calls=%async_computation | async-start | bytes 16384 | tf_op jit(solution)/shard_map/all_to_all | solution.py:794
  31.6 14.4 %all-to-all-start.1 = ((f32[16,1,3072]{2,1,0:T(1,128)}), f32[16,1,3072]{2,1,0:T(1,128)S(1)}, u32[]{:S(2)}, u32[]{:S(2)}) async-start(f32[16,1,3072]{2,1,0:T(1,128)} %copy.88), calls=%async_computation.1 | async-start | bytes 393216 | tf_op jit(solution)/shard_map/all_to_all | solution.py:807
  36.0 109.8 %all-gather.5.cloned.1.call-start = ((), (), s32[]{:S(2)}) async-start(), calls=%async_computation.5 | async-start | bytes 8912896 | tf_op jit(solution)/shard_map/all_gather | solution.py:720
  55.6 12.1 %collective-permute-start.3 = (bf16[64,1024]{1,0:T(8,128)(2,1)S(1)}, bf16[64,1024]{1,0:T(8,128)(2,1)S(1)}, u32[]{:S(2)}, u32[]{:S(2)}) collective-permute-start(bf16[64,1024]{1,0:T(8,128)(2,1)S(1)} %constant_dynamic-update-slice_fusion), channel_id=1, source_target_pairs={{0,16},{2,18},{4,20},{6,22},{8,24},{10,26},{12,28},{14,30},{16,0},... | collective-permute-start | bytes 393224 | tf_op jit(solution)/shard_map/ppermute | solution.py:628
  67.7 256.5 %reduce-scatter.2.cloned.1.call-start = ((), (), s32[]{:S(2)}) async-start(), calls=%async_computation.6 | async-start | bytes 8912896 | tf_op jit(solution)/shard_map/reduce_scatter | solution.py:724
  68.2 31.4 %collective-permute-start.6 = (bf16[512,1024]{1,0:T(8,128)(2,1)S(1)}, bf16[512,1024]{1,0:T(8,128)(2,1)S(1)}, u32[]{:S(2)}, u32[]{:S(2)}) collective-permute-start(bf16[512,1024]{1,0:T(8,128)(2,1)S(1)} %multiply_convert_fusion.grad_ref.refs_4_), channel_id=1, source_target_pairs={{0,1},{1,0},{2,3},{3,2},{4,5},{5,4},{6,7},{7,6},{8,9},{9,8},{10,11... | collective-permute-start | bytes 3145736 | tf_op jit(solution)/shard_map/ppermute | solution.py:611
  76.3 23.3 %collective-permute-start.5 = (bf16[256,1024]{1,0:T(8,128)(2,1)S(1)}, bf16[256,1024]{1,0:T(8,128)(2,1)S(1)}, u32[]{:S(2)}, u32[]{:S(2)}) collective-permute-start(bf16[256,1024]{1,0:T(8,128)(2,1)S(1)} %constant_dynamic-update-slice_fusion.2.refs_0_), channel_id=1, source_target_pairs={{0,4},{2,6},{4,0},{6,2},{8,12},{10,14},{12,8},{14,10},{16,20},{18,... | collective-permute-start | bytes 1572872 | tf_op jit(solution)/shard_map/ppermute | solution.py:628
  88.1 13.8 %collective-permute-start.8 = (bf16[512,256]{1,0:T(8,128)(2,1)S(1)}, bf16[512,256]{1,0:T(8,128)(2,1)S(1)}, u32[]{:S(2)}, u32[]{:S(2)}) collective-permute-start(bf16[512,256]{1,0:T(8,128)(2,1)S(1)} %get-tuple-element.358), channel_id=1, source_target_pairs={{0,1},{1,0},{2,3},{3,2},{4,5},{5,4},{6,7},{7,6},{8,9},{9,8},{10,11... | collective-permute-start | bytes 786440 | tf_op jit(solution)/shard_map/ppermute | solution.py:611
  120.4 24.6 %collective-permute-start.11 = (bf16[512,1024]{1,0:T(8,128)(2,1)}, bf16[512,1024]{1,0:T(8,128)(2,1)S(1)}, u32[]{:S(2)}, u32[]{:S(2)}) collective-permute-start(bf16[512,1024]{1,0:T(8,128)(2,1)} %get-tuple-element.177.normed_ref.refs_0_), channel_id=1, source_target_pairs={{0,1},{1,0},{2,3},{3,2},{4,5},{5,4},{6,7},{7,6},{8,9},{9,8},{10,11... | collective-permute-start | bytes 3145736 | tf_op jit(solution)/shard_map/ppermute | solution.py:611
  161.4 34.3 %collective-permute-start.12 = (bf16[512,1024]{1,0:T(8,128)(2,1)}, bf16[512,1024]{1,0:T(8,128)(2,1)S(1)}, u32[]{:S(2)}, u32[]{:S(2)}) collective-permute-start(bf16[512,1024]{1,0:T(8,128)(2,1)} %get-tuple-element.165), channel_id=1, source_target_pairs={{0,1},{1,0},{2,3},{3,2},{4,5},{5,4},{6,7},{7,6},{8,9},{9,8},{10,11... | collective-permute-start | bytes 3145736 | tf_op jit(solution)/shard_map/ppermute | solution.py:611
  197.3 25.0 %collective-permute-start.13 = (bf16[512,1024]{1,0:T(8,128)(2,1)S(1)}, bf16[512,1024]{1,0:T(8,128)(2,1)S(1)}, u32[]{:S(2)}, u32[]{:S(2)}) collective-permute-start(bf16[512,1024]{1,0:T(8,128)(2,1)S(1)} %copy-done.33), channel_id=1, source_target_pairs={{0,1},{1,0},{2,3},{3,2},{4,5},{5,4},{6,7},{7,6},{8,9},{9,8},{10,11... | collective-permute-start | bytes 3145736 | tf_op jit(solution)/shard_map/ppermute | solution.py:611
  231.7 15.7 %collective-permute-start.15 = (bf16[512,256]{1,0:T(8,128)(2,1)}, bf16[512,256]{1,0:T(8,128)(2,1)S(1)}, u32[]{:S(2)}, u32[]{:S(2)}) collective-permute-start(bf16[512,256]{1,0:T(8,128)(2,1)} %get-tuple-element.197), channel_id=1, source_target_pairs={{0,1},{1,0},{2,3},{3,2},{4,5},{5,4},{6,7},{7,6},{8,9},{9,8},{10,11... | collective-permute-start | bytes 786440 | tf_op jit(solution)/shard_map/ppermute | solution.py:611
  263.8 29.0 %collective-permute-start.18 = (bf16[256,1792]{1,0:T(8,128)(2,1)S(1)}, bf16[256,1792]{1,0:T(8,128)(2,1)S(1)}, u32[]{:S(2)}, u32[]{:S(2)}) collective-permute-start(bf16[256,1792]{1,0:T(8,128)(2,1)S(1)} %add_convert_fusion.2), channel_id=1, source_target_pairs={{0,4},{2,6},{4,0},{6,2},{8,12},{10,14},{12,8},{14,10},{16,20},{18,... | collective-permute-start | bytes 2752520 | tf_op jit(solution)/shard_map/ppermute | solution.py:628
  285.1 25.8 %collective-permute-start.17 = (bf16[512,1024]{1,0:T(8,128)(2,1)}, bf16[512,1024]{1,0:T(8,128)(2,1)}, u32[]{:S(2)}, u32[]{:S(2)}) collective-permute-start(bf16[512,1024]{1,0:T(8,128)(2,1)} %product_back.2), channel_id=1, source_target_pairs={{0,1},{1,0},{2,3},{3,2},{4,5},{5,4},{6,7},{7,6},{8,9},{9,8},{10,11... | collective-permute-start | bytes 3145736 | tf_op jit(solution)/shard_map/ppermute | solution.py:611
  293.7 17.2 %collective-permute-start.19 = (bf16[512,768]{1,0:T(8,128)(2,1)}, bf16[512,768]{1,0:T(8,128)(2,1)S(1)}, u32[]{:S(2)}, u32[]{:S(2)}) collective-permute-start(bf16[512,768]{1,0:T(8,128)(2,1)} %get-tuple-element.219), channel_id=1, source_target_pairs={{0,2},{2,0},{4,6},{6,4},{8,10},{10,8},{12,14},{14,12},{16,18},{18,... | collective-permute-start | bytes 2359304 | tf_op jit(solution)/shard_map/ppermute | solution.py:628
  311.0 13.1 %collective-permute-start.20 = (bf16[256,768]{1,0:T(8,128)(2,1)S(1)}, bf16[256,768]{1,0:T(8,128)(2,1)}, u32[]{:S(2)}, u32[]{:S(2)}) collective-permute-start(bf16[256,768]{1,0:T(8,128)(2,1)S(1)} %add_convert_fusion.3), channel_id=1, source_target_pairs={{0,4},{2,6},{4,0},{6,2},{8,12},{10,14},{12,8},{14,10},{16,20},{18,... | collective-permute-start | bytes 1179656 | tf_op jit(solution)/shard_map/ppermute | solution.py:628
  313.6 24.1 %collective-permute-start.22 = (bf16[64,1792]{1,0:T(8,128)(2,1)}, bf16[64,1792]{1,0:T(8,128)(2,1)S(1)}, u32[]{:S(2)}, u32[]{:S(2)}) collective-permute-start(bf16[64,1792]{1,0:T(8,128)(2,1)} %get-tuple-element.349), channel_id=1, source_target_pairs={{0,8},{2,10},{4,12},{6,14},{8,16},{10,18},{12,20},{14,22},{16,24},... | collective-permute-start | bytes 688136 | tf_op jit(solution)/shard_map/ppermute | solution.py:628
  314.1 33.0 %collective-permute-start.23 = (bf16[64,1792]{1,0:T(8,128)(2,1)}, bf16[64,1792]{1,0:T(8,128)(2,1)}, u32[]{:S(2)}, u32[]{:S(2)}) collective-permute-start(bf16[64,1792]{1,0:T(8,128)(2,1)} %get-tuple-element.348), channel_id=1, source_target_pairs={{0,16},{2,18},{4,20},{6,22},{8,24},{10,26},{12,28},{14,30},{16,0},... | collective-permute-start | bytes 688136 | tf_op jit(solution)/shard_map/ppermute | solution.py:628
  315.0 32.1 %collective-permute-start.24 = (bf16[64,1792]{1,0:T(8,128)(2,1)}, bf16[64,1792]{1,0:T(8,128)(2,1)}, u32[]{:S(2)}, u32[]{:S(2)}) collective-permute-start(bf16[64,1792]{1,0:T(8,128)(2,1)} %get-tuple-element.347), channel_id=1, source_target_pairs={{0,24},{2,26},{4,28},{6,30},{8,0},{10,2},{12,4},{14,6},{16,8},{18,... | collective-permute-start | bytes 688136 | tf_op jit(solution)/shard_map/ppermute | solution.py:628
  326.1 21.1 %collective-permute-start.25 = (bf16[64,768]{1,0:T(8,128)(2,1)}, bf16[64,768]{1,0:T(8,128)(2,1)}, u32[]{:S(2)}, u32[]{:S(2)}) collective-permute-start(bf16[64,768]{1,0:T(8,128)(2,1)} %get-tuple-element.353), channel_id=1, source_target_pairs={{0,8},{2,10},{4,12},{6,14},{8,16},{10,18},{12,20},{14,22},{16,24},... | collective-permute-start | bytes 294920 | tf_op jit(solution)/shard_map/ppermute | solution.py:628
  331.0 16.2 %collective-permute-start.26 = (bf16[64,768]{1,0:T(8,128)(2,1)S(1)}, bf16[64,768]{1,0:T(8,128)(2,1)S(1)}, u32[]{:S(2)}, u32[]{:S(2)}) collective-permute-start(bf16[64,768]{1,0:T(8,128)(2,1)S(1)} %get-tuple-element.352), channel_id=1, source_target_pairs={{0,16},{2,18},{4,20},{6,22},{8,24},{10,26},{12,28},{14,30},{16,0},... | collective-permute-start | bytes 294920 | tf_op jit(solution)/shard_map/ppermute | solution.py:628
  333.3 13.8 %all-to-all-start.2 = ((f32[16,1,3072]{2,1,0:T(1,128)}), f32[16,1,3072]{2,1,0:T(1,128)S(1)}, u32[]{:S(2)}, u32[]{:S(2)}) async-start(f32[16,1,3072]{2,1,0:T(1,128)} %broadcast_in_dim.10), calls=%async_computation.3 | async-start | bytes 393216 | tf_op jit(solution)/shard_map/all_to_all | solution.py:740
  (50 other events, 431.5 us)
Sparse Core Ops, SparseCore 0:
  10.9 49.5 all-gather.2
  67.8 77.9 all-gather.4
  195.8 111.0 reduce-scatter.1

commit v6 on v5

--- a/solution.py
+++ b/solution.py
@@ -873,7 +873,6 @@
     after_grad, attn_grad, pieces, second_sums = second_back(
         fed[0][1], back_parts, after_attn, attn_branch, cotangent, merge_whole, gate_one, scale_two, cuts
     )
-    pieces, branch_parts = together(pieces, branch_parts)
     attended_grads = []
     for index in range(len(spans)):
         mine = pieces[index :: len(spans)]
@@ -885,7 +884,7 @@
     triple_grads = [
         attend_backward(triple, 0, *mixes[0], attended_grads[0], spans[0][1])
     ]
-    triple_grads, attended_grads = together(triple_grads, attended_grads)
+    triple_grads, branch_parts, attended_grads = together(triple_grads, branch_parts, attended_grads)
     pair = token_sum([([attn_grad], [attended_own]), ([normed_one], triple_grads)], fsdp_count)
     state = scatter_core(pair, fsdp_count)
     block_out, last_sums = last_forward(fed[0][0], branch_parts, after_attn, cotangent, gate_two)

time: 368 us -> 362 us (0.984)
  waiting for transfers between devices: 71.4 us -> 66.1 us
    ppermute x13, waiting for transfers between devices: 52.8 us -> 43.3 us  [shift_tp(): lax.ppermute(values, 'tp', [(i, (i + steps) % count) for i in range(count)])]
    ppermute x16, waiting for transfers between devices: 5.02 us -> 8.9 us  [shift_fsdp(): return lax.ppermute(values, 'fsdp', pairs)]
  transfers between devices with their start and end apart: 35 -> 35, of which waited for: 12 -> 14; matrix products, arithmetic and copies ran while one was open for 10% -> 11% of each run, Pallas kernels for 44% -> 45%
where the time goes in v6:
time: 362 us; the launch traced here: 357 us
  Pallas kernels  176 us (49%)
  waiting for transfers between devices  66.1 us (18%)
  starting transfers between devices  49 us (14%)
  other arithmetic  28.7 us (8%)
  local copies, waits for them, and re-layouts  14.8 us (4%)
  between operations  14.6 us (4%)
  blocking collectives  4.42 us (1%)
  matrix products  3.63 us (1%)
    ppermute x13, waiting for transfers between devices, shift_tp(): lax.ppermute(values, 'tp', [(i, (i + steps) % count) for i in range(count)])  43.3 us
    pallas_call x3, Pallas kernels, token_sum(): pl.pallas_call(body, grid=(width // tile,), in_specs=in_specs, out_specs=...  32.5 us
    pallas_call x2, Pallas kernels, feed_both(): pl.pallas_call(body, grid=(steps,), in_specs=[resident((tokens, depth)),...  31.9 us
    pallas_call x2, Pallas kernels, attend_backward(): pl.pallas_call(body, grid=(pairs, steps), in_specs=[pl.BlockSpec((block,...  30.9 us
    pallas_call x4, Pallas kernels, by_tokens(): pl.pallas_call(body, grid=(tokens // block,), in_specs=[cut(value.shape)...  25 us
    ppermute x16, starting transfers between devices, shift_fsdp(): return lax.ppermute(values, 'fsdp', pairs)  20.4 us
    pallas_call x2, Pallas kernels, attend_forward(): pl.pallas_call(body, grid=(pairs, tokens // block), in_specs=[pl.BlockSpe...  19.9 us
    pallas_call x2, Pallas kernels, probabilities(): pl.pallas_call(body, grid=(pairs, tokens // block), in_specs=[pl.BlockSpe...  14.3 us
  transfers between devices with their start and end apart: 35, of which 14 were waited for; matrix products, arithmetic and copies ran while one was open for 11% of the time, Pallas kernels for 45%

profile of v6, /device:TPU:0, one launch (start us, length us, event | category | flops | bytes accessed | tf_op | source)
XLA Modules:
  0.0 356.9 jit_solution(8268236859336950111)
XLA Ops:
  17.3 5.9 %all-to-all-start = ((bf16[16,1,64]{2,1,0:T(2,128)(2,1)}), bf16[16,1,64]{2,1,0:T(2,128)(2,1)S(1)}, u32[]{:S(2)}, u32[]{:S(2)}) async-start(bf16[16,1,64]{2,1,0:T(2,128)(2,1)} %all_to_all.30), calls=%async_computation | async-start | bytes 16384 | tf_op jit(solution)/shard_map/all_to_all | solution.py:794
  37.8 8.2 %all-to-all-done.1 = f32[16,1,3072]{2,1,0:T(1,128)S(1)} async-done(((f32[16,1,3072]{2,1,0:T(1,128)}), f32[16,1,3072]{2,1,0:T(1,128)S(1)}, u32[]{:S(2)}, u32[]{:S(2)}) %all-to-all-start.1) | async-done | bytes 196640 | tf_op jit(solution)/shard_map/all_to_all | solution.py:807
  69.1 7.0 %product.1.query_ref.keys_ref.values_ref = bf16[1024,1536]{1,0:T(8,128)(2,1)} custom-call(bf16[1024,1024]{1,0:T(8,128)(2,1)} %pad_maximum_fusion.left_ref.refs_2_.refs_0_, bf16[1024,1536]{1,0:T(8,128)(2,1)} %all-gather.3.cloned.1.call-done.right_ref.refs_2_), custom_call_target="tpu_custom_call" | custom-call | flops 3221225472 | bytes 11534336 | tf_op jit(solution)/shard_map/product/pallas_call | solution.py:45
  77.1 10.0 %attend_forward.3 = (bf16[1024,256]{1,0:T(8,128)(2,1)}, f32[1024,256]{1,0:T(8,128)}) custom-call(bf16[1024,1536]{1,0:T(8,128)(2,1)} %product.1.query_ref.keys_ref.values_ref, bf16[1024,1536]{1,0:T(8,128)(2,1)} %product.1.query_ref.keys_ref.values_ref, bf16[1024,1536]{1,0:T(8,128)(2,1)} %product.1.query_ref.keys_ref.values_ref), custom_call_target="tpu_custom_call" | custom-call | flops 4294967296 | bytes 3145728 | tf_op jit(solution)/shard_map/attend_forward/pallas_call | solution.py:219
  89.6 9.9 %attend_forward.2 = (bf16[1024,256]{1,0:T(8,128)(2,1)}, f32[1024,256]{1,0:T(8,128)}) custom-call(bf16[1024,1536]{1,0:T(8,128)(2,1)} %product.1.query_ref.keys_ref.values_ref, bf16[1024,1536]{1,0:T(8,128)(2,1)} %product.1.query_ref.keys_ref.values_ref, bf16[1024,1536]{1,0:T(8,128)(2,1)} %product.1.query_ref.keys_ref.values_ref), custom_call_target="tpu_custom_call" | custom-call | flops 4294967296 | bytes 3145728 | tf_op jit(solution)/shard_map/attend_forward/pallas_call | solution.py:219
  101.9 7.7 %collective-permute-done.7 = bf16[512,256]{1,0:T(8,128)(2,1)S(1)} collective-permute-done((bf16[512,256]{1,0:T(8,128)(2,1)S(1)}, bf16[512,256]{1,0:T(8,128)(2,1)S(1)}, u32[]{:S(2)}, u32[]{:S(2)}) %collective-permute-start.7) | collective-permute-done | bytes 262176 | tf_op jit(solution)/shard_map/ppermute | solution.py:611
  114.9 5.5 %merge_and_normalize.1 = (f32[512,1024]{1,0:T(8,128)}, f32[512,1024]{1,0:T(8,128)}, bf16[512,1024]{1,0:T(8,128)(2,1)}) custom-call(bf16[512,1024]{1,0:T(8,128)(2,1)} %pad_maximum_fusion.1.attended_ref.refs_1_, f32[512,1024]{1,0:T(8,128)} %bitcast.83, bf16[1024,1024]{1,0:T(8,128)(2,1)} %arrange.1.merge_ref.refs_5_, ...), custom_call_target="tpu_custom_call" | custom-call | flops 1073741824 | bytes 10498048 | tf_op jit(solution)/shard_map/merge_and_normalize/pallas_call | solution.py:477
  121.1 7.2 %probabilities.2.probs_ref = bf16[2,2,1024,1024]{3,2,1,0:T(8,128)(2,1)} custom-call(bf16[1024,1536]{1,0:T(8,128)(2,1)} %product.1.query_ref.keys_ref.values_ref, bf16[1024,1536]{1,0:T(8,128)(2,1)} %product.1.query_ref.keys_ref.values_ref, f32[1024,256]{1,0:T(8,128)} %get-tuple-element.153.level_ref), custom_call_target="tpu_custom_call" | custom-call | flops 1073741824 | bytes 8388608 | tf_op jit(solution)/shard_map/probabilities/pallas_call | solution.py:261
  128.2 7.2 %probabilities.3.probs_ref = bf16[2,2,1024,1024]{3,2,1,0:T(8,128)(2,1)} custom-call(bf16[1024,1536]{1,0:T(8,128)(2,1)} %product.1.query_ref.keys_ref.values_ref, bf16[1024,1536]{1,0:T(8,128)(2,1)} %product.1.query_ref.keys_ref.values_ref, f32[1024,256]{1,0:T(8,128)} %get-tuple-element.154.level_ref), custom_call_target="tpu_custom_call" | custom-call | flops 1073741824 | bytes 8388608 | tf_op jit(solution)/shard_map/probabilities/pallas_call | solution.py:261
  135.4 9.7 %collective-permute-done.11.normed_ref.refs_1_ = bf16[512,1024]{1,0:T(8,128)(2,1)S(1)} collective-permute-done((bf16[512,1024]{1,0:T(8,128)(2,1)}, bf16[512,1024]{1,0:T(8,128)(2,1)S(1)}, u32[]{:S(2)}, u32[]{:S(2)}) %collective-permute-start.11) | collective-permute-done | bytes 1048608 | tf_op jit(solution)/shard_map/ppermute | solution.py:611
  146.1 15.4 %feed_both.2 = (bf16[512,1024]{1,0:T(8,128)(2,1)}, bf16[512,1024]{1,0:T(8,128)(2,1)}, bf16[512,2048]{1,0:T(8,128)(2,1)}, bf16[512,2048]{1,0:T(8,128)(2,1)}) custom-call(bf16[512,1024]{1,0:T(8,128)(2,1)} %copy-done.34, bf16[512,1024]{1,0:T(8,128)(2,1)} %copy-done.32, bf16[1024,4096]{1,0:T(8,128)(2,1)} %all-gather.5.cloned.1.call-done.up_ref.down_ref, ...), custom_call_target="tpu_custom_call" | custom-call | flops 8589934592 | bytes 18874368 | tf_op jit(solution)/shard_map/feed_both/pallas_call | solution.py:403
  162.8 16.5 %feed_both.3 = (f32[512,1024]{1,0:T(8,128)}, f32[512,1024]{1,0:T(8,128)}, bf16[512,2048]{1,0:T(8,128)(2,1)}, bf16[512,2048]{1,0:T(8,128)(2,1)}) custom-call(bf16[512,1024]{1,0:T(8,128)(2,1)} %get-tuple-element.173.normed_ref.refs_0_, bf16[512,1024]{1,0:T(8,128)(2,1)} %copy-done.12, bf16[1024,4096]{1,0:T(8,128)(2,1)} %all-gather.5.cloned.1.call-done.up_ref.down_ref, ...), custom_call_target="tpu_custom_call" | custom-call | flops 8589934592 | bytes 18874368 | tf_op jit(solution)/shard_map/feed_both/pallas_call | solution.py:403
  179.2 16.5 %token_sum.3 = bf16[1024,4096]{1,0:T(8,128)(2,1)} custom-call(bf16[512,1024]{1,0:T(8,128)(2,1)} %get-tuple-element.173.normed_ref.refs_0_, bf16[512,1024]{1,0:T(8,128)(2,1)} %copy-done.34, bf16[512,2048]{1,0:T(8,128)(2,1)} %get-tuple-element.174.refs_2_, bf16[512,2048]{1,0:T(8,128)(2,1)} %get-tuple-element.175.refs_3_, bf16[512,1024]{1,0:T(8,128)(2,1)} %copy-done.12, ...), custom_call_target="tpu_custom_call" | custom-call | flops 8589934592 | bytes 20971520 | tf_op jit(solution)/shard_map/token_sum/pallas_call | solution.py:158
  196.7 7.9 %second_back.1 = (f32[512,1024]{1,0:T(8,128)}, bf16[512,1024]{1,0:T(8,128)(2,1)}, bf16[512,256]{1,0:T(8,128)(2,1)}, bf16[512,256]{1,0:T(8,128)(2,1)}, bf16[512,2...) custom-call(f32[512,1024]{1,0:T(8,128)} %get-tuple-element.172.refs_0_, bf16[512,1024]{1,0:T(8,128)(2,1)} %copy-done.10, ...), custom_call_target="tpu_custom_call" | custom-call | flops 1073741824 | bytes 15769600 | tf_op jit(solution)/shard_map/second_back/pallas_call | solution.py:477
  206.7 7.4 %collective-permute-done.13 = bf16[512,256]{1,0:T(8,128)(2,1)S(1)} collective-permute-done((bf16[512,256]{1,0:T(8,128)(2,1)}, bf16[512,256]{1,0:T(8,128)(2,1)S(1)}, u32[]{:S(2)}, u32[]{:S(2)}) %collective-permute-start.13) | collective-permute-done | bytes 262176 | tf_op jit(solution)/shard_map/ppermute | solution.py:611
  216.7 15.5 %attend_backward.2.refs_3_.refs_0_ = bf16[1024,768]{1,0:T(8,128)(2,1)} custom-call(bf16[1024,1536]{1,0:T(8,128)(2,1)} %product.1.query_ref.keys_ref.values_ref, bf16[1024,1536]{1,0:T(8,128)(2,1)} %product.1.query_ref.keys_ref.values_ref, bf16[1024,1536]{1,0:T(8,128)(2,1)} %product.1.query_ref.keys_ref.values_ref, ...), custom_call_target="tpu_custom_call" | custom-call | flops 8589934592 | bytes 13631488 | tf_op jit(solution)/shard_map/attend_backward/pallas_call | solution.py:343
  232.2 8.9 %collective-permute-done.15 = bf16[512,256]{1,0:T(8,128)(2,1)S(1)} collective-permute-done((bf16[512,256]{1,0:T(8,128)(2,1)}, bf16[512,256]{1,0:T(8,128)(2,1)S(1)}, u32[]{:S(2)}, u32[]{:S(2)}) %collective-permute-start.15) | collective-permute-done | bytes 262176 | tf_op jit(solution)/shard_map/ppermute | solution.py:611
  242.0 10.1 %token_sum.4 = (bf16[512,1792]{1,0:T(8,128)(2,1)}, bf16[512,1792]{1,0:T(8,128)(2,1)}) custom-call(bf16[512,1024]{1,0:T(8,128)(2,1)} %get-tuple-element.191.refs_0_, bf16[512,1024]{1,0:T(8,128)(2,1)} %pad_maximum_fusion.1.attended_ref.refs_1_, bf16[1024,1024]{1,0:T(8,128)(2,1)} %pad_maximum_fusion.left_ref.refs_2_.refs_0_, ...), custom_call_target="tpu_custom_call" | custom-call | flops 3758096384 | bytes 11534336 | tf_op jit(solution)/shard_map/token_sum/pallas_call | solution.py:158
  258.4 15.4 %attend_backward.3.refs_1_ = bf16[1024,768]{1,0:T(8,128)(2,1)} custom-call(bf16[1024,1536]{1,0:T(8,128)(2,1)} %product.1.query_ref.keys_ref.values_ref, bf16[1024,1536]{1,0:T(8,128)(2,1)} %product.1.query_ref.keys_ref.values_ref, bf16[1024,1536]{1,0:T(8,128)(2,1)} %product.1.query_ref.keys_ref.values_ref, bf16[1024,256]{1,0:T(8,128)(2,1)} %get-tuple-element.199.out_low_ref, ...), custom_call_target="tpu_custom_call" | custom-call | flops 8589934592 | bytes 13631488 | tf_op jit(solution)/shard_map/attend_backward/pallas_call | solution.py:343
  273.8 5.5 %product_back.2 = bf16[512,1024]{1,0:T(8,128)(2,1)} custom-call(bf16[1024,768]{1,0:T(8,128)(2,1)} %attend_backward.2.refs_3_.refs_0_, bf16[1024,768]{1,0:T(8,128)(2,1)} %attend_backward.3.refs_1_, bf16[1024,1536]{1,0:T(8,128)(2,1)} %all-gather.3.cloned.1.call-done.right_ref.refs_2_), custom_call_target="tpu_custom_call" | custom-call | flops 1610612736 | bytes 6815744 | tf_op jit(solution)/shard_map/product_back/pallas_call | solution.py:76
  280.1 6.0 %token_sum.5 = (bf16[512,768]{1,0:T(8,128)(2,1)}, bf16[512,768]{1,0:T(8,128)(2,1)}) custom-call(bf16[1024,1024]{1,0:T(8,128)(2,1)} %pad_maximum_fusion.left_ref.refs_2_.refs_0_, bf16[1024,768]{1,0:T(8,128)(2,1)} %attend_backward.3.refs_1_), custom_call_target="tpu_custom_call" | custom-call | flops 1610612736 | bytes 5242880 | tf_op jit(solution)/shard_map/token_sum/pallas_call | solution.py:158
  291.8 5.9 %product_back.3.refs_0_ = f32[512,1024]{1,0:T(8,128)} custom-call(bf16[1024,768]{1,0:T(8,128)(2,1)} %attend_backward.2.refs_3_.refs_0_, bf16[1024,768]{1,0:T(8,128)(2,1)} %attend_backward.3.refs_1_, bf16[1024,1536]{1,0:T(8,128)(2,1)} %all-gather.3.cloned.1.call-done.right_ref.refs_2_), custom_call_target="tpu_custom_call" | custom-call | flops 1610612736 | bytes 6815744 | tf_op jit(solution)/shard_map/product_back/pallas_call | solution.py:76
  297.7 7.1 %collective-permute-done.17.refs_1_ = bf16[512,1024]{1,0:T(8,128)(2,1)} collective-permute-done((bf16[512,1024]{1,0:T(8,128)(2,1)}, bf16[512,1024]{1,0:T(8,128)(2,1)}, u32[]{:S(2)}, u32[]{:S(2)}) %collective-permute-start.17) | collective-permute-done | bytes 1048608 | tf_op jit(solution)/shard_map/ppermute | solution.py:611
  312.1 6.2 %first_back.1 = (f32[512,8,128]{2,1,0:T(8,128)}, f32[8,1024]{1,0:T(8,128)}) custom-call(f32[512,1024]{1,0:T(8,128)} %product_back.3.refs_0_, bf16[512,1024]{1,0:T(8,128)(2,1)} %collective-permute-done.17.refs_1_, f32[512,1024]{1,0:T(8,128)} %bitcast.84, f32[512,1024]{1,0:T(8,128)} %get-tuple-element.214.refs_3_, f32[1,1024]{1,0:T(1,128)} %get-tuple-element.353.refs_4_), custom_call_target="tpu_custom_call" | custom-call | flops 10485760 | bytes 9474048 | tf_op jit(solution)/shard_map/first_back/pallas_call | solution.py:477
  (213 shorter events, 119.7 us)
Async XLA Ops:
  7.2 60.5 %all-gather.3.cloned.1.call-start = ((), (), s32[]{:S(2)}) async-start(), calls=%async_computation.4 | async-start | bytes 3342336 | tf_op jit(solution)/shard_map/all_gather | solution.py:720
  13.6 32.4 %collective-permute-start = (bf16[512,1024]{1,0:T(8,128)(2,1)}, bf16[512,1024]{1,0:T(8,128)(2,1)}, u32[]{:S(2)}, u32[]{:S(2)}) collective-permute-start(bf16[512,1024]{1,0:T(8,128)(2,1)} %multiply_convert_fusion.1), channel_id=1, source_target_pairs={{0,1},{1,0},{2,3},{3,2},{4,5},{5,4},{6,7},{7,6},{8,9},{9,8},{10,11... | collective-permute-start | bytes 3145736 | tf_op jit(solution)/shard_map/ppermute | solution.py:611
  17.3 12.3 %all-to-all-start = ((bf16[16,1,64]{2,1,0:T(2,128)(2,1)}), bf16[16,1,64]{2,1,0:T(2,128)(2,1)S(1)}, u32[]{:S(2)}, u32[]{:S(2)}) async-start(bf16[16,1,64]{2,1,0:T(2,128)(2,1)} %all_to_all.30), calls=%async_computation | async-start | bytes 16384 | tf_op jit(solution)/shard_map/all_to_all | solution.py:794
  31.6 14.4 %all-to-all-start.1 = ((f32[16,1,3072]{2,1,0:T(1,128)}), f32[16,1,3072]{2,1,0:T(1,128)S(1)}, u32[]{:S(2)}, u32[]{:S(2)}) async-start(f32[16,1,3072]{2,1,0:T(1,128)} %copy.88), calls=%async_computation.1 | async-start | bytes 393216 | tf_op jit(solution)/shard_map/all_to_all | solution.py:807
  36.0 109.8 %all-gather.5.cloned.1.call-start = ((), (), s32[]{:S(2)}) async-start(), calls=%async_computation.5 | async-start | bytes 8912896 | tf_op jit(solution)/shard_map/all_gather | solution.py:720
  55.6 12.1 %collective-permute-start.3 = (bf16[64,1024]{1,0:T(8,128)(2,1)S(1)}, bf16[64,1024]{1,0:T(8,128)(2,1)S(1)}, u32[]{:S(2)}, u32[]{:S(2)}) collective-permute-start(bf16[64,1024]{1,0:T(8,128)(2,1)S(1)} %constant_dynamic-update-slice_fusion), channel_id=1, source_target_pairs={{0,16},{2,18},{4,20},{6,22},{8,24},{10,26},{12,28},{14,30},{16,0},... | collective-permute-start | bytes 393224 | tf_op jit(solution)/shard_map/ppermute | solution.py:628
  67.7 250.7 %reduce-scatter.2.cloned.1.call-start = ((), (), s32[]{:S(2)}) async-start(), calls=%async_computation.6 | async-start | bytes 8912896 | tf_op jit(solution)/shard_map/reduce_scatter | solution.py:724
  68.2 31.4 %collective-permute-start.6 = (bf16[512,1024]{1,0:T(8,128)(2,1)S(1)}, bf16[512,1024]{1,0:T(8,128)(2,1)S(1)}, u32[]{:S(2)}, u32[]{:S(2)}) collective-permute-start(bf16[512,1024]{1,0:T(8,128)(2,1)S(1)} %multiply_convert_fusion.grad_ref.refs_4_), channel_id=1, source_target_pairs={{0,1},{1,0},{2,3},{3,2},{4,5},{5,4},{6,7},{7,6},{8,9},{9,8},{10,11... | collective-permute-start | bytes 3145736 | tf_op jit(solution)/shard_map/ppermute | solution.py:611
  76.3 23.3 %collective-permute-start.5 = (bf16[256,1024]{1,0:T(8,128)(2,1)S(1)}, bf16[256,1024]{1,0:T(8,128)(2,1)S(1)}, u32[]{:S(2)}, u32[]{:S(2)}) collective-permute-start(bf16[256,1024]{1,0:T(8,128)(2,1)S(1)} %constant_dynamic-update-slice_fusion.2.refs_0_), channel_id=1, source_target_pairs={{0,4},{2,6},{4,0},{6,2},{8,12},{10,14},{12,8},{14,10},{16,20},{18,... | collective-permute-start | bytes 1572872 | tf_op jit(solution)/shard_map/ppermute | solution.py:628
  88.1 13.8 %collective-permute-start.8 = (bf16[512,256]{1,0:T(8,128)(2,1)S(1)}, bf16[512,256]{1,0:T(8,128)(2,1)S(1)}, u32[]{:S(2)}, u32[]{:S(2)}) collective-permute-start(bf16[512,256]{1,0:T(8,128)(2,1)S(1)} %get-tuple-element.350), channel_id=1, source_target_pairs={{0,1},{1,0},{2,3},{3,2},{4,5},{5,4},{6,7},{7,6},{8,9},{9,8},{10,11... | collective-permute-start | bytes 786440 | tf_op jit(solution)/shard_map/ppermute | solution.py:611
  120.5 24.6 %collective-permute-start.11 = (bf16[512,1024]{1,0:T(8,128)(2,1)}, bf16[512,1024]{1,0:T(8,128)(2,1)S(1)}, u32[]{:S(2)}, u32[]{:S(2)}) collective-permute-start(bf16[512,1024]{1,0:T(8,128)(2,1)} %get-tuple-element.173.normed_ref.refs_0_), channel_id=1, source_target_pairs={{0,1},{1,0},{2,3},{3,2},{4,5},{5,4},{6,7},{7,6},{8,9},{9,8},{10,11... | collective-permute-start | bytes 3145736 | tf_op jit(solution)/shard_map/ppermute | solution.py:611
  161.5 34.2 %collective-permute-start.12 = (bf16[512,1024]{1,0:T(8,128)(2,1)}, bf16[512,1024]{1,0:T(8,128)(2,1)S(1)}, u32[]{:S(2)}, u32[]{:S(2)}) collective-permute-start(bf16[512,1024]{1,0:T(8,128)(2,1)} %get-tuple-element.161), channel_id=1, source_target_pairs={{0,1},{1,0},{2,3},{3,2},{4,5},{5,4},{6,7},{7,6},{8,9},{9,8},{10,11... | collective-permute-start | bytes 3145736 | tf_op jit(solution)/shard_map/ppermute | solution.py:611
  205.5 36.5 %collective-permute-start.14 = (bf16[512,1024]{1,0:T(8,128)(2,1)S(1)}, bf16[512,1024]{1,0:T(8,128)(2,1)S(1)}, u32[]{:S(2)}, u32[]{:S(2)}) collective-permute-start(bf16[512,1024]{1,0:T(8,128)(2,1)S(1)} %copy-done.33), channel_id=1, source_target_pairs={{0,1},{1,0},{2,3},{3,2},{4,5},{5,4},{6,7},{7,6},{8,9},{9,8},{10,11... | collective-permute-start | bytes 3145736 | tf_op jit(solution)/shard_map/ppermute | solution.py:611
  215.9 25.3 %collective-permute-start.15 = (bf16[512,256]{1,0:T(8,128)(2,1)}, bf16[512,256]{1,0:T(8,128)(2,1)S(1)}, u32[]{:S(2)}, u32[]{:S(2)}) collective-permute-start(bf16[512,256]{1,0:T(8,128)(2,1)} %get-tuple-element.189), channel_id=1, source_target_pairs={{0,1},{1,0},{2,3},{3,2},{4,5},{5,4},{6,7},{7,6},{8,9},{9,8},{10,11... | collective-permute-start | bytes 786440 | tf_op jit(solution)/shard_map/ppermute | solution.py:611
  257.8 32.3 %collective-permute-start.18 = (bf16[256,1792]{1,0:T(8,128)(2,1)S(1)}, bf16[256,1792]{1,0:T(8,128)(2,1)S(1)}, u32[]{:S(2)}, u32[]{:S(2)}) collective-permute-start(bf16[256,1792]{1,0:T(8,128)(2,1)S(1)} %add_convert_fusion.2), channel_id=1, source_target_pairs={{0,4},{2,6},{4,0},{6,2},{8,12},{10,14},{12,8},{14,10},{16,20},{18,... | collective-permute-start | bytes 2752520 | tf_op jit(solution)/shard_map/ppermute | solution.py:628
  279.3 25.5 %collective-permute-start.17 = (bf16[512,1024]{1,0:T(8,128)(2,1)}, bf16[512,1024]{1,0:T(8,128)(2,1)}, u32[]{:S(2)}, u32[]{:S(2)}) collective-permute-start(bf16[512,1024]{1,0:T(8,128)(2,1)} %product_back.2), channel_id=1, source_target_pairs={{0,1},{1,0},{2,3},{3,2},{4,5},{5,4},{6,7},{7,6},{8,9},{9,8},{10,11... | collective-permute-start | bytes 3145736 | tf_op jit(solution)/shard_map/ppermute | solution.py:611
  291.0 13.8 %collective-permute-start.19 = (bf16[512,768]{1,0:T(8,128)(2,1)}, bf16[512,768]{1,0:T(8,128)(2,1)S(1)}, u32[]{:S(2)}, u32[]{:S(2)}) collective-permute-start(bf16[512,768]{1,0:T(8,128)(2,1)} %get-tuple-element.211), channel_id=1, source_target_pairs={{0,2},{2,0},{4,6},{6,4},{8,10},{10,8},{12,14},{14,12},{16,18},{18,... | collective-permute-start | bytes 2359304 | tf_op jit(solution)/shard_map/ppermute | solution.py:628
  304.9 13.4 %collective-permute-start.20 = (bf16[256,768]{1,0:T(8,128)(2,1)S(1)}, bf16[256,768]{1,0:T(8,128)(2,1)}, u32[]{:S(2)}, u32[]{:S(2)}) collective-permute-start(bf16[256,768]{1,0:T(8,128)(2,1)S(1)} %add_convert_fusion.3), channel_id=1, source_target_pairs={{0,4},{2,6},{4,0},{6,2},{8,12},{10,14},{12,8},{14,10},{16,20},{18,... | collective-permute-start | bytes 1179656 | tf_op jit(solution)/shard_map/ppermute | solution.py:628
  307.6 23.9 %collective-permute-start.22 = (bf16[64,1792]{1,0:T(8,128)(2,1)}, bf16[64,1792]{1,0:T(8,128)(2,1)S(1)}, u32[]{:S(2)}, u32[]{:S(2)}) collective-permute-start(bf16[64,1792]{1,0:T(8,128)(2,1)} %get-tuple-element.341), channel_id=1, source_target_pairs={{0,8},{2,10},{4,12},{6,14},{8,16},{10,18},{12,20},{14,22},{16,24},... | collective-permute-start | bytes 688136 | tf_op jit(solution)/shard_map/ppermute | solution.py:628
  308.6 32.9 %collective-permute-start.23 = (bf16[64,1792]{1,0:T(8,128)(2,1)}, bf16[64,1792]{1,0:T(8,128)(2,1)}, u32[]{:S(2)}, u32[]{:S(2)}) collective-permute-start(bf16[64,1792]{1,0:T(8,128)(2,1)} %get-tuple-element.340), channel_id=1, source_target_pairs={{0,16},{2,18},{4,20},{6,22},{8,24},{10,26},{12,28},{14,30},{16,0},... | collective-permute-start | bytes 688136 | tf_op jit(solution)/shard_map/ppermute | solution.py:628
  309.7 31.8 %collective-permute-start.24 = (bf16[64,1792]{1,0:T(8,128)(2,1)}, bf16[64,1792]{1,0:T(8,128)(2,1)}, u32[]{:S(2)}, u32[]{:S(2)}) collective-permute-start(bf16[64,1792]{1,0:T(8,128)(2,1)} %get-tuple-element.339), channel_id=1, source_target_pairs={{0,24},{2,26},{4,28},{6,30},{8,0},{10,2},{12,4},{14,6},{16,8},{18,... | collective-permute-start | bytes 688136 | tf_op jit(solution)/shard_map/ppermute | solution.py:628
  320.3 21.2 %collective-permute-start.25 = (bf16[64,768]{1,0:T(8,128)(2,1)}, bf16[64,768]{1,0:T(8,128)(2,1)}, u32[]{:S(2)}, u32[]{:S(2)}) collective-permute-start(bf16[64,768]{1,0:T(8,128)(2,1)} %get-tuple-element.345), channel_id=1, source_target_pairs={{0,8},{2,10},{4,12},{6,14},{8,16},{10,18},{12,20},{14,22},{16,24},... | collective-permute-start | bytes 294920 | tf_op jit(solution)/shard_map/ppermute | solution.py:628
  324.9 16.6 %collective-permute-start.26 = (bf16[64,768]{1,0:T(8,128)(2,1)S(1)}, bf16[64,768]{1,0:T(8,128)(2,1)S(1)}, u32[]{:S(2)}, u32[]{:S(2)}) collective-permute-start(bf16[64,768]{1,0:T(8,128)(2,1)S(1)} %get-tuple-element.344), channel_id=1, source_target_pairs={{0,16},{2,18},{4,20},{6,22},{8,24},{10,26},{12,28},{14,30},{16,0},... | collective-permute-start | bytes 294920 | tf_op jit(solution)/shard_map/ppermute | solution.py:628
  327.2 14.3 %all-to-all-start.2 = ((f32[16,1,3072]{2,1,0:T(1,128)}), f32[16,1,3072]{2,1,0:T(1,128)S(1)}, u32[]{:S(2)}, u32[]{:S(2)}) async-start(f32[16,1,3072]{2,1,0:T(1,128)} %broadcast_in_dim.10), calls=%async_computation.3 | async-start | bytes 393216 | tf_op jit(solution)/shard_map/all_to_all | solution.py:740
  (50 other events, 426.6 us)
Sparse Core Ops, SparseCore 0:
  10.9 49.5 all-gather.2
  67.8 77.9 all-gather.4
  195.8 116.0 reduce-scatter.1
